TPU v7x, 32 devices: a whole 2x2x4 slice. The times are simulated.
32 devices in a mesh: items: 8 (over z, x), stream: 4 (over y, core).
Axes of the slice: x: 2, y: 2, z: 4, core: 2. Of those that a mesh axis runs over, the one named last changes fastest.
Arguments:
- tokens: bfloat16 [16384, 768], P(('items', 'stream')), may hold values from -6 to 6
- group_kind: int32 [8], P('items'), may hold values from 0 to 1
- ln1_gain: bfloat16 [768], P(('items', 'stream')), may hold values from 0.099609375 to 1.8984375
- ln1_bias: bfloat16 [768], P(('items', 'stream')), may hold values from -3 to 3
- w_qkv: bfloat16 [768, 2304], P(('items', 'stream')), may hold values from -0.21875 to 0.21875
- q_bias: bfloat16 [768], P(('items', 'stream')), may hold values from -3 to 3
- v_bias: bfloat16 [768], P(('items', 'stream')), may hold values from -3 to 3
- w_out: bfloat16 [768, 768], P(('items', 'stream')), may hold values from -0.625 to 0.625
- out_bias: bfloat16 [768], P(('items', 'stream')), may hold values from -2 to 2
- ln2_gain: bfloat16 [768], P(('items', 'stream')), may hold values from 0.099609375 to 1.8984375
- ln2_bias: bfloat16 [768], P(('items', 'stream')), may hold values from -3 to 3
- w_up: bfloat16 [2, 768, 3072], P(None, ('items', 'stream')), may hold values from -0.21875 to 0.21875
- b_up: bfloat16 [2, 3072], P(None, ('items', 'stream')), may hold values from -3 to 3
- w_down: bfloat16 [2, 3072, 768], P(None, ('items', 'stream')), may hold values from -0.109375 to 0.109375
- b_down: bfloat16 [2, 768], P(None, ('items', 'stream')), may hold values from -2 to 2
- cotangent: bfloat16 [16384, 768], P(('items', 'stream')), may hold values from -6 to 6
Outputs:
- output: bfloat16 [16384, 768], P(('items', 'stream'))
- token_grad: bfloat16 [16384, 768], P(('items', 'stream'))
- grad_ln1_gain: float32 [768], P(('items', 'stream'))
- grad_ln1_bias: float32 [768], P(('items', 'stream'))
- grad_w_qkv: float32 [768, 2304], P(('items', 'stream'))
- grad_q_bias: float32 [768], P(('items', 'stream'))
- grad_v_bias: float32 [768], P(('items', 'stream'))
- grad_w_out: float32 [768, 768], P(('items', 'stream'))
- grad_out_bias: float32 [768], P(('items', 'stream'))
- grad_ln2_gain: float32 [768], P(('items', 'stream'))
- grad_ln2_bias: float32 [768], P(('items', 'stream'))
- grad_w_up: float32 [2, 768, 3072], P(None, ('items', 'stream'))
- grad_b_up: float32 [2, 3072], P(None, ('items', 'stream'))
- grad_w_down: float32 [2, 3072, 768], P(None, ('items', 'stream'))
- grad_b_down: float32 [2, 768], P(None, ('items', 'stream'))
- counts: float32 [2], replicated
Inputs may be any that keep to these rules, and one draw needn't show every extreme that they name: `group_kind`: 0 marks a group of 7 items with 197 patch rows, 1 a group of 2 items with 577 patch rows; item and modality of each row follow from it as the steps state.
All inputs are finite; a program needn't handle non-finite values.
Results may differ from a plain program's by a relative error of at most 0.014.
Values may be sent and summed in bfloat16 or wider, within the bound.
A program may use at most 256 MiB of HBM per device.

v0:
```python
import jax
import jax.numpy as jnp
from jax import lax
from jax.sharding import PartitionSpec as P

HEADS = 12
HEAD_DIM = 64
PATCH_S = 197
PATCH_L = 577
TEXT_LEN = 40
ITEMS_S = 7
ITEMS_L = 2


NORM_EPS = 1e-05
MASKED = -1000000000.0


def layer_norm(values, gain_row, shift_row):
    row_mean = jnp.mean(values, axis=-1, keepdims=True)
    centred = values - row_mean
    variance = jnp.mean(centred * centred, axis=-1, keepdims=True)
    return centred * lax.rsqrt(variance + NORM_EPS) * gain_row + shift_row


def gelu_exact(values):
    return jax.nn.gelu(values, approximate=False)


def layout(group_type, positions, row_count):
    patch_len = jnp.where(group_type == 0, PATCH_S, PATCH_L).astype(jnp.int32)
    members = jnp.where(group_type == 0, ITEMS_S, ITEMS_L).astype(jnp.int32)
    is_patch = positions < 3 * row_count
    patch_item = positions // patch_len
    text_item = jnp.maximum(positions - 3 * row_count, 0) // TEXT_LEN
    member = jnp.where(is_patch, patch_item, text_item)
    member = jnp.where(member < members, member, -1)
    modality = jnp.where(member < 0, 2, jnp.where(is_patch, 0, 1)).astype(jnp.int32)
    return (member, modality)


def product(first_op, second_op):
    return jnp.dot(first_op, second_op, preferred_element_type=jnp.float32)


def product_lead(first_op, second_op):
    return lax.dot_general(
        first_op, second_op, (((0,), (0,)), ((), ())), preferred_element_type=jnp.float32
    )


def product_trail(first_op, second_op):
    return lax.dot_general(
        first_op, second_op, (((1,), (1,)), ((), ())), preferred_element_type=jnp.float32
    )


def body(
    tokens,
    group_kind,
    ln1_gain,
    ln1_bias,
    w_qkv,
    q_bias,
    v_bias,
    w_out,
    out_bias,
    ln2_gain,
    ln2_bias,
    w_up,
    b_up,
    w_down,
    b_down,
    cotangent,
):
    row_count = tokens.shape[0]
    model_width = tokens.shape[1]
    stream_size = lax.axis_size("stream")
    stream_place = lax.axis_index("stream")
    group_type = group_kind[0]
    own_positions = stream_place * row_count + jnp.arange(row_count, dtype=jnp.int32)
    own_member, own_modality = layout(group_type, own_positions, row_count)
    key_member = layout(
        group_type, jnp.arange(stream_size * row_count, dtype=jnp.int32), row_count
    )[0]
    local_counts = jnp.stack(
        [
            jnp.sum((own_modality == 0).astype(jnp.float32)),
            jnp.sum((own_modality == 1).astype(jnp.float32)),
        ]
    )
    totals = lax.psum(local_counts, ("items", "stream"))
    gathered = (
        lax.all_gather(ln1_gain, ("items", "stream"), axis=0, tiled=True),
        lax.all_gather(ln1_bias, ("items", "stream"), axis=0, tiled=True),
        lax.all_gather(w_qkv, ("items", "stream"), axis=0, tiled=True),
        lax.all_gather(q_bias, ("items", "stream"), axis=0, tiled=True),
        lax.all_gather(v_bias, ("items", "stream"), axis=0, tiled=True),
        lax.all_gather(w_out, ("items", "stream"), axis=0, tiled=True),
        lax.all_gather(out_bias, ("items", "stream"), axis=0, tiled=True),
        lax.all_gather(ln2_gain, ("items", "stream"), axis=0, tiled=True),
        lax.all_gather(ln2_bias, ("items", "stream"), axis=0, tiled=True),
        lax.all_gather(w_up, ("items", "stream"), axis=1, tiled=True),
        lax.all_gather(b_up, ("items", "stream"), axis=1, tiled=True),
        lax.all_gather(w_down, ("items", "stream"), axis=1, tiled=True),
        lax.all_gather(b_down, ("items", "stream"), axis=1, tiled=True),
    )
    (
        gain_one,
        shift_one,
        qkv_weight,
        query_shift,
        value_shift,
        out_weight,
        out_shift,
        gain_two,
        shift_two,
        up_all,
        up_shift_all,
        down_all,
        down_shift_all,
    ) = gathered
    expert_pick = jnp.where(stream_place == stream_size - 1, 1, 0).astype(jnp.int32)
    tokens_f = tokens.astype(jnp.float32)
    normed_one, pull_one = jax.vjp(
        layer_norm, tokens_f, gain_one.astype(jnp.float32), shift_one.astype(jnp.float32)
    )
    normed_low = normed_one.astype(jnp.bfloat16)
    projected = product(normed_low, qkv_weight)
    queries = (projected[:, :model_width] + query_shift.astype(jnp.float32)).astype(jnp.bfloat16)
    keys_own = projected[:, model_width : 2 * model_width].astype(jnp.bfloat16)
    values_own = (projected[:, 2 * model_width :] + value_shift.astype(jnp.float32)).astype(
        jnp.bfloat16
    )
    keys_all, values_all = (
        lax.all_gather(keys_own, "stream", axis=0, tiled=True),
        lax.all_gather(values_own, "stream", axis=0, tiled=True),
    )
    allowed = own_member[:, None] == key_member[None, :]
    score_scale = HEAD_DIM ** (-0.5)

    def head_scores(head_index):
        columns = slice(head_index * HEAD_DIM, (head_index + 1) * HEAD_DIM)
        raw_scores = product_trail(queries[:, columns], keys_all[:, columns])
        return jnp.where(allowed, raw_scores * score_scale, MASKED)

    attended = []
    log_totals = []
    for head_index in range(HEADS):
        columns = slice(head_index * HEAD_DIM, (head_index + 1) * HEAD_DIM)
        scores = head_scores(head_index)
        row_top = jnp.max(scores, axis=1, keepdims=True)
        exponent = jnp.exp(scores - row_top)
        row_total = jnp.sum(exponent, axis=1, keepdims=True)
        softmax_low = (exponent / row_total).astype(jnp.bfloat16)
        attended.append(product(softmax_low, values_all[:, columns]))
        log_totals.append(row_top + jnp.log(row_total))
    mixed_low = jnp.concatenate(attended, axis=1).astype(jnp.bfloat16)
    residual = tokens_f + product(mixed_low, out_weight) + out_shift.astype(jnp.float32)
    normed_two, pull_two = jax.vjp(
        layer_norm, residual, gain_two.astype(jnp.float32), shift_two.astype(jnp.float32)
    )
    normed_two_low = normed_two.astype(jnp.bfloat16)
    up_weight = lax.dynamic_index_in_dim(up_all, expert_pick, 0, keepdims=False)
    up_shift = lax.dynamic_index_in_dim(up_shift_all, expert_pick, 0, keepdims=False)
    down_weight = lax.dynamic_index_in_dim(down_all, expert_pick, 0, keepdims=False)
    down_shift = lax.dynamic_index_in_dim(down_shift_all, expert_pick, 0, keepdims=False)
    hidden_pre = product(normed_two_low, up_weight) + up_shift.astype(jnp.float32)
    hidden, pull_gelu = jax.vjp(gelu_exact, hidden_pre)
    hidden_low = hidden.astype(jnp.bfloat16)
    branch = product(hidden_low, down_weight) + down_shift.astype(jnp.float32)
    expert_mask = (own_modality == expert_pick).astype(jnp.float32)[:, None]
    output = (residual + branch * expert_mask).astype(jnp.bfloat16)
    live_rows = (own_modality < 2).astype(jnp.float32)[:, None]
    out_grad = cotangent.astype(jnp.float32) * live_rows
    branch_grad = (out_grad * expert_mask).astype(jnp.bfloat16)
    grad_down = product_lead(hidden_low, branch_grad)
    grad_down_shift = jnp.sum(branch_grad.astype(jnp.float32), axis=0)
    hidden_grad = product_trail(branch_grad, down_weight)
    pre_grad = pull_gelu(hidden_grad)[0].astype(jnp.bfloat16)
    grad_up = product_lead(normed_two_low, pre_grad)
    grad_up_shift = jnp.sum(pre_grad.astype(jnp.float32), axis=0)
    picker = (jnp.arange(2, dtype=jnp.int32) == expert_pick).astype(jnp.float32)
    expert_summed = (
        lax.psum_scatter(
            picker[:, None, None] * grad_up[None],
            ("items", "stream"),
            scatter_dimension=1,
            tiled=True,
        ),
        lax.psum_scatter(
            picker[:, None] * grad_up_shift[None],
            ("items", "stream"),
            scatter_dimension=1,
            tiled=True,
        ),
        lax.psum_scatter(
            picker[:, None, None] * grad_down[None],
            ("items", "stream"),
            scatter_dimension=1,
            tiled=True,
        ),
        lax.psum_scatter(
            picker[:, None] * grad_down_shift[None],
            ("items", "stream"),
            scatter_dimension=1,
            tiled=True,
        ),
    )
    norm_two_grad = product_trail(pre_grad, up_weight)
    residual_part, grad_gain_two, grad_shift_two = pull_two(norm_two_grad)
    residual_grad = out_grad + residual_part
    residual_low = residual_grad.astype(jnp.bfloat16)
    grad_out_weight = product_lead(mixed_low, residual_low)
    grad_out_shift = jnp.sum(residual_low.astype(jnp.float32), axis=0)
    mixed_grad = product_trail(residual_low, out_weight).astype(jnp.bfloat16)
    query_parts = []
    key_parts = []
    value_parts = []
    centres = []
    for head_index in range(HEADS):
        columns = slice(head_index * HEAD_DIM, (head_index + 1) * HEAD_DIM)
        softmax_out = jnp.exp(head_scores(head_index) - log_totals[head_index])
        mixed_part = mixed_grad[:, columns]
        prob_grad = product_trail(mixed_part, values_all[:, columns])
        centre = jnp.sum(softmax_out * prob_grad, axis=1, keepdims=True)
        centres.append(centre)
        score_grad = (softmax_out * (prob_grad - centre) * score_scale).astype(jnp.bfloat16)
        query_parts.append(product(score_grad, keys_all[:, columns]))
        key_parts.append(product_lead(score_grad, queries[:, columns]))
        value_parts.append(product_lead(softmax_out.astype(jnp.bfloat16), mixed_part))
    key_terms = jnp.concatenate(key_parts, axis=1)
    value_terms = jnp.concatenate(value_parts, axis=1)
    key_grad, value_grad = (
        lax.psum_scatter(key_terms, "stream", scatter_dimension=0, tiled=True),
        lax.psum_scatter(value_terms, "stream", scatter_dimension=0, tiled=True),
    )
    qkv_grad = jnp.concatenate(
        [
            jnp.concatenate(query_parts, axis=1).astype(jnp.bfloat16),
            key_grad.astype(jnp.bfloat16),
            value_grad.astype(jnp.bfloat16),
        ],
        axis=1,
    )
    grad_qkv = product_lead(normed_low, qkv_grad)
    grad_query_shift = jnp.sum(qkv_grad[:, :model_width].astype(jnp.float32), axis=0)
    grad_value_shift = jnp.sum(qkv_grad[:, 2 * model_width :].astype(jnp.float32), axis=0)
    norm_one_grad = product_trail(qkv_grad, qkv_weight)
    token_part, grad_gain_one, grad_shift_one = pull_one(norm_one_grad)
    token_grad = (residual_grad + token_part).astype(jnp.bfloat16)
    summed = (
        lax.psum_scatter(grad_gain_one, ("items", "stream"), scatter_dimension=0, tiled=True),
        lax.psum_scatter(grad_shift_one, ("items", "stream"), scatter_dimension=0, tiled=True),
        lax.psum_scatter(grad_qkv, ("items", "stream"), scatter_dimension=0, tiled=True),
        lax.psum_scatter(grad_query_shift, ("items", "stream"), scatter_dimension=0, tiled=True),
        lax.psum_scatter(grad_value_shift, ("items", "stream"), scatter_dimension=0, tiled=True),
        lax.psum_scatter(grad_out_weight, ("items", "stream"), scatter_dimension=0, tiled=True),
        lax.psum_scatter(grad_out_shift, ("items", "stream"), scatter_dimension=0, tiled=True),
        lax.psum_scatter(grad_gain_two, ("items", "stream"), scatter_dimension=0, tiled=True),
        lax.psum_scatter(grad_shift_two, ("items", "stream"), scatter_dimension=0, tiled=True),
    )
    factor = lax.rsqrt(totals)
    return (
        output,
        token_grad,
        summed[0],
        summed[1],
        summed[2],
        summed[3],
        summed[4],
        summed[5],
        summed[6],
        summed[7],
        summed[8],
        expert_summed[0] * factor[:, None, None],
        expert_summed[1] * factor[:, None],
        expert_summed[2] * factor[:, None, None],
        expert_summed[3] * factor[:, None],
        totals,
    )


def solution(mesh):
    placed = (
        P(("items", "stream"), None),
        P("items"),
        P(("items", "stream")),
        P(("items", "stream")),
        P(("items", "stream"), None),
        P(("items", "stream")),
        P(("items", "stream")),
        P(("items", "stream"), None),
        P(("items", "stream")),
        P(("items", "stream")),
        P(("items", "stream")),
        P(None, ("items", "stream"), None),
        P(None, ("items", "stream")),
        P(None, ("items", "stream"), None),
        P(None, ("items", "stream")),
        P(("items", "stream"), None),
    )
    return jax.shard_map(
        body,
        mesh=mesh,
        in_specs=placed,
        out_specs=(
            P(("items", "stream"), None),
            P(("items", "stream"), None),
            P(("items", "stream")),
            P(("items", "stream")),
            P(("items", "stream"), None),
            P(("items", "stream")),
            P(("items", "stream")),
            P(("items", "stream"), None),
            P(("items", "stream")),
            P(("items", "stream")),
            P(("items", "stream")),
            P(None, ("items", "stream"), None),
            P(None, ("items", "stream")),
            P(None, ("items", "stream"), None),
            P(None, ("items", "stream")),
            P(),
        ),
        check_vma=False,
    )
```

profile of v0, /device:TPU:0, one launch (start us, length us, event | category | flops | bytes accessed | tf_op | source)
XLA Modules:
  0.0 1307.9 jit_solution(13353327654674793183)
XLA Ops:
  13.8 42.5 %all-reduce.16 = (bf16[768]{0:T(1024)(128)(2,1)S(1)}, bf16[768]{0:T(1024)(128)(2,1)S(1)}, bf16[768]{0:T(1024)(128)(2,1)S(1)}, bf16[768]{0:T(1024)(128)(2,1)S(1)}...) all-reduce(bf16[768]{0:T(1024)(128)(2,1)S(1)} %dynamic-update-slice, ...), channel_id=1, replica_groups=mesh['items'=8,'stream'=4] {'items','stream'}, use_global_device_ids=true, to_apply=%add.1 | all-reduce | flops 5376 | bytes 21504
  59.8 14.2 %all-gather.9.cloned.1.call-done = bf16[768,2304]{1,0:T(8,128)(2,1)} async-done(((bf16[24,2304]{1,0:T(8,128)(2,1)}), bf16[768,2304]{1,0:T(8,128)(2,1)}) %all-gather.9.cloned.1.call-update) | async-done | bytes 3538960 | tf_op jit(solution)/shard_map/all_gather | solution.py:96
  74.1 4.4 fusion.250
  78.5 2.2 copy-done.77
  81.8 3.3 fusion.90
  88.5 39.3 %all-gather = bf16[32,96,2]{1,2,0:T(2,128)(2,1)S(1)} all-gather(bf16[1,96,2]{1,2,0:T(2,128)(2,1)S(1)} %bitcast.81), channel_id=1, replica_groups=mesh['items'=8,'stream'=4] {'items','stream'}, dimensions={0}, use_global_device_ids=true | all-gather | bytes 12672 | tf_op jit(solution)/shard_map/all_gather | solution.py:104
  128.0 2.0 fusion.264
  130.8 2.6 fusion.263
  134.1 2.7 fusion.262
  137.5 2.6 fusion.261
  140.8 2.7 fusion.260
  144.1 2.6 fusion.259
  147.4 2.6 fusion.265
  150.7 2.7 fusion.266
  154.5 2.3 fusion.267
  157.5 2.7 fusion.268
  160.9 2.6 fusion.269
  164.2 2.7 fusion.270
  166.8 2.0 copy-done.36
  169.6 3.4 fusion.106
  197.4 2.5 fusion.271
  200.3 80.4 %all-gather.17.cloned.1.call-done = bf16[2,768,3072]{2,1,0:T(8,128)(2,1)} async-done(((bf16[2,24,3072]{2,1,0:T(8,128)(2,1)}), bf16[2,768,3072]{2,1,0:T(8,128)(2,1)}) %all-gather.17.cloned.1.call-update) | async-done | bytes 9437200 | tf_op jit(solution)/shard_map/all_gather | solution.py:103
  280.7 19.7 %multiply_convert_fusion = (bf16[512,3072]{1,0:T(8,128)(2,1)}, f32[512,3072]{1,0:T(8,128)}, f32[512,3072]{1,0:T(8,128)}) fusion(f32[3072]{0:T(1024)S(1)} %bitcast.79, bf16[2,768,3072]{2,1,0:T(8,128)(2,1)} %all-gather.17.cloned.1.call-done, s32[]{:T(128)S(6)} %select_n.209, f32[512,768]{1,0:T(8,128)S(1)} %get-tuple-element.102, ...), kind=kOutput, calls=%fused_computation.18 | convolution fusion | flops 2521694208 | bytes 22042628 | tf_op jit(solution)/shard_map/dot_general | solution.py:43
  300.5 63.7 %all-gather.19.cloned.1.call-done = bf16[2,3072,768]{2,1,0:T(8,128)(2,1)} async-done(((bf16[2,96,768]{2,1,0:T(8,128)(2,1)}), bf16[2,3072,768]{2,1,0:T(8,128)(2,1)}) %all-gather.19.cloned.1.call-update) | async-done | bytes 9437200 | tf_op jit(solution)/shard_map/all_gather | solution.py:105
  364.2 9.1 convert_reduce_fusion
  373.2 7.0 multiply_reduce_fusion.12
  431.1 4.0 convolution_dynamic-update-slice_fusion.11
  435.1 4.1 convolution_dynamic-update-slice_fusion.10
  439.3 1.7 convolution_dynamic-update-slice_fusion.9
  441.0 1.6 convolution_dynamic-update-slice_fusion.8
  442.6 1.6 convolution_dynamic-update-slice_fusion.7
  444.3 1.7 convolution_dynamic-update-slice_fusion.6
  445.9 1.7 convolution_dynamic-update-slice_fusion.5
  447.6 1.6 convolution_dynamic-update-slice_fusion.4
  449.2 1.7 convolution_dynamic-update-slice_fusion.3
  450.9 1.7 convolution_dynamic-update-slice_fusion.2
  452.7 1.6 convolution_dynamic-update-slice_fusion.1
  454.3 1.6 convolution_dynamic-update-slice_fusion
  456.2 1.7 copy.36
  457.8 8.3 fusion.254
  466.2 10.5 broadcast_multiply_fusion
  477.0 5.2 fusion.253
  482.2 7.2 broadcast_multiply_fusion.1
  489.4 3.6 fusion.272
  493.1 2.6 constant_dynamic-update-slice_fusion.23
  495.7 4.0 constant_dynamic-update-slice_fusion.22
  499.7 2.8 constant_dynamic-update-slice_fusion.21
  514.6 1.6 constant_dynamic-update-slice_fusion.12
  516.2 2.4 convert_dynamic-update-slice_fusion
  518.6 30.3 %reduce-scatter.13.cloned.1.call-done = f32[512,768]{0,1:T(8,128)} async-done(((f32[2048,768]{0,1:T(8,128)}), f32[512,768]{0,1:T(8,128)}) %reduce-scatter.13.cloned.1.call-update) | async-done | bytes 1572880 | tf_op jit(solution)/shard_map/reduce_scatter | solution.py:236
  548.9 2.4 convert_dynamic-update-slice_fusion.1
  551.3 6.9 fusion.248
  558.9 40.5 %all-gather.1 = bf16[32,24,2]{1,2,0:T(2,128)(2,1)S(1)} all-gather(bf16[1,24,2]{1,2,0:T(2,128)(2,1)S(1)} %bitcast.82), channel_id=1, replica_groups=mesh['items'=8,'stream'=4] {'items','stream'}, dimensions={0}, use_global_device_ids=true | all-gather | bytes 3168 | tf_op jit(solution)/shard_map/all_gather | solution.py:106
  602.3 7.3 add_convert_fusion.2
  609.7 41.5 %reduce-scatter.23.cloned.1.call-done = f32[96,2]{1,0:T(8,128)} async-done(((f32[3072,2]{1,0:T(8,128)}), f32[96,2]{1,0:T(8,128)}) %reduce-scatter.23.cloned.1.call-update) | async-done | bytes 784
  652.3 5.1 fusion.255
  659.4 40.7 %all-reduce.15 = (f32[768]{0:T(1024)S(1)}, f32[768]{0:T(1024)S(1)}, f32[768]{0:T(1024)S(1)}, f32[768]{0:T(1024)S(1)}, f32[768]{0:T(1024)S(1)}, /*index=5*/f32[76...) all-reduce(f32[768]{0:T(1024)S(1)} %get-tuple-element.18, ...), channel_id=4, replica_groups=mesh['items'=8,'stream'=4] {'items','stream'}, use_global_device_ids=true, to_apply=%region_47.48.clone | all-reduce | flops 6914 | bytes 55312
  705.5 2.8 add_convert_fusion.1
  708.3 153.3 %reduce-scatter.21.cloned.1.call-done = f32[2,96,768]{2,1,0:T(8,128)} async-done(((f32[2,3072,768]{2,1,0:T(8,128)}), f32[2,96,768]{2,1,0:T(8,128)}) %reduce-scatter.21.cloned.1.call-update) | async-done | bytes 589840 | tf_op jit(solution)/shard_map/reduce_scatter | solution.py:197
  861.6 2.0 broadcast_multiply_fusion.2
  863.6 208.4 %reduce-scatter.19.cloned.1.call-done = f32[2,24,3072]{2,1,0:T(8,128)} async-done(((f32[2,768,3072]{2,1,0:T(8,128)}), f32[2,24,3072]{2,1,0:T(8,128)}) %reduce-scatter.19.cloned.1.call-update) | async-done | bytes 589840 | tf_op jit(solution)/shard_map/reduce_scatter | solution.py:185
  1072.0 2.0 broadcast_multiply_fusion.3
  1074.0 101.8 %reduce-scatter.17.cloned.1.call-done = f32[24,768]{1,0:T(8,128)} async-done(((f32[768,768]{1,0:T(8,128)}), f32[24,768]{1,0:T(8,128)}) %reduce-scatter.17.cloned.1.call-update) | async-done | bytes 73744 | tf_op jit(solution)/shard_map/reduce_scatter | solution.py:258
  1175.7 125.4 %reduce-scatter.15.cloned.1.call-done = f32[24,2304]{1,0:T(8,128)} async-done(((f32[768,2304]{1,0:T(8,128)}), f32[24,2304]{1,0:T(8,128)}) %reduce-scatter.15.cloned.1.call-update) | async-done | bytes 221200 | tf_op jit(solution)/shard_map/reduce_scatter | solution.py:255
  (375 shorter events, 122.7 us)
Async XLA Ops:
  7.2 66.9 %all-gather.9.cloned.1.call-start = ((), (), s32[]{:S(2)}) async-start(), calls=%async_computation.7 | async-start | bytes 3649536 | tf_op jit(solution)/shard_map/all_gather | solution.py:96
  7.9 120.1 %all-gather.11.cloned.1.call-start = ((), (), s32[]{:S(2)}) async-start(), calls=%async_computation.8 | async-start | bytes 3932160 | tf_op jit(solution)/shard_map/all_gather | solution.py:136
  56.3 22.1 %copy-start.82 = (f32[768]{0:T(1024)}, f32[768]{0:T(1024)S(1)}, u32[]{:S(2)}) copy-start(f32[768]{0:T(1024)S(1)} %convert_element_type.228) | copy-start | bytes 9220
  56.3 22.1 %copy-start.95 = (f32[768]{0:T(1024)}, f32[768]{0:T(1024)S(1)}, u32[]{:S(2)}) copy-start(f32[768]{0:T(1024)S(1)} %convert_element_type.229) | copy-start | bytes 9220
  57.7 20.8 %copy-start.84 = (f32[512]{0:T(512)}, f32[512]{0:T(512)S(1)}, u32[]{:S(2)}) copy-start(f32[512]{0:T(512)S(1)} %broadcast_multiply_fusion.7) | copy-start | bytes 6148
  59.8 18.7 %copy-start.86 = (f32[512]{0:T(512)}, f32[512]{0:T(512)S(1)}, u32[]{:S(2)}) copy-start(f32[512]{0:T(512)S(1)} %fusion.242) | copy-start | bytes 6148
  80.7 7.8 copy-start.97
  81.7 87.9 %all-gather.13.cloned.1.call-start = ((), (), s32[]{:S(2)}) async-start(), calls=%async_computation.9 | async-start | bytes 3932160 | tf_op jit(solution)/shard_map/all_gather | solution.py:137
  85.1 112.3 %all-gather.15.cloned.1.call-start = ((), (), s32[]{:S(2)}) async-start(), calls=%async_computation.10 | async-start | bytes 1216512 | tf_op jit(solution)/shard_map/all_gather | solution.py:99
  85.7 195.1 %all-gather.17.cloned.1.call-start = ((), (), s32[]{:S(2)}) async-start(), calls=%async_computation.11 | async-start | bytes 9732096 | tf_op jit(solution)/shard_map/all_gather | solution.py:103
  86.2 277.9 %all-gather.19.cloned.1.call-start = ((), (), s32[]{:S(2)}) async-start(), calls=%async_computation.12 | async-start | bytes 9732096 | tf_op jit(solution)/shard_map/all_gather | solution.py:105
  86.8 429.4 %reduce-scatter.11.cloned.1.call-start = ((), (), s32[]{:S(2)}) async-start(), calls=%async_computation.13 | async-start | bytes 7864320 | tf_op jit(solution)/shard_map/reduce_scatter | solution.py:235
  133.4 3.4 copy-start.4
  140.0 3.4 copy-start.16
  150.0 3.4 copy-start.12
  153.4 3.4 copy-start.20
  156.8 3.4 copy-start.24
  163.4 3.4 copy-start.32
  169.5 3.6 copy-start.41
  169.5 4.6 copy-start.68
  197.3 103.2 %copy-start.81 = (bf16[512,768]{0,1:T(8,128)(2,1)}, bf16[512,768]{0,1:T(8,128)(2,1)S(1)}, u32[]{:S(2)}) copy-start(bf16[512,768]{0,1:T(8,128)(2,1)S(1)} %fusion.117) | copy-start | bytes 2359300
  199.8 180.5 %copy-start.75 = (f32[512,768]{1,0:T(8,128)}, f32[512,768]{1,0:T(8,128)S(1)}, u32[]{:S(2)}) copy-start(f32[512,768]{1,0:T(8,128)S(1)} %get-tuple-element.102) | copy-start | bytes 4718596
  280.7 83.4 %copy-start.78 = (bf16[512,768]{1,0:T(8,128)(2,1)S(1)}, bf16[512,768]{1,0:T(8,128)(2,1)}, u32[]{:S(2)}) copy-start(bf16[512,768]{1,0:T(8,128)(2,1)} %param.31) | copy-start | bytes 2359300
  373.2 7.0 copy-start.101
  380.9 4.8 copy-start.66
  380.9 3.8 copy-start.44
  381.0 4.8 copy-start.90
  382.0 3.7 copy-start.80
  430.7 118.2 %reduce-scatter.13.cloned.1.call-start = ((), (), s32[]{:S(2)}) async-start(), calls=%async_computation.14 | async-start | bytes 7864320 | tf_op jit(solution)/shard_map/reduce_scatter | solution.py:236
  431.1 8.1 copy-start.19
  435.1 5.9 copy-start.11
  439.3 3.4 copy-start.7
  447.6 3.3 copy-start.31
  449.2 3.5 copy-start.35
  450.9 3.5 copy-start.39
  456.0 195.2 %reduce-scatter.23.cloned.1.call-start = ((), (), s32[]{:S(2)}) async-start(), calls=%async_computation.19 | async-start | bytes 1622016
  466.1 395.5 %reduce-scatter.21.cloned.1.call-start = ((), (), s32[]{:S(2)}) async-start(), calls=%async_computation.18 | async-start | bytes 19464192 | tf_op jit(solution)/shard_map/reduce_scatter | solution.py:197
  476.7 595.3 %reduce-scatter.19.cloned.1.call-start = ((), (), s32[]{:S(2)}) async-start(), calls=%async_computation.17 | async-start | bytes 19464192 | tf_op jit(solution)/shard_map/reduce_scatter | solution.py:185
  489.4 686.3 %reduce-scatter.17.cloned.1.call-start = ((), (), s32[]{:S(2)}) async-start(), calls=%async_computation.16 | async-start | bytes 2433024 | tf_op jit(solution)/shard_map/reduce_scatter | solution.py:258
  493.0 808.1 %reduce-scatter.15.cloned.1.call-start = ((), (), s32[]{:S(2)}) async-start(), calls=%async_computation.15 | async-start | bytes 7299072 | tf_op jit(solution)/shard_map/reduce_scatter | solution.py:255
  493.1 6.7 copy-start.47
  493.1 9.4 copy-start.49
  493.1 9.4 copy-start.72
  495.7 8.4 copy-start.51
  499.7 5.8 copy-start.53
  502.5 4.6 copy-start.55
  504.1 4.4 copy-start.57
  505.5 4.6 copy-start.59
  507.1 4.4 copy-start.61
  508.5 4.6 copy-start.63
  510.1 4.4 copy-start.65
  514.5 36.7 %copy-start.71 = (bf16[512,768]{1,0:T(8,128)(2,1)S(1)}, bf16[512,768]{1,0:T(8,128)(2,1)}, u32[]{:S(2)}) copy-start(bf16[512,768]{1,0:T(8,128)(2,1)} %param.16) | copy-start | bytes 2359300
  514.6 36.7 %copy-start.83 = (f32[768]{0:T(1024)S(1)}, f32[768]{0:T(1024)}, u32[]{:S(2)}) copy-start(f32[768]{0:T(1024)} %copy-done.82) | copy-start | bytes 9220
  514.6 36.7 %copy-start.85 = (f32[512]{0:T(512)S(1)}, f32[512]{0:T(512)}, u32[]{:S(2)}) copy-start(f32[512]{0:T(512)} %copy-done.84) | copy-start | bytes 6148
  514.6 36.7 %copy-start.87 = (f32[512]{0:T(512)S(1)}, f32[512]{0:T(512)}, u32[]{:S(2)}) copy-start(f32[512]{0:T(512)} %copy-done.86) | copy-start | bytes 6148
  514.6 36.7 %copy-start.96 = (f32[768]{0:T(1024)S(1)}, f32[768]{0:T(1024)}, u32[]{:S(2)}) copy-start(f32[768]{0:T(1024)} %copy-done.95) | copy-start | bytes 9220
  602.3 49.7 %copy-start.74 = (f32[512,768]{0,1:T(8,128)S(1)}, f32[512,768]{0,1:T(8,128)}, u32[]{:S(2)}) copy-start(f32[512,768]{0,1:T(8,128)} %reduce-scatter.13.cloned.1.call-done) | copy-start | bytes 4718596
  652.3 5.2 copy-start.89
  652.3 7.1 copy-start.92
  652.3 7.1 copy-start.93
  652.3 7.1 copy-start.94
  652.3 53.2 %copy-start.67 = (f32[512,768]{1,0:T(8,128)S(1)}, f32[512,768]{1,0:T(8,128)}, u32[]{:S(2)}) copy-start(f32[512,768]{1,0:T(8,128)} %copy-done.66) | copy-start | bytes 4718596
  652.3 53.2 %copy-start.91 = (f32[512]{0:T(512)S(1)}, f32[512]{0:T(512)}, u32[]{:S(2)}) copy-start(f32[512]{0:T(512)} %copy-done.90) | copy-start | bytes 6148
  700.1 601.0 %copy-start.100 = (f32[2]{0:T(128)}, f32[2]{0:T(128)S(1)}, u32[]{:S(2)}) copy-start(f32[2]{0:T(128)S(1)} %get-tuple-element.32) | copy-start | bytes 28
  (51 other events, 123.7 us)
Sparse Core Ops, SparseCore 0:
  10.9 63.0 all-gather.8
  81.8 27.4 all-gather.10
  111.4 28.6 all-gather.12
  142.9 54.0 all-gather.14
  199.7 81.0 all-gather.16
  283.4 80.6 all-gather.18
  430.8 56.9 reduce-scatter.10
  490.4 58.3 reduce-scatter.12
  554.1 97.0 reduce-scatter.22
  657.4 204.1 reduce-scatter.20
  868.0 203.9 reduce-scatter.18
  1077.7 97.9 reduce-scatter.16
  1182.9 118.1 reduce-scatter.14
where the time goes:
time: 1310 us
  waiting for transfers between devices  822 us (63%)
  matrix products  204 us (16%)
  blocking collectives  163 us (12%)
  other arithmetic  65.3 us (5%)
  local copies, waits for them, and re-layouts  36.5 us (3%)
  between operations  16.1 us (1%)
    reduce_scatter x1, waiting for transfers between devices, body(): lax.psum_scatter(picker[:, None, None] * grad_up[None], ('items', 'stream...  208 us
    reduce_scatter x1, waiting for transfers between devices, body(): lax.psum_scatter(picker[:, None, None] * grad_down[None], ('items', 'stre...  153 us
    reduce_scatter x1, waiting for transfers between devices, body(): lax.psum_scatter(grad_qkv, ('items', 'stream'), scatter_dimension=0, tile...  125 us
    reduce_scatter x1, waiting for transfers between devices, body(): lax.psum_scatter(grad_out_weight, ('items', 'stream'), scatter_dimension=...  102 us
    unnamed x2, blocking collectives  83.2 us
    all_gather x1, waiting for transfers between devices, body(): lax.all_gather(w_up, ('items', 'stream'), axis=1, tiled=True)  80.4 us
    dot_general x28, matrix products, product(): return jnp.dot(first_op, second_op, preferred_element_type=jnp.float32)  72.9 us
    dot_general x28, matrix products, product_trail(): lax.dot_general(first_op, second_op, (((1,), (1,)), ((), ())), preferred_...  66 us
  transfers between devices with their start and end apart: 13, of which 9 were waited for; matrix products, arithmetic and copies ran while one was open for 17% of the time, Pallas kernels for 0%

commit v1 on v0

--- a/solution.py
+++ b/solution.py
@@ -1,6 +1,10 @@
+import functools
+
 import jax
 import jax.numpy as jnp
 from jax import lax
+from jax.experimental import pallas as pl
+from jax.experimental.pallas import tpu as pltpu
 from jax.sharding import PartitionSpec as P
 
 HEADS = 12
@@ -55,7 +59,341 @@
     )
 
 
+def halves(length):
+    return ((0, length // 2), (length // 2, length // 2))
+
+
+def gather_chunks(model_rows, width, ff_rows, ff):
+    rows, down_rows = (0, model_rows), (0, ff_rows)
+    chunks = [
+        [((0, None), (0, 16), (0, 128), 0, False)]
+        + [((1, None), rows, cols, order, False) for order, cols in enumerate(halves(3 * width))],
+        [((2, None), rows, cols, order, False) for order, cols in enumerate(halves(width))],
+    ]
+    for e in range(2):
+        chunks.append([((3, e), rows, cols, o, e == 1) for o, cols in enumerate(halves(ff))])
+        chunks.append(
+            [((4, e), band, (0, width), o, e == 1) for o, band in enumerate(halves(ff_rows))]
+        )
+    return chunks
+
+
+def scatter_chunks(model_rows, width, ff_rows, ff):
+    rows = (0, model_rows)
+    chunks = []
+    for e in range(2):
+        chunks.append([(0, e, rows, cols, order) for order, cols in enumerate(halves(ff))])
+        chunks.append(
+            [(1, e, band, (0, width), order) for order, band in enumerate(halves(ff_rows))]
+        )
+    chunks.append([(2, 0, rows, cols, order) for order, cols in enumerate(halves(width))])
+    chunks.append(
+        [(3, 0, rows, cols, order) for order, cols in enumerate(halves(3 * width))]
+        + [(4, 0, (0, 8), (0, 128), 0)]
+    )
+    return chunks
+
+
+MESH = pl.DeviceIdType.MESH
+GATHER_ORDERS = (("z", "x", "y"), ("z", "y", "x"), ("y", "x", "z"))
+SCATTER_ORDERS = (("y", "x"), ("x", "y"))
+
+
+def coords():
+    items, stream = lax.axis_index("items"), lax.axis_index("stream")
+    return dict(z=items // 2, x=items % 2, y=stream // 2, c=stream % 2)
+
+
+def place(at):
+    return (at["z"] * 2 + at["x"], at["y"] * 2 + at["c"])
+
+
+def moved(at, dim, by, depth):
+    return {**at, dim: lax.rem(at[dim] + by, depth if dim == "z" else 2)}
+
+
+def greet(at, depth):
+    peers = [moved(at, "z", k, depth) for k in range(1, depth)]
+    peers += [moved(at, d, 1, depth) for d in "xyc"]
+    barrier = pltpu.get_barrier_semaphore()
+    for peer in peers:
+        pl.semaphore_signal(barrier, inc=1, device_id=place(peer), device_id_type=MESH)
+    pl.semaphore_wait(barrier, len(peers))
+
+
+def guard(cond, act):
+    if cond is None:
+        act()
+    else:
+        pl.when(cond)(act)
+
+
+def pipelined(chunks, n_steps, ahead, start, wait):
+    count = len(chunks)
+    for j in range(min(ahead, count)):
+        start(chunks[j], 0)
+    for t in range(count + n_steps - 1):
+        if t + ahead < count:
+            start(chunks[t + ahead], 0)
+        for step in range(n_steps - 1, -1, -1):
+            j = t - step
+            if 0 <= j < count:
+                wait(chunks[j], step)
+                if step < n_steps - 1:
+                    start(chunks[j], step + 1)
+
+
+def gather_kernel(depth, chunks, entries, n_in, *refs):
+    ins, outs = refs[:n_in], refs[n_in : 2 * n_in]
+    local_sem, send_sem, recv_sem = refs[2 * n_in :]
+    at = coords()
+    mine = (at["z"], at["x"], at["y"], at["c"])
+
+    def source(entry):
+        k, e = entry
+        return ins[k] if e is None else ins[k].at[e]
+
+    def target(entry):
+        k, e = entry
+        return outs[k] if e is None else outs[k].at[e]
+
+    local = [
+        pltpu.make_async_copy(source(entry), target(entry).at[mine], local_sem.at[j])
+        for j, entry in enumerate(entries)
+    ]
+    for copy in local:
+        copy.start()
+    greet(at, depth)
+    for copy in local:
+        copy.wait()
+    lower, upper = at["y"] == 0, at["y"] == 1
+    number = {piece: j for j, piece in enumerate(piece for chunk in chunks for piece in chunk)}
+
+    def stage(piece, step):
+        entry, rows, cols, order, text = piece
+        dims = GATHER_ORDERS[order] + ("c",)
+        dim = dims[step]
+        held = tuple(slice(None) if d in dims[:step] else pl.ds(at[d], 1) for d in "zxyc")
+        view = target(entry).at[held + (pl.ds(*rows), pl.ds(*cols))]
+        sends = recvs = None
+        if text and dim == "y":
+            sends, recvs = lower, upper
+        elif text and "y" in dims[:step]:
+            sends = recvs = upper
+        found = []
+        for k in range(1, depth if dim == "z" else 2):
+            sem = {"z": k - 1, "x": depth - 1, "y": depth, "c": depth + 1}[dim]
+            found.append(
+                pltpu.make_async_remote_copy(
+                    src_ref=view,
+                    dst_ref=view,
+                    send_sem=send_sem.at[number[piece], sem],
+                    recv_sem=recv_sem.at[number[piece], sem],
+                    device_id=place(moved(at, dim, k, depth)),
+                    device_id_type=MESH,
+                )
+            )
+        return found, sends, recvs
+
+    def each(chunk, step, which, call):
+        for piece in chunk:
+            found = stage(piece, step)
+
+            def act(copies=found[0]):
+                for copy in copies:
+                    call(copy)
+
+            guard(found[which], act)
+
+    pipelined(
+        chunks,
+        4,
+        2,
+        lambda chunk, step: each(chunk, step, 1, lambda copy: copy.start()),
+        lambda chunk, step: each(chunk, step, 2, lambda copy: copy.wait_recv()),
+    )
+    for chunk in chunks:
+        for step in range(4):
+            each(chunk, step, 1, lambda copy: copy.wait_send())
+
+
+def gather_all(arrays, lead, chunks, depth):
+    n_in = len(arrays)
+    entries = []
+    out_shape = []
+    for k, (array, wide) in enumerate(zip(arrays, lead)):
+        entries += [(k, e) for e in range(array.shape[0])] if wide else [(k, None)]
+        head = array.shape[:1] if wide else ()
+        out_shape.append(
+            jax.ShapeDtypeStruct(head + (depth, 2, 2, 2) + array.shape[-2:], array.dtype)
+        )
+    n_pieces = sum(len(chunk) for chunk in chunks)
+    anywhere = pl.BlockSpec(memory_space=pl.ANY)
+    return pl.pallas_call(
+        functools.partial(gather_kernel, depth, chunks, entries, n_in),
+        out_shape=out_shape,
+        in_specs=[anywhere] * n_in,
+        out_specs=[anywhere] * n_in,
+        scratch_shapes=[pltpu.SemaphoreType.DMA((len(entries),))]
+        + [pltpu.SemaphoreType.DMA((n_pieces, depth + 2))] * 2,
+        compiler_params=pltpu.CompilerParams(
+            collective_id=1, has_side_effects=True, vmem_limit_bytes=16 << 20
+        ),
+    )(*arrays)
+
+
+def scatter_kernel(depth, kinds, chunks, *refs):
+    n = len(kinds)
+    ins, factor, outs = refs[:n], refs[n], refs[n + 1 : 2 * n + 1]
+    acc, first, second, last = (
+        refs[2 * n + 1 + k * n : 2 * n + 1 + (k + 1) * n] for k in range(4)
+    )
+    send_sem, recv_sem = refs[6 * n + 1 :]
+    at = coords()
+    z, x, y, c = (at[d] for d in "zxyc")
+    greet(at, depth)
+    lower, upper = y == 0, y == 1
+    text_device = jnp.logical_and(upper, c == 1)
+    image_device = jnp.logical_or(lower, c == 0)
+    beside_text = jnp.logical_and(upper, c == 0)
+    beside_image = jnp.logical_or(lower, c == 1)
+    number = {piece: j for j, piece in enumerate(piece for chunk in chunks for piece in chunk)}
+    every = slice(None)
+
+    def copies_of(piece, step):
+        k, e, rows, cols, order = piece
+        box = (pl.ds(*rows), pl.ds(*cols))
+        image, text = kinds[k] and e == 0, kinds[k] and e == 1
+        dims = ("c",) + SCATTER_ORDERS[order] + ("z",)
+        dim = dims[step]
+        here = acc[k].at[e]
+
+        def make(src, dst, sem, by=1):
+            return pltpu.make_async_remote_copy(
+                src_ref=src,
+                dst_ref=dst,
+                send_sem=send_sem.at[number[piece], sem],
+                recv_sem=recv_sem.at[number[piece], sem],
+                device_id=place(moved(at, dim, by, depth)),
+                device_id_type=MESH,
+            )
+
+        sends = recvs = None
+        if dim == "c":
+            if image:
+                sends, recvs = image_device, beside_image
+            elif text:
+                sends, recvs = text_device, beside_text
+            src = ins[k].at[(every, every, every, 1 - c) + box]
+            return [(make(src, here.at[(every, every, every) + box], 0), sends, recvs)]
+        if dim == "z":
+            found = []
+            for by in range(1, depth):
+                src = here.at[(lax.rem(z + by, depth), x, y) + box]
+                found.append((make(src, last[k].at[(e, by - 1) + box], 2 + by, by), None, None))
+            return found
+        if text and dim == "y":
+            sends, recvs = upper, lower
+        elif text and step == 1:
+            sends = recvs = upper
+        if step == 1:
+            spot = (every, every, 1 - y) if dim == "y" else (every, 1 - x, every)
+            dst = first[k].at[(e, every, every) + box]
+        else:
+            spot = (every, x, 1 - y) if dim == "y" else (every, 1 - x, y)
+            dst = second[k].at[(e, every) + box]
+        return [(make(here.at[spot + box], dst, step), sends, recvs)]
+
+    def combine(piece, step):
+        k, e, rows, cols, order = piece
+        box = (pl.ds(*rows), pl.ds(*cols))
+        image, text = kinds[k] and e == 0, kinds[k] and e == 1
+        here = acc[k].at[e]
+
+        def over(spots, value_of, keep):
+            @pl.loop(0, depth)
+            def _(level):
+                for index, spot in enumerate(spots):
+                    where = (level,) + spot + box
+                    value = value_of(level, index, spot)
+                    here[where] = value if keep else here[where] + value
+
+        if step == 0:
+            spots = [(0, 0), (0, 1), (1, 0), (1, 1)]
+            own = lambda level, index, spot: ins[k][(level,) + spot + (c,) + box]
+            if image:
+                pl.when(lower)(lambda: over(spots, own, False))
+                pl.when(beside_text)(lambda: over(spots, own, True))
+            elif text:
+                pl.when(text_device)(lambda: over(spots, own, True))
+            else:
+                over(spots, own, False)
+        elif step == 1:
+            dim = SCATTER_ORDERS[order][0]
+            spots = [(0, y), (1, y)] if dim == "y" else [(x, 0), (x, 1)]
+            got = lambda level, index, spot: first[k][(e, level, index) + box]
+            if text and dim == "y":
+                pl.when(lower)(lambda: over(spots, got, True))
+            elif text:
+                pl.when(upper)(lambda: over(spots, got, False))
+            else:
+                over(spots, got, False)
+        elif step == 2:
+            dim = SCATTER_ORDERS[order][1]
+            got = lambda level, index, spot: second[k][(e, level) + box]
+            if text and dim == "y":
+                pl.when(lower)(lambda: over([(x, y)], got, True))
+            else:
+                over([(x, y)], got, False)
+        else:
+            total = here[(z, x, y) + box].astype(jnp.float32)
+            for by in range(depth - 1):
+                total = total + last[k][(e, by) + box].astype(jnp.float32)
+            if kinds[k]:
+                total = total * factor[0:1, e * 128 : e * 128 + 1]
+            outs[k][(e,) + box] = total
+
+    def start(chunk, step):
+        for piece in chunk:
+            for copy, sends, _ in copies_of(piece, step):
+                guard(sends, copy.start)
+
+    def wait(chunk, step):
+        for piece in chunk:
+            for copy, _, recvs in copies_of(piece, step):
+                guard(recvs, copy.wait_recv)
+            combine(piece, step)
+
+    pipelined(chunks, 4, 2, start, wait)
+    for chunk in chunks:
+        for step in range(4):
+            for piece in chunk:
+                for copy, sends, _ in copies_of(piece, step):
+                    guard(sends, copy.wait_send)
+
+
+def scatter_all(arrays, factor, kinds, chunks, depth, collective):
+    n = len(arrays)
+    n_pieces = sum(len(chunk) for chunk in chunks)
+    inside = pl.BlockSpec(memory_space=pltpu.VMEM)
+    shapes = [((2 if kind else 1,), a.shape[4:], a.dtype) for kind, a in zip(kinds, arrays)]
+    scratch = []
+    for middle in ((depth, 2, 2), (depth, 2), (depth,), (depth - 1,)):
+        scratch += [pltpu.VMEM(head + middle + tail, dtype) for head, tail, dtype in shapes]
+    return pl.pallas_call(
+        functools.partial(scatter_kernel, depth, kinds, chunks),
+        out_shape=[jax.ShapeDtypeStruct(head + tail, jnp.float32) for head, tail, _ in shapes],
+        in_specs=[inside] * (n + 1),
+        out_specs=[inside] * n,
+        scratch_shapes=scratch + [pltpu.SemaphoreType.DMA((n_pieces, depth + 2))] * 2,
+        compiler_params=pltpu.CompilerParams(
+            collective_id=collective, has_side_effects=True, vmem_limit_bytes=60 << 20
+        ),
+    )(*arrays, factor)
+
+
 def body(
+    near,
     tokens,
     group_kind,
     ln1_gain,
@@ -83,44 +421,55 @@
     key_member = layout(
         group_type, jnp.arange(stream_size * row_count, dtype=jnp.int32), row_count
     )[0]
-    local_counts = jnp.stack(
-        [
-            jnp.sum((own_modality == 0).astype(jnp.float32)),
-            jnp.sum((own_modality == 1).astype(jnp.float32)),
-        ]
-    )
-    totals = lax.psum(local_counts, ("items", "stream"))
-    gathered = (
-        lax.all_gather(ln1_gain, ("items", "stream"), axis=0, tiled=True),
-        lax.all_gather(ln1_bias, ("items", "stream"), axis=0, tiled=True),
-        lax.all_gather(w_qkv, ("items", "stream"), axis=0, tiled=True),
-        lax.all_gather(q_bias, ("items", "stream"), axis=0, tiled=True),
-        lax.all_gather(v_bias, ("items", "stream"), axis=0, tiled=True),
-        lax.all_gather(w_out, ("items", "stream"), axis=0, tiled=True),
-        lax.all_gather(out_bias, ("items", "stream"), axis=0, tiled=True),
-        lax.all_gather(ln2_gain, ("items", "stream"), axis=0, tiled=True),
-        lax.all_gather(ln2_bias, ("items", "stream"), axis=0, tiled=True),
-        lax.all_gather(w_up, ("items", "stream"), axis=1, tiled=True),
-        lax.all_gather(b_up, ("items", "stream"), axis=1, tiled=True),
-        lax.all_gather(w_down, ("items", "stream"), axis=1, tiled=True),
-        lax.all_gather(b_down, ("items", "stream"), axis=1, tiled=True),
-    )
-    (
-        gain_one,
-        shift_one,
-        qkv_weight,
-        query_shift,
-        value_shift,
-        out_weight,
-        out_shift,
-        gain_two,
-        shift_two,
-        up_all,
-        up_shift_all,
-        down_all,
-        down_shift_all,
-    ) = gathered
+    devices = lax.axis_size("items") * stream_size
+    totals = None
     expert_pick = jnp.where(stream_place == stream_size - 1, 1, 0).astype(jnp.int32)
+    share, ff_share, ff = model_width // devices, w_down.shape[1], w_up.shape[2]
+    thin = jnp.concatenate(
+        [ln1_gain, ln1_bias, q_bias, v_bias, out_bias, ln2_gain, ln2_bias]
+        + [b_up.reshape(-1), b_down.reshape(-1), group_kind.astype(jnp.bfloat16)]
+    )
+    thin = jnp.pad(thin, (0, 2048 - thin.shape[0])).reshape(16, 128)
+    if near:
+        depth = lax.axis_size("items") // 2
+        thin_all, qkv_weight, out_weight, up_all, down_all = gather_all(
+            [thin, w_qkv, w_out, w_up, w_down],
+            [False, False, False, True, True],
+            gather_chunks(share, model_width, ff_share, ff),
+            depth,
+        )
+        qkv_weight = qkv_weight.reshape(model_width, -1)
+        out_weight = out_weight.reshape(model_width, model_width)
+        up_all = up_all.reshape(2, model_width, ff)
+        down_all = down_all.reshape(2, ff, model_width)
+    else:
+        both = ("items", "stream")
+        thin_all = lax.all_gather(thin, both, axis=0, tiled=True)
+        qkv_weight = lax.all_gather(w_qkv, both, axis=0, tiled=True)
+        out_weight = lax.all_gather(w_out, both, axis=0, tiled=True)
+        up_all = lax.all_gather(w_up, both, axis=1, tiled=True)
+        down_all = lax.all_gather(w_down, both, axis=1, tiled=True)
+    thin_all = thin_all.reshape(devices, 2048)
+    cut = 7 * share
+    seven = thin_all[:, :cut].reshape(devices, 7, share).transpose(1, 0, 2).reshape(7, model_width)
+    gain_one, shift_one, query_shift, value_shift, out_shift, gain_two, shift_two = seven
+    up_shift_all = (
+        thin_all[:, cut : cut + 2 * ff_share].reshape(devices, 2, ff_share).transpose(1, 0, 2)
+    ).reshape(2, ff)
+    cut = cut + 2 * ff_share
+    down_shift_all = (
+        thin_all[:, cut : cut + 2 * share].reshape(devices, 2, share).transpose(1, 0, 2)
+    ).reshape(2, model_width)
+    kinds = thin_all[::stream_size, cut + 2 * share].astype(jnp.int32)
+    tally = []
+    for kind in range(2):
+        modality = layout(
+            jnp.int32(kind), jnp.arange(stream_size * row_count, dtype=jnp.int32), row_count
+        )[1]
+        tally.append([jnp.sum((modality == e).astype(jnp.float32)) for e in range(2)])
+    totals = jnp.stack(
+        [jnp.sum(jnp.where(kinds == 0, tally[0][e], tally[1][e])) for e in range(2)]
+    )
     tokens_f = tokens.astype(jnp.float32)
     normed_one, pull_one = jax.vjp(
         layer_norm, tokens_f, gain_one.astype(jnp.float32), shift_one.astype(jnp.float32)
@@ -180,33 +529,6 @@
     pre_grad = pull_gelu(hidden_grad)[0].astype(jnp.bfloat16)
     grad_up = product_lead(normed_two_low, pre_grad)
     grad_up_shift = jnp.sum(pre_grad.astype(jnp.float32), axis=0)
-    picker = (jnp.arange(2, dtype=jnp.int32) == expert_pick).astype(jnp.float32)
-    expert_summed = (
-        lax.psum_scatter(
-            picker[:, None, None] * grad_up[None],
-            ("items", "stream"),
-            scatter_dimension=1,
-            tiled=True,
-        ),
-        lax.psum_scatter(
-            picker[:, None] * grad_up_shift[None],
-            ("items", "stream"),
-            scatter_dimension=1,
-            tiled=True,
-        ),
-        lax.psum_scatter(
-            picker[:, None, None] * grad_down[None],
-            ("items", "stream"),
-            scatter_dimension=1,
-            tiled=True,
-        ),
-        lax.psum_scatter(
-            picker[:, None] * grad_down_shift[None],
-            ("items", "stream"),
-            scatter_dimension=1,
-            tiled=True,
-        ),
-    )
     norm_two_grad = product_trail(pre_grad, up_weight)
     residual_part, grad_gain_two, grad_shift_two = pull_two(norm_two_grad)
     residual_grad = out_grad + residual_part
@@ -249,34 +571,69 @@
     norm_one_grad = product_trail(qkv_grad, qkv_weight)
     token_part, grad_gain_one, grad_shift_one = pull_one(norm_one_grad)
     token_grad = (residual_grad + token_part).astype(jnp.bfloat16)
-    summed = (
-        lax.psum_scatter(grad_gain_one, ("items", "stream"), scatter_dimension=0, tiled=True),
-        lax.psum_scatter(grad_shift_one, ("items", "stream"), scatter_dimension=0, tiled=True),
-        lax.psum_scatter(grad_qkv, ("items", "stream"), scatter_dimension=0, tiled=True),
-        lax.psum_scatter(grad_query_shift, ("items", "stream"), scatter_dimension=0, tiled=True),
-        lax.psum_scatter(grad_value_shift, ("items", "stream"), scatter_dimension=0, tiled=True),
-        lax.psum_scatter(grad_out_weight, ("items", "stream"), scatter_dimension=0, tiled=True),
-        lax.psum_scatter(grad_out_shift, ("items", "stream"), scatter_dimension=0, tiled=True),
-        lax.psum_scatter(grad_gain_two, ("items", "stream"), scatter_dimension=0, tiled=True),
-        lax.psum_scatter(grad_shift_two, ("items", "stream"), scatter_dimension=0, tiled=True),
-    )
     factor = lax.rsqrt(totals)
+    pick = (jnp.arange(2, dtype=jnp.int32) == expert_pick).astype(jnp.float32)[:, None] * factor[:, None]
+
+    def dealt(vector):
+        return vector.reshape(devices, -1)
+
+    thin_grad = jnp.concatenate(
+        [dealt(v) for v in (grad_gain_one, grad_shift_one, grad_query_shift, grad_value_shift)]
+        + [dealt(v) for v in (grad_out_shift, grad_gain_two, grad_shift_two)]
+        + [(pick * grad_up_shift[None]).reshape(2, devices, ff_share).transpose(1, 0, 2).reshape(devices, -1)]
+        + [(pick * grad_down_shift[None]).reshape(2, devices, share).transpose(1, 0, 2).reshape(devices, -1)],
+        axis=1,
+    )
+    thin_grad = jnp.pad(thin_grad, ((0, 0), (0, 1024 - thin_grad.shape[1])))
+    if near:
+        box = (depth, 2, 2, 2)
+        low = jnp.bfloat16
+        up_sum, down_sum, out_sum, qkv_sum, thin_sum = scatter_all(
+            [
+                grad_up.astype(low).reshape(box + (share, ff)),
+                grad_down.astype(low).reshape(box + (ff_share, model_width)),
+                grad_out_weight.astype(low).reshape(box + (share, model_width)),
+                grad_qkv.astype(low).reshape(box + (share, 3 * model_width)),
+                thin_grad.reshape(box + (8, 128)),
+            ],
+            jnp.broadcast_to(jnp.repeat(factor, 128)[None], (8, 256)),
+            (True, True, False, False, False),
+            scatter_chunks(share, model_width, ff_share, ff),
+            depth,
+            2,
+        )
+        out_sum, qkv_sum = out_sum[0], qkv_sum[0]
+    else:
+        both = ("items", "stream")
+        scatter = functools.partial(
+            lax.psum_scatter, axis_name=both, scatter_dimension=0, tiled=True
+        )
+        wide = functools.partial(lax.psum_scatter, axis_name=both, scatter_dimension=1, tiled=True)
+        up_sum = wide(pick[:, :, None] * grad_up[None])
+        down_sum = wide(pick[:, :, None] * grad_down[None])
+        out_sum, qkv_sum, thin_sum = scatter(grad_out_weight), scatter(grad_qkv), scatter(thin_grad)
+    thin_sum = thin_sum.reshape(-1)
+    seven = [thin_sum[k * share : (k + 1) * share] for k in range(7)]
+    cut = 7 * share
+    up_shift_sum = thin_sum[cut : cut + 2 * ff_share].reshape(2, ff_share)
+    cut = cut + 2 * ff_share
+    down_shift_sum = thin_sum[cut : cut + 2 * share].reshape(2, share)
     return (
         output,
         token_grad,
-        summed[0],
-        summed[1],
-        summed[2],
-        summed[3],
-        summed[4],
-        summed[5],
-        summed[6],
-        summed[7],
-        summed[8],
-        expert_summed[0] * factor[:, None, None],
-        expert_summed[1] * factor[:, None],
-        expert_summed[2] * factor[:, None, None],
-        expert_summed[3] * factor[:, None],
+        seven[0],
+        seven[1],
+        qkv_sum,
+        seven[2],
+        seven[3],
+        out_sum,
+        seven[4],
+        seven[5],
+        seven[6],
+        up_sum,
+        up_shift_sum,
+        down_sum,
+        down_shift_sum,
         totals,
     )
 
@@ -300,8 +657,9 @@
         P(None, ("items", "stream")),
         P(("items", "stream"), None),
     )
+    near = mesh.shape["items"] == 8 and mesh.shape["stream"] == 4
     return jax.shard_map(
-        body,
+        functools.partial(body, near),
         mesh=mesh,
         in_specs=placed,
         out_specs=(

time: 1310 us -> 651 us (0.50)
  waiting for transfers between devices: 822 us -> 70.9 us
  Pallas kernels: 0 us -> 245 us
  blocking collectives: 163 us -> 0 us
  local copies, waits for them, and re-layouts: 36.5 us -> 66.4 us
  matrix products: 204 us -> 187 us
    reduce_scatter x4 -> x0, waiting for transfers between devices: 589 us -> none  [the longest x1 208 us: body(): lax.psum_scatter(picker[:, None, None] * grad_up[None], ('items', 'stream...]
    pallas_call x0 -> x2, Pallas kernels: none -> 245 us  [the longest x1 127 us: scatter_all(): pl.pallas_call(functools.partial(scatter_kernel, depth, kinds, chunks), o...]
    all_gather x4 -> x0, waiting for transfers between devices: 158 us -> none  [the longest x1 80.4 us: body(): lax.all_gather(w_up, ('items', 'stream'), axis=1, tiled=True)]
    unnamed x2 -> x0, blocking collectives: 83.2 us -> none
    all_gather x2 -> x0, blocking collectives: 79.8 us -> none  [the longest x1 40.5 us: body(): lax.all_gather(b_down, ('items', 'stream'), axis=1, tiled=True)]
    unnamed x14 -> x4, waiting for transfers between devices: 43.9 us -> 0.07 us
    all_gather x1, waiting for transfers between devices: 0.02 us -> 32.6 us  [body(): lax.all_gather(keys_own, 'stream', axis=0, tiled=True)]
    mul x8 -> x3, other arithmetic: 23.1 us -> 0.7 us  [the longest x1 0.62 us: body(): pick * grad_up_shift[None]]
  transfers between devices with their start and end apart: 13 -> 4, of which waited for: 9 -> 2; matrix products, arithmetic and copies ran while one was open for 17% -> 18% of each run, Pallas kernels for 0% -> 0%
where the time goes in v1:
time: 651 us; the launch traced here: 645 us
  Pallas kernels  245 us (38%)
  matrix products  187 us (29%)
  waiting for transfers between devices  70.9 us (11%)
  local copies, waits for them, and re-layouts  66.4 us (10%)
  other arithmetic  59.1 us (9%)
  between operations  16.3 us (3%)
    pallas_call x1, Pallas kernels, scatter_all(): pl.pallas_call(functools.partial(scatter_kernel, depth, kinds, chunks), o...  127 us
    pallas_call x1, Pallas kernels, gather_all(): pl.pallas_call(functools.partial(gather_kernel, depth, chunks, entries, n...  118 us
    dot_general x28, matrix products, product_lead(): lax.dot_general(first_op, second_op, (((0,), (0,)), ((), ())), preferred_...  67.9 us
    dot_general x28, matrix products, product(): return jnp.dot(first_op, second_op, preferred_element_type=jnp.float32)  64.5 us
    dot_general x28, matrix products, product_trail(): lax.dot_general(first_op, second_op, (((1,), (1,)), ((), ())), preferred_...  54.3 us
    unnamed x318, local copies, waits for them, and re-layouts  41.3 us
    reduce_scatter x1, waiting for transfers between devices, body(): lax.psum_scatter(value_terms, 'stream', scatter_dimension=0, tiled=True)  38.2 us
    all_gather x1, waiting for transfers between devices, body(): lax.all_gather(keys_own, 'stream', axis=0, tiled=True)  32.6 us
  transfers between devices with their start and end apart: 4, of which 2 were waited for; matrix products, arithmetic and copies ran while one was open for 18% of the time, Pallas kernels for 0%

profile of v1, /device:TPU:0, one launch (start us, length us, event | category | flops | bytes accessed | tf_op | source)
XLA Modules:
  0.0 645.2 jit_solution(11458611463764838306)
XLA Ops:
  9.4 4.8 concatenate.28
  17.7 118.0 %shard_map.279 = (bf16[4,2,2,2,16,128]{5,4,3,2,1,0:T(8,128)(2,1)S(1)}, bf16[4,2,2,2,24,2304]{5,4,3,2,1,0:T(8,128)(2,1)S(1)}, bf16[4,2,2,2,24,768]{5,4,3,2,1,0:T(...) custom-call(bf16[16,128]{1,0:T(8,128)(2,1)S(1)} %pad_bitcast_fusion.1.refs_0_, ...), custom_call_target="tpu_custom_call" | custom-call | tf_op jit(solution)/shard_map/pallas_call | solution.py:232
  135.8 3.6 copy-done.4
  139.4 3.6 copy-done.5
  145.9 2.1 fusion.230
  152.1 1.5 fusion.87
  154.2 3.3 fusion.268
  157.5 2.1 copy-done.93
  162.3 3.0 fusion.90
  167.3 32.6 %all-gather.3.cloned.1.call-done = bf16[2048,768]{1,0:T(8,128)(2,1)} async-done(((bf16[512,768]{1,0:T(8,128)(2,1)}), bf16[2048,768]{1,0:T(8,128)(2,1)}) %all-gather.3.cloned.1.call-update) | async-done | bytes 3145744 | tf_op jit(solution)/shard_map/all_gather | solution.py:485
  199.9 2.0 fusion.277
  232.4 2.0 copy-done.51
  235.7 3.4 fusion.106
  266.1 18.7 %multiply_convert_fusion = (bf16[512,3072]{1,0:T(8,128)(2,1)}, f32[512,3072]{1,0:T(8,128)}, f32[512,3072]{1,0:T(8,128)}) fusion(f32[3072]{0:T(1024)S(1)} %bitcast.123, bf16[2,768,3072]{2,1,0:T(8,128)(2,1)S(1)} %bitcast.104, s32[]{:T(128)S(6)} %select_n.284, f32[512,768]{1,0:T(8,128)S(1)} %get-tuple-element.119, f32[768]{0:T(1024)S(1)} %reshape.547, ...), kind=kOutput, calls=%fused_computation.16 | convolution fusion | flops 2521694208 | bytes 22044676 | tf_op jit(solution)/shard_map/dot_general | solution.py:47
  284.8 9.0 %convert_reduce_fusion = (f32[3072]{0:T(1024)S(1)}, bf16[512,3072]{1,0:T(8,128)(2,1)}) fusion(f32[512,3072]{1,0:T(8,128)} %get-tuple-element.59, bf16[2,3072,768]{2,1,0:T(8,128)(2,1)S(1)} %bitcast.97, s32[]{:T(128)S(6)} %select_n.284, bf16[512,768]{1,0:T(8,128)(2,1)S(1)} %copy-done.94, f32[512]{0:T(512)S(1)} %get-tuple-element.150, ...), kind=kOutput, calls=%fused_computation.14 | convolution fusion | flops 2444227584 | bytes 21262340 | tf_op jit(solution)/shard_map/dot_general | solution.py:57
  293.8 6.8 %multiply_reduce_fusion.12 = (f32[768]{0:T(1024)S(1)}, f32[512]{0:T(512)S(1)}, f32[768]{0:T(1024)S(1)}, f32[512,768]{1,0:T(8,128)S(1)}) fusion(f32[512,768]{1,0:T(8,128)} %copy-done.89, f32[512]{0:T(512)S(1)} %fusion.262, f32[512]{0:T(512)S(1)} %broadcast_multiply_fusion.1, f32[768]{0:T(1024)S(1)} %reshape.546, bf16[512,3072]{1,0:T(8,128)(2,1)} %get-tuple-element.148, ...), kind=kOutput, calls=%fused_computation.200 | convolution fusion | flops 2419062784 | bytes 11025412 | tf_op jit(solution)/shard_map/dot_general | solution.py:57
  318.0 1.5 convolution_dynamic-update-slice_fusion.20
  321.6 1.5 convolution_dynamic-update-slice_fusion.19
  325.4 3.0 convolution_dynamic-update-slice_fusion.18
  328.4 2.1 multiply_reduce_fusion.5
  331.6 2.9 convolution_dynamic-update-slice_fusion.17
  334.6 2.3 multiply_reduce_fusion.4
  338.0 3.0 convolution_dynamic-update-slice_fusion.16
  341.0 2.4 multiply_reduce_fusion.3
  344.5 2.9 convolution_dynamic-update-slice_fusion.15
  347.4 2.3 multiply_reduce_fusion.2
  350.8 3.0 convolution_dynamic-update-slice_fusion.14
  353.8 2.1 multiply_reduce_fusion.1
  357.1 2.9 convolution_dynamic-update-slice_fusion.13
  360.0 2.3 multiply_reduce_fusion
  364.7 2.4 convolution_dynamic-update-slice_fusion.12
  367.6 4.0 convolution_dynamic-update-slice_fusion.11
  371.6 1.6 convolution_dynamic-update-slice_fusion.10
  373.3 1.6 convolution_dynamic-update-slice_fusion.9
  375.1 1.7 convolution_dynamic-update-slice_fusion.8
  377.0 1.6 convolution_dynamic-update-slice_fusion.7
  379.5 1.6 convolution_dynamic-update-slice_fusion.6
  381.1 1.7 convolution_dynamic-update-slice_fusion.5
  382.8 1.6 convolution_dynamic-update-slice_fusion.4
  384.4 1.7 convolution_dynamic-update-slice_fusion.3
  386.1 1.7 convolution_dynamic-update-slice_fusion.2
  387.8 1.7 convolution_dynamic-update-slice_fusion.1
  389.5 1.6 convolution_dynamic-update-slice_fusion
  395.3 3.2 select_reduce_fusion.1
  401.6 2.8 constant_dynamic-update-slice_fusion.23
  404.4 3.4 constant_dynamic-update-slice_fusion.22
  407.8 2.6 constant_dynamic-update-slice_fusion.21
  410.4 1.6 constant_dynamic-update-slice_fusion.20
  413.4 1.6 constant_dynamic-update-slice_fusion.18
  416.4 1.6 constant_dynamic-update-slice_fusion.16
  419.3 1.6 constant_dynamic-update-slice_fusion.14
  422.3 1.6 constant_dynamic-update-slice_fusion.12
  427.9 1.8 convolution_convert_fusion.3
  429.8 7.5 %convolution_convert_fusion.1 = bf16[3072,768]{1,0:T(8,128)(2,1)} fusion(bf16[512,3072]{1,0:T(8,128)(2,1)} %get-tuple-element.58, bf16[512,768]{1,0:T(8,128)(2,1)S(1)} %copy-done.95, f32[512]{0:T(512)S(1)} %get-tuple-element.150, f32[512]{0:T(512)S(1)} %get-tuple-element.149), kind=kOutput, calls=%fused_computation.31 | convolution fusion | flops 2419851264 | bytes 8654848 | tf_op jit(solution)/shard_map/dot_general | solution.py:51
  437.2 5.1 convolution_convert_fusion.2
  442.3 3.5 add_convert_fusion.2
  445.9 2.6 convert_dynamic-update-slice_fusion
  448.4 38.2 %reduce-scatter.5.cloned.1.call-done = f32[512,768]{0,1:T(8,128)} async-done(((f32[2048,768]{0,1:T(8,128)}), f32[512,768]{0,1:T(8,128)}) %reduce-scatter.5.cloned.1.call-update) | async-done | bytes 1572880 | tf_op jit(solution)/shard_map/reduce_scatter | solution.py:558
  486.6 2.4 convert_dynamic-update-slice_fusion.1
  489.0 4.9 fusion.271
  494.1 4.1 convolution_convert_fusion
  501.0 127.2 %shard_map.280 = (f32[2,24,3072]{2,1,0:T(8,128)}, f32[2,96,768]{2,1,0:T(8,128)}, f32[1,24,768]{2,1,0:T(8,128)}, f32[1,24,2304]{2,1,0:T(8,128)}, f32[1,8,128]{2,1,0:T(8,128)}) custom-call(bf16[4,2,2,2,24,3072]{5,4,3,2,1,0:T(8,128)(2,1)} %bitcast.110, bf16[4,2,2,2,96,768]{5,4,3,2,1,0:T(8,128)(2,1)} %bitcast.109, bf16[4,2,2,2,24,768]{5,4,3,2,1,0:T(8,128)(2,1)} %bitcast.112, ...), custom_call_target="tpu_custom_call" | custom-call | tf_op jit(solution)/shard_map/pallas_call | solution.py:383
  628.2 1.5 fusion.276
  632.6 2.9 add_convert_fusion.1
  (473 shorter events, 132.1 us)
Async XLA Ops:
  7.2 192.8 %all-gather.3.cloned.1.call-start = ((), (), s32[]{:S(2)}) async-start(), calls=%async_computation.2 | async-start | bytes 3932160 | tf_op jit(solution)/shard_map/all_gather | solution.py:485
  144.0 13.5 %copy-start.6 = (bf16[4,2,2,2,24,2304]{5,4,3,2,1,0:T(8,128)(2,1)}, bf16[4,2,2,2,24,2304]{5,4,3,2,1,0:T(8,128)(2,1)S(1)}, u32[]{:S(2)}) copy-start(bf16[4,2,2,2,24,2304]{5,4,3,2,1,0:T(8,128)(2,1)S(1)} %get-tuple-element.27) | copy-start | bytes 10616836
  152.1 5.4 copy-start.113
  160.6 6.1 copy-start.106
  160.6 6.2 copy-start.105
  160.6 75.1 %all-gather.5.cloned.1.call-start = ((), (), s32[]{:S(2)}) async-start(), calls=%async_computation.3 | async-start | bytes 3932160 | tf_op jit(solution)/shard_map/all_gather | solution.py:486
  165.3 156.3 %copy-start.87 = (bf16[512,768]{1,0:T(8,128)(2,1)}, bf16[512,768]{1,0:T(8,128)(2,1)S(1)}, u32[]{:S(2)}) copy-start(bf16[512,768]{1,0:T(8,128)(2,1)S(1)} %get-tuple-element.61) | copy-start | bytes 2359300
  165.3 280.5 %reduce-scatter.3.cloned.1.call-start = ((), (), s32[]{:S(2)}) async-start(), calls=%async_computation.4 | async-start | bytes 7864320 | tf_op jit(solution)/shard_map/reduce_scatter | solution.py:557
  167.2 262.5 %copy-start.133 = (f32[512]{0:T(512)}, f32[512]{0:T(512)S(1)}, u32[]{:S(2)}) copy-start(f32[512]{0:T(512)S(1)} %get-tuple-element.150) | copy-start | bytes 6148
  260.0 6.0 slice-start.6
  260.0 6.0 slice-start.7
  263.3 21.4 %copy-start.142 = (bf16[512,768]{0,1:T(8,128)(2,1)}, bf16[512,768]{0,1:T(8,128)(2,1)S(1)}, u32[]{:S(2)}) copy-start(bf16[512,768]{0,1:T(8,128)(2,1)S(1)} %fusion.117) | copy-start | bytes 2359300
  264.7 20.0 %slice-start = ((s8[9437184]{0:T(1024)(128)(4,1)}), s8[4194304]{0:T(1024)(128)(4,1)S(1)}, s32[]{:S(2)}) async-start(s8[9437184]{0:T(1024)(128)(4,1)} %bitcast.95), calls=%async_computation.6 | async-start | bytes 8388608
  265.7 19.1 %copy-start.89 = (f32[512,768]{1,0:T(8,128)}, f32[512,768]{1,0:T(8,128)S(1)}, u32[]{:S(2)}) copy-start(f32[512,768]{1,0:T(8,128)S(1)} %get-tuple-element.119) | copy-start | bytes 4718596
  266.0 18.7 %slice-start.1 = ((s8[9437184]{0:T(1024)(128)(4,1)}), s8[4194304]{0:T(1024)(128)(4,1)S(1)}, s32[]{:S(2)}) async-start(s8[9437184]{0:T(1024)(128)(4,1)} %bitcast.95), calls=%async_computation.7 | async-start | bytes 8388608
  266.0 18.7 %slice-start.2 = ((s8[9437184]{0:T(1024)(128)(4,1)}), s8[1048576]{0:T(1024)(128)(4,1)S(1)}, s32[]{:S(2)}) async-start(s8[9437184]{0:T(1024)(128)(4,1)} %bitcast.95), calls=%async_computation.8 | async-start | bytes 2097152
  266.0 18.7 %copy-start.94 = (bf16[512,768]{1,0:T(8,128)(2,1)S(1)}, bf16[512,768]{1,0:T(8,128)(2,1)}, u32[]{:S(2)}) copy-start(bf16[512,768]{1,0:T(8,128)(2,1)} %param.31) | copy-start | bytes 2359300
  293.8 6.8 %copy-start.90 = (f32[512,768]{1,0:T(8,128)S(1)}, f32[512,768]{1,0:T(8,128)}, u32[]{:S(2)}) copy-start(f32[512,768]{1,0:T(8,128)} %copy-done.89) | copy-start | bytes 4718596
  304.6 18.4 %copy-start.78 = (bf16[512,768]{1,0:T(8,128)(2,1)}, bf16[512,768]{1,0:T(8,128)(2,1)S(1)}, u32[]{:S(2)}) copy-start(bf16[512,768]{1,0:T(8,128)(2,1)S(1)} %convolution_convert_fusion.4) | copy-start | bytes 2359300
  325.4 5.1 copy-start.62
  331.6 5.3 copy-start.64
  338.0 5.4 copy-start.66
  344.5 5.3 copy-start.68
  350.8 5.2 copy-start.70
  357.1 5.3 copy-start.72
  367.1 119.5 %reduce-scatter.5.cloned.1.call-start = ((), (), s32[]{:S(2)}) async-start(), calls=%async_computation.5 | async-start | bytes 7864320 | tf_op jit(solution)/shard_map/reduce_scatter | solution.py:558
  367.6 5.6 copy-start.18
  400.9 6.8 %copy-start.57 = (bf16[512,2048]{1,0:T(8,128)(2,1)S(1)}, bf16[512,2048]{1,0:T(8,128)(2,1)}, u32[]{:S(2)}) copy-start(bf16[512,2048]{1,0:T(8,128)(2,1)} %copy-done.56) | copy-start | bytes 6291460
  400.9 9.5 %copy-start.59 = (bf16[512,2048]{1,0:T(8,128)(2,1)S(1)}, bf16[512,2048]{1,0:T(8,128)(2,1)}, u32[]{:S(2)}) copy-start(bf16[512,2048]{1,0:T(8,128)(2,1)} %copy-done.58) | copy-start | bytes 6291460
  400.9 9.5 %copy-start.86 = (bf16[2048,768]{1,0:T(8,128)(2,1)S(1)}, bf16[2048,768]{1,0:T(8,128)(2,1)}, u32[]{:S(2)}) copy-start(bf16[2048,768]{1,0:T(8,128)(2,1)} %all-gather.3.cloned.1.call-done) | copy-start | bytes 9437188
  404.4 7.6 %copy-start.61 = (bf16[512,2048]{1,0:T(8,128)(2,1)S(1)}, bf16[512,2048]{1,0:T(8,128)(2,1)}, u32[]{:S(2)}) copy-start(bf16[512,2048]{1,0:T(8,128)(2,1)} %copy-done.60) | copy-start | bytes 6291460
  407.8 5.6 copy-start.63
  419.3 8.6 %copy-start.98 = (bf16[512,768]{1,0:T(8,128)(2,1)S(1)}, bf16[512,768]{1,0:T(8,128)(2,1)}, u32[]{:S(2)}) copy-start(bf16[512,768]{1,0:T(8,128)(2,1)} %copy-done.97) | copy-start | bytes 2359300
  419.3 8.6 %copy-start.143 = (bf16[512,768]{0,1:T(8,128)(2,1)S(1)}, bf16[512,768]{0,1:T(8,128)(2,1)}, u32[]{:S(2)}) copy-start(bf16[512,768]{0,1:T(8,128)(2,1)} %copy-done.142) | copy-start | bytes 2359300
  422.3 7.4 %copy-start.95 = (bf16[512,768]{1,0:T(8,128)(2,1)S(1)}, bf16[512,768]{1,0:T(8,128)(2,1)}, u32[]{:S(2)}) copy-start(bf16[512,768]{1,0:T(8,128)(2,1)} %param.31) | copy-start | bytes 2359300
  429.7 7.5 %copy-start.91 = (f32[512,768]{1,0:T(8,128)S(1)}, f32[512,768]{1,0:T(8,128)}, u32[]{:S(2)}) copy-start(f32[512,768]{1,0:T(8,128)} %copy-done.89) | copy-start | bytes 4718596
  429.7 7.5 %copy-start.144 = (bf16[512,3072]{1,0:T(8,128)(2,1)S(1)}, bf16[512,3072]{1,0:T(8,128)(2,1)}, u32[]{:S(2)}) copy-start(bf16[512,3072]{1,0:T(8,128)(2,1)} %get-tuple-element.148) | copy-start | bytes 9437188
  429.7 12.6 %slice-start.3 = ((s8[9437184]{0:T(1024)(128)(4,1)}), s8[4194304]{0:T(1024)(128)(4,1)S(1)}, s32[]{:S(2)}) async-start(s8[9437184]{0:T(1024)(128)(4,1)} %bitcast.98), calls=%async_computation.9 | async-start | bytes 8388608
  429.8 12.6 %slice-start.4 = ((s8[9437184]{0:T(1024)(128)(4,1)}), s8[4194304]{0:T(1024)(128)(4,1)S(1)}, s32[]{:S(2)}) async-start(s8[9437184]{0:T(1024)(128)(4,1)} %bitcast.98), calls=%async_computation.10 | async-start | bytes 8388608
  437.2 5.1 slice-start.5
  437.2 5.1 copy-start.145
  445.9 43.1 %copy-start.7 = (bf16[4,2,2,2,24,2304]{5,4,3,2,1,0:T(8,128)(2,1)S(1)}, bf16[4,2,2,2,24,2304]{5,4,3,2,1,0:T(8,128)(2,1)}, u32[]{:S(2)}) copy-start(bf16[4,2,2,2,24,2304]{5,4,3,2,1,0:T(8,128)(2,1)} %copy-done.6) | copy-start | bytes 10616836
  489.0 4.9 copy-start.83
  489.0 4.9 copy-start.111
  489.0 4.9 copy-start.114
  489.0 4.9 copy-start.129
  494.0 5.1 copy-start.138
  494.0 5.2 copy-start.88
  494.0 5.5 copy-start.103
  494.0 5.5 copy-start.107
  494.0 5.5 copy-start.108
  494.0 5.5 copy-start.109
  494.1 5.5 copy-start.110
  500.9 131.6 %copy-start.77 = (f32[512,768]{1,0:T(8,128)S(1)}, f32[512,768]{1,0:T(8,128)}, u32[]{:S(2)}) copy-start(f32[512,768]{1,0:T(8,128)} %copy-done.76) | copy-start | bytes 4718596
  500.9 131.6 %copy-start.84 = (bf16[512,768]{1,0:T(8,128)(2,1)S(1)}, bf16[512,768]{1,0:T(8,128)(2,1)}, u32[]{:S(2)}) copy-start(bf16[512,768]{1,0:T(8,128)(2,1)} %param.16) | copy-start | bytes 2359300
  500.9 131.6 %copy-start.96 = (bf16[512,768]{1,0:T(8,128)(2,1)S(1)}, bf16[512,768]{1,0:T(8,128)(2,1)}, u32[]{:S(2)}) copy-start(bf16[512,768]{1,0:T(8,128)(2,1)} %param.31) | copy-start | bytes 2359300
  500.9 131.6 %copy-start.112 = (f32[768]{0:T(1024)S(1)}, f32[768]{0:T(1024)}, u32[]{:S(2)}) copy-start(f32[768]{0:T(1024)} %reshape.541) | copy-start | bytes 9220
  501.0 131.6 %copy-start.115 = (f32[512]{0:T(512)S(1)}, f32[512]{0:T(512)}, u32[]{:S(2)}) copy-start(f32[512]{0:T(512)} %copy-done.113) | copy-start | bytes 6148
  501.0 131.6 %copy-start.130 = (f32[512]{0:T(512)S(1)}, f32[512]{0:T(512)}, u32[]{:S(2)}) copy-start(f32[512]{0:T(512)} %copy-done.128) | copy-start | bytes 6148
  501.0 131.6 %copy-start.134 = (f32[512]{0:T(512)S(1)}, f32[512]{0:T(512)}, u32[]{:S(2)}) copy-start(f32[512]{0:T(512)} %copy-done.133) | copy-start | bytes 6148
  501.0 131.6 %copy-start.136 = (f32[512]{0:T(512)S(1)}, f32[512]{0:T(512)}, u32[]{:S(2)}) copy-start(f32[512]{0:T(512)} %copy-done.135) | copy-start | bytes 6148
  628.2 7.3 %copy-start.102 = (f32[1,24,2304]{2,1,0:T(8,128)S(1)}, f32[1,24,2304]{2,1,0:T(8,128)}, u32[]{:S(2)}) copy-start(f32[1,24,2304]{2,1,0:T(8,128)} %get-tuple-element.32) | copy-start | bytes 663556
  628.2 8.0 %copy-start.104 = (f32[1,24,768]{2,1,0:T(8,128)S(1)}, f32[1,24,768]{2,1,0:T(8,128)}, u32[]{:S(2)}) copy-start(f32[1,24,768]{2,1,0:T(8,128)} %get-tuple-element.33) | copy-start | bytes 221188
  632.6 5.1 copy-start.99
  (95 other events, 289.8 us)
Sparse Core Ops, SparseCore 0:
  160.8 39.1 all-gather.2
  202.1 28.5 all-gather.4
  367.3 58.3 reduce-scatter.2
  428.2 58.3 reduce-scatter.4

commit v2 on v1

v2 whole, which is shorter than its diff:
```python
import functools

import jax
import jax.numpy as jnp
from jax import lax
from jax.experimental import pallas as pl
from jax.experimental.pallas import tpu as pltpu
from jax.sharding import PartitionSpec as P

HEADS = 12
HEAD_DIM = 64
PATCH_S = 197
PATCH_L = 577
TEXT_LEN = 40
ITEMS_S = 7
ITEMS_L = 2


NORM_EPS = 1e-05
MASKED = -1000000000.0
KV_HOOKS = ((0, 3), (4, 3))
SCATTER_HOOKS = ((0, 0), (3, 0))


def layer_norm(values, gain_row, shift_row):
    row_mean = jnp.mean(values, axis=-1, keepdims=True)
    centred = values - row_mean
    variance = jnp.mean(centred * centred, axis=-1, keepdims=True)
    return centred * lax.rsqrt(variance + NORM_EPS) * gain_row + shift_row


def gelu_exact(values):
    return jax.nn.gelu(values, approximate=False)


def layout(group_type, positions, row_count):
    patch_len = jnp.where(group_type == 0, PATCH_S, PATCH_L).astype(jnp.int32)
    members = jnp.where(group_type == 0, ITEMS_S, ITEMS_L).astype(jnp.int32)
    is_patch = positions < 3 * row_count
    patch_item = positions // patch_len
    text_item = jnp.maximum(positions - 3 * row_count, 0) // TEXT_LEN
    member = jnp.where(is_patch, patch_item, text_item)
    member = jnp.where(member < members, member, -1)
    modality = jnp.where(member < 0, 2, jnp.where(is_patch, 0, 1)).astype(jnp.int32)
    return (member, modality)


def product(first_op, second_op):
    return jnp.dot(first_op, second_op, preferred_element_type=jnp.float32)


def product_lead(first_op, second_op):
    return lax.dot_general(
        first_op, second_op, (((0,), (0,)), ((), ())), preferred_element_type=jnp.float32
    )


def product_trail(first_op, second_op):
    return lax.dot_general(
        first_op, second_op, (((1,), (1,)), ((), ())), preferred_element_type=jnp.float32
    )


def halves(length):
    return ((0, length // 2), (length // 2, length // 2))


def gather_chunks(share, width, ff_share, ff):
    rows = (0, share)
    chunks = [
        [((0, None), (0, THIN_ROWS), (0, 128), 0, False)]
        + [((1, None), rows, cols, order, False) for order, cols in enumerate(halves(3 * width))],
        [((2, None), rows, cols, order, False) for order, cols in enumerate(halves(width))],
    ]
    for e in range(2):
        chunks.append([((3, e), rows, cols, o, e == 1) for o, cols in enumerate(halves(ff))])
        chunks.append(
            [((4, e), band, (0, width), o, e == 1) for o, band in enumerate(halves(ff_share))]
        )
    return chunks


def scatter_chunks(share, width, ff_share, ff):
    rows = (0, share)
    chunks = [[(2, 0, rows, cols, order) for order, cols in enumerate(halves(width))]]
    for e in range(2):
        chunks.append([(0, e, rows, cols, order) for order, cols in enumerate(halves(ff))])
        chunks.append(
            [(1, e, band, (0, width), order) for order, band in enumerate(halves(ff_share))]
        )
    chunks.append([])
    chunks.append(
        [(3, 0, rows, cols, order) for order, cols in enumerate(halves(3 * width))]
        + [(4, 0, (0, THIN_ROWS), (0, 128), 0)]
    )
    return chunks


MESH = pl.DeviceIdType.MESH
GATHER_ORDERS = (("z", "x", "y"), ("z", "y", "x"), ("y", "x", "z"))
SCATTER_ORDERS = (("y", "x"), ("x", "y"))
EVERY = slice(None)
THIN_ROWS = 16


def coords():
    items, stream = lax.axis_index("items"), lax.axis_index("stream")
    return dict(z=items // 2, x=items % 2, y=stream // 2, c=stream % 2)


def place(at):
    return (at["z"] * 2 + at["x"], at["y"] * 2 + at["c"])


def moved(at, dim, by, depth):
    return {**at, dim: lax.rem(at[dim] + by, depth if dim == "z" else 2)}


def greet(at, depth):
    peers = [moved(at, "z", k, depth) for k in range(1, depth)]
    peers += [moved(at, d, 1, depth) for d in "xyc"]
    barrier = pltpu.get_barrier_semaphore()
    for peer in peers:
        pl.semaphore_signal(barrier, inc=1, device_id=place(peer), device_id_type=MESH)
    pl.semaphore_wait(barrier, len(peers))


def guard(cond, act):
    if cond is None:
        act()
    else:
        pl.when(cond)(act)


def remote(src, dst, sems, index, device):
    return pltpu.make_async_remote_copy(
        src_ref=src,
        dst_ref=dst,
        send_sem=sems[0].at[index],
        recv_sem=sems[1].at[index],
        device_id=place(device),
        device_id_type=MESH,
    )


def pipelined(chunks, n_steps, ahead, start, wait, hooks):
    count = len(chunks)
    for j in range(min(ahead, count)):
        start(chunks[j], 0)
    for t in range(count + n_steps - 1):
        if t + ahead < count:
            start(chunks[t + ahead], 0)
        for step in range(n_steps - 1, -1, -1):
            j = t - step
            if 0 <= j < count:
                wait(chunks[j], step)
                if step < n_steps - 1:
                    start(chunks[j], step + 1)
                if (j, step) in hooks:
                    hooks[(j, step)]()


def spots_of(depth):
    return [(a, b, c, d) for a in range(depth) for b in range(2) for c in range(2) for d in range(2)]


def columns_over(share, width):
    column = lax.broadcasted_iota(jnp.int32, (1, width), 1).astype(jnp.float32)
    owner = jnp.floor((column + 0.5) * (1.0 / share))
    return owner, column - owner * share


def spread(thin, share, width):
    owner, lane = columns_over(share, width)
    picks = lax.broadcasted_iota(jnp.int32, (128, width), 0).astype(jnp.float32) == lane
    wide = jnp.dot(thin, picks.astype(jnp.bfloat16), preferred_element_type=jnp.float32)
    total = jnp.zeros((THIN_ROWS, width), jnp.float32)
    for device in range(thin.shape[0] // THIN_ROWS):
        part = wide[device * THIN_ROWS : (device + 1) * THIN_ROWS]
        total = total + jnp.where(owner == device, part, 0.0)
    return total


def dealt(rows, share, devices):
    width = rows.shape[1]
    owner, lane = columns_over(share, width)
    picks = lax.broadcasted_iota(jnp.int32, (128, width), 0).astype(jnp.float32) == lane
    tall = jnp.concatenate(
        [jnp.where(owner == device, rows, 0.0) for device in range(devices)], axis=0
    )
    return lax.dot_general(
        tall,
        picks.astype(jnp.float32),
        (((1,), (1,)), ((), ())),
        precision=lax.Precision.HIGHEST,
        preferred_element_type=jnp.float32,
    )


def gather_kernel(depth, chunks, entries, kv_hooks, *refs):
    n_in = 5
    ins, tokens = refs[:n_in], refs[n_in]
    thin_out, out_all, up_all, down_all, qkv_weight, normed, queries, vectors, kv = refs[n_in + 1 : n_in + 10]
    thin_all, qkv_all, kv_own = refs[n_in + 10 : n_in + 13]
    local_sem, *sems = refs[n_in + 13 : n_in + 16]
    kv_sems = refs[n_in + 16 : n_in + 18]
    keep_sem = refs[n_in + 18]
    outs = (thin_all, qkv_all, out_all, up_all, down_all)
    rows, width = tokens.shape
    devices = depth * 8
    share = width // devices
    at = coords()
    mine = (at["z"], at["x"], at["y"], at["c"])
    slot = at["y"] * 2 + at["c"]

    def source(entry):
        k, e = entry
        return ins[k] if e is None else ins[k].at[e]

    def target(entry):
        k, e = entry
        return outs[k] if e is None else outs[k].at[e]

    local = [
        pltpu.make_async_copy(source(entry), target(entry).at[mine], local_sem.at[j])
        for j, entry in enumerate(entries)
    ]
    for copy in local:
        copy.start()
    greet(at, depth)
    for copy in local:
        copy.wait()
    lower, upper = at["y"] == 0, at["y"] == 1
    number = {piece: j for j, piece in enumerate(piece for chunk in chunks for piece in chunk)}

    def stage(piece, step):
        entry, band, cols, order, text = piece
        dims = GATHER_ORDERS[order] + ("c",)
        dim = dims[step]
        held = tuple(EVERY if d in dims[:step] else pl.ds(at[d], 1) for d in "zxyc")
        view = target(entry).at[held + (pl.ds(*band), pl.ds(*cols))]
        sends = recvs = None
        if text and dim == "y":
            sends, recvs = lower, upper
        elif text and "y" in dims[:step]:
            sends = recvs = upper
        found = []
        for k in range(1, depth if dim == "z" else 2):
            sem = {"z": k - 1, "x": depth - 1, "y": depth, "c": depth + 1}[dim]
            found.append(remote(view, view, sems, (number[piece], sem), moved(at, dim, k, depth)))
        return found, sends, recvs

    def each(chunk, step, which, call):
        for piece in chunk:
            found = stage(piece, step)

            def act(copies=found[0]):
                for copy in copies:
                    call(copy)

            guard(found[which], act)

    beside, across = moved(at, "c", 1, depth), moved(at, "y", 1, depth)
    other = across["y"] * 2 + across["c"]
    to_across = remote(kv_own, kv.at[slot], kv_sems, 0, across)
    to_beside = remote(kv_own, kv.at[slot], kv_sems, 1, beside)
    onward = remote(kv.at[other], kv.at[other], kv_sems, 2, beside)
    keep = [
        pltpu.make_async_copy(kv_own, kv.at[slot], keep_sem.at[0]),
        pltpu.make_async_copy(thin_all, thin_out, keep_sem.at[1]),
    ]

    def project():
        spots = spots_of(depth)
        for j, spot in enumerate(spots):
            qkv_weight[j * share : (j + 1) * share, :] = qkv_all[spot]
        thin = jnp.concatenate([thin_all[spot] for spot in spots], axis=0)
        vectors[...] = spread(thin, share, width)

        @pl.loop(0, rows // 128)
        def _(j):
            block = pl.ds(pl.multiple_of(j * 128, 128), 128)
            value = tokens[block, :].astype(jnp.float32)
            centred = value - jnp.mean(value, axis=-1, keepdims=True)
            scale = lax.rsqrt(jnp.mean(centred * centred, axis=-1, keepdims=True) + NORM_EPS)
            normed[block, :] = (centred * scale * vectors[0:1, :] + vectors[1:2, :]).astype(
                jnp.bfloat16
            )

        step = width // 2
        for part in range(3):

            @pl.loop(0, 2)
            def _(j, part=part):
                cols = pl.ds(pl.multiple_of(j * step, 128), step)
                value = jnp.dot(
                    normed[...],
                    qkv_weight[:, pl.ds(pl.multiple_of(part * width + j * step, 128), step)],
                    preferred_element_type=jnp.float32,
                )
                if part == 0:
                    queries[:, cols] = (value + vectors[2:3, cols]).astype(jnp.bfloat16)
                elif part == 1:
                    kv_own[:, cols] = value.astype(jnp.bfloat16)
                else:
                    kv_own[:, pl.ds(pl.multiple_of(width + j * step, 128), step)] = (
                        value + vectors[3:4, cols]
                    ).astype(jnp.bfloat16)

        to_across.start()
        to_beside.start()
        for copy in keep:
            copy.start()

    def pass_on():
        to_across.wait_recv()
        onward.start()

    pipelined(
        chunks,
        4,
        2,
        lambda chunk, step: each(chunk, step, 1, lambda copy: copy.start()),
        lambda chunk, step: each(chunk, step, 2, lambda copy: copy.wait_recv()),
        {kv_hooks[0]: project, kv_hooks[1]: pass_on},
    )
    to_beside.wait_recv()
    onward.wait_recv()
    for copy in (to_across, to_beside, onward):
        copy.wait_send()
    for copy in keep:
        copy.wait()
    for chunk in chunks:
        for step in range(4):
            each(chunk, step, 1, lambda copy: copy.wait_send())


def gather_all(thin, w_qkv, w_out, w_up, w_down, tokens, depth):
    rows, width = tokens.shape
    share, ff_share, ff = w_qkv.shape[0], w_down.shape[1], w_up.shape[2]
    entries = [(0, None), (1, None), (2, None), (3, 0), (3, 1), (4, 0), (4, 1)]
    chunks = gather_chunks(share, width, ff_share, ff)
    n_pieces = sum(len(chunk) for chunk in chunks)
    anywhere = pl.BlockSpec(memory_space=pl.ANY)
    inside = pl.BlockSpec(memory_space=pltpu.VMEM)
    low = jnp.bfloat16
    box = (depth, 2, 2, 2)
    return pl.pallas_call(
        functools.partial(gather_kernel, depth, chunks, entries, KV_HOOKS),
        out_shape=[
            jax.ShapeDtypeStruct(box + thin.shape, low),
            jax.ShapeDtypeStruct(box + (share, width), low),
            jax.ShapeDtypeStruct((2,) + box + (share, ff), low),
            jax.ShapeDtypeStruct((2,) + box + (ff_share, width), low),
            jax.ShapeDtypeStruct((width, 3 * width), low),
            jax.ShapeDtypeStruct((rows, width), low),
            jax.ShapeDtypeStruct((rows, width), low),
            jax.ShapeDtypeStruct((THIN_ROWS, width), jnp.float32),
            jax.ShapeDtypeStruct((4, rows, 2 * width), low),
        ],
        in_specs=[anywhere] * 5 + [inside],
        out_specs=[anywhere] * 4 + [inside] * 4 + [anywhere],
        scratch_shapes=[
            pltpu.VMEM(box + thin.shape, low),
            pltpu.VMEM(box + (share, 3 * width), low),
            pltpu.VMEM((rows, 2 * width), low),
            pltpu.SemaphoreType.DMA((len(entries),)),
            pltpu.SemaphoreType.DMA((n_pieces, depth + 2)),
            pltpu.SemaphoreType.DMA((n_pieces, depth + 2)),
            pltpu.SemaphoreType.DMA((3,)),
            pltpu.SemaphoreType.DMA((3,)),
            pltpu.SemaphoreType.DMA((2,)),
        ],
        compiler_params=pltpu.CompilerParams(
            collective_id=1, has_side_effects=True, vmem_limit_bytes=40 << 20
        ),
    )(thin, w_qkv, w_out, w_up, w_down, tokens)


def scatter_kernel(depth, kinds, chunks, hook_at, n_thin, *refs):
    n = len(kinds)
    n_far = 3
    it = iter(refs)
    take = lambda count: [next(it) for _ in range(count)]
    far = take(n_far)
    factor, thin_in, dq, dkv, normed, weight, tokens, residual_grad, vectors = take(9)
    outs = take(n)
    (token_grad,) = take(1)
    acc, first, second, last = take(n), take(n), take(n), take(n)
    own_half = take(n_far)
    qkv_terms, thin_terms, kv_sum, kv_got, kv_mine, qkv_grad, flipped = take(7)
    sems = take(2)
    local_sem = next(it)
    kv_sems = take(2)
    rows, width = tokens.shape
    devices = depth * 8
    share = width // devices
    at = coords()
    z, x, y, c = (at[d] for d in "zxyc")
    ins = far + [qkv_terms, thin_terms]
    halves_in = [
        pltpu.make_async_copy(far[k].at[EVERY, EVERY, EVERY, c], own_half[k], local_sem.at[k])
        for k in range(n_far)
    ] + [
        pltpu.make_async_copy(dkv.at[EVERY, c], kv_mine, local_sem.at[n_far]),
    ]
    for copy in halves_in:
        copy.start()
    greet(at, depth)
    beside, across = moved(at, "c", 1, depth), moved(at, "y", 1, depth)
    kv_beside = remote(dkv.at[EVERY, 1 - c], kv_sum, kv_sems, 0, beside)
    kv_across = remote(kv_sum.at[1 - y], kv_got, kv_sems, 1, across)
    kv_beside.start()
    lower, upper = y == 0, y == 1
    text_device = jnp.logical_and(upper, c == 1)
    image_device = jnp.logical_or(lower, c == 0)
    beside_text = jnp.logical_and(upper, c == 0)
    beside_image = jnp.logical_or(lower, c == 1)
    number = {piece: j for j, piece in enumerate(piece for chunk in chunks for piece in chunk)}

    def copies_of(piece, step):
        k, e, band, cols, order = piece
        box = (pl.ds(*band), pl.ds(*cols))
        image, text = kinds[k] and e == 0, kinds[k] and e == 1
        dim = (("c",) + SCATTER_ORDERS[order] + ("z",))[step]
        here = acc[k].at[e]

        def make(src, dst, sem, by=1):
            return remote(src, dst, sems, (number[piece], sem), moved(at, dim, by, depth))

        sends = recvs = None
        if dim == "c":
            if image:
                sends, recvs = image_device, beside_image
            elif text:
                sends, recvs = text_device, beside_text
            src = ins[k].at[(EVERY, EVERY, EVERY, 1 - c) + box]
            return [(make(src, here.at[(EVERY, EVERY, EVERY) + box], 0), sends, recvs)]
        if dim == "z":
            found = []
            for by in range(1, depth):
                src = here.at[(lax.rem(z + by, depth), x, y) + box]
                found.append((make(src, last[k].at[(e, by - 1) + box], 2 + by, by), None, None))
            return found
        if text and dim == "y":
            sends, recvs = upper, lower
        elif text and step == 1:
            sends = recvs = upper
        if step == 1:
            spot = (EVERY, EVERY, 1 - y) if dim == "y" else (EVERY, 1 - x, EVERY)
            dst = first[k].at[(e, EVERY, EVERY) + box]
        else:
            spot = (EVERY, x, 1 - y) if dim == "y" else (EVERY, 1 - x, y)
            dst = second[k].at[(e, EVERY) + box]
        return [(make(here.at[spot + box], dst, step), sends, recvs)]

    def combine(piece, step):
        k, e, band, cols, order = piece
        box = (pl.ds(*band), pl.ds(*cols))
        image, text = kinds[k] and e == 0, kinds[k] and e == 1
        here = acc[k].at[e]

        def over(spots, value_of, keep):
            @pl.loop(0, depth)
            def _(level):
                for index, spot in enumerate(spots):
                    where = (level,) + spot + box
                    value = value_of(level, index, spot)
                    here[where] = value if keep else here[where] + value

        if step == 0:
            spots = [(0, 0), (0, 1), (1, 0), (1, 1)]

            def own(level, index, spot):
                if k < n_far:
                    return own_half[k][(level,) + spot + box]
                return ins[k][(level,) + spot + (c,) + box]

            if image:
                pl.when(lower)(lambda: over(spots, own, False))
                pl.when(beside_text)(lambda: over(spots, own, True))
            elif text:
                pl.when(text_device)(lambda: over(spots, own, True))
            else:
                over(spots, own, False)
        elif step == 1:
            dim = SCATTER_ORDERS[order][0]
            spots = [(0, y), (1, y)] if dim == "y" else [(x, 0), (x, 1)]
            got = lambda level, index, spot: first[k][(e, level, index) + box]
            if text and dim == "y":
                pl.when(lower)(lambda: over(spots, got, True))
            elif text:
                pl.when(upper)(lambda: over(spots, got, False))
            else:
                over(spots, got, False)
        elif step == 2:
            dim = SCATTER_ORDERS[order][1]
            got = lambda level, index, spot: second[k][(e, level) + box]
            if text and dim == "y":
                pl.when(lower)(lambda: over([(x, y)], got, True))
            else:
                over([(x, y)], got, False)
        else:
            total = here[(z, x, y) + box].astype(jnp.float32)
            for by in range(depth - 1):
                total = total + last[k][(e, by) + box].astype(jnp.float32)
            if kinds[k]:
                total = total * factor[0:1, e * 128 : e * 128 + 1]
            outs[k][(e,) + box] = total

    def start(chunk, step):
        for piece in chunk:
            for copy, sends, _ in copies_of(piece, step):
                guard(sends, copy.start)

    def wait(chunk, step):
        for piece in chunk:
            for copy, _, recvs in copies_of(piece, step):
                guard(recvs, copy.wait_recv)
            combine(piece, step)

    def halve():
        kv_beside.wait_recv()

        @pl.loop(0, rows // 64)
        def _(j):
            block = pl.ds(pl.multiple_of(j * 64, 64), 64)
            for level in range(2):
                kv_sum[level, block, :] = kv_sum[level, block, :] + kv_mine[level, block, :]

        kv_across.start()

    def project_back():
        kv_across.wait_recv()
        sums = [jnp.zeros((8, width), jnp.float32) for _ in range(4)]
        qkv_grad[:, :width] = dq[...]
        thin_terms[...] = thin_in[...]

        def fold(value):
            return jnp.sum(value.reshape(-1, 8, width), axis=0)

        def join(j, carry):
            block = pl.ds(pl.multiple_of(j * 64, 64), 64)
            total = (
                kv_sum[y, block, :].astype(jnp.float32) + kv_got[block, :].astype(jnp.float32)
            ).astype(jnp.bfloat16)
            qkv_grad[block, width:] = total
            return (
                carry[0] + fold(dq[block, :].astype(jnp.float32)),
                carry[1] + fold(total[:, width:].astype(jnp.float32)),
            )

        sums[2], sums[3] = lax.fori_loop(0, rows // 64, join, (sums[2], sums[3]))
        flipped[...] = normed[...].T
        step = width // 2
        spots = spots_of(depth)

        @pl.loop(0, 6)
        def _(j):
            cols = pl.ds(pl.multiple_of(j * step, 128), step)
            value = jnp.dot(
                flipped[...], qkv_grad[:, cols], preferred_element_type=jnp.float32
            ).astype(jnp.bfloat16)
            for index, spot in enumerate(spots):
                qkv_terms[spot + (EVERY, cols)] = value[index * share : (index + 1) * share]

        def back(j, carry):
            block = pl.ds(pl.multiple_of(j * 128, 128), 128)
            value = tokens[block, :].astype(jnp.float32)
            centred = value - jnp.mean(value, axis=-1, keepdims=True)
            scale = lax.rsqrt(jnp.mean(centred * centred, axis=-1, keepdims=True) + NORM_EPS)
            unit = centred * scale
            grad = product_trail(qkv_grad[block, :], weight[...])
            lifted = grad * vectors[0:1, :]
            inner = jnp.mean(lifted * unit, axis=-1, keepdims=True)
            part = scale * (lifted - jnp.mean(lifted, axis=-1, keepdims=True) - unit * inner)
            token_grad[block, :] = (residual_grad[block, :] + part).astype(jnp.bfloat16)
            return carry[0] + fold(grad * unit), carry[1] + fold(grad)

        sums[0], sums[1] = lax.fori_loop(0, rows // 128, back, (sums[0], sums[1]))
        lines = [jnp.sum(value, axis=0, keepdims=True) for value in sums]
        stacked = jnp.concatenate(lines + [jnp.zeros((4, width), jnp.float32)], axis=0)
        flat = dealt(stacked, share, devices)
        for index, spot in enumerate(spots):
            thin_terms[spot + (slice(0, 8),)] += flat[index * 8 : (index + 1) * 8]

    for copy in halves_in:
        copy.wait()
    pipelined(chunks, 4, 2, start, wait, {hook_at[0]: halve, hook_at[1]: project_back})
    for copy in (kv_beside, kv_across):
        copy.wait_send()
    for chunk in chunks:
        for step in range(4):
            for piece in chunk:
                for copy, sends, _ in copies_of(piece, step):
                    guard(sends, copy.wait_send)


def scatter_all(up, down, out, factor, thin, dq, dkv, normed, weight, tokens, residual_grad, vectors, depth):
    rows, width = tokens.shape
    far = [up, down, out]
    kinds = (True, True, False, False, False)
    share, ff_share, ff = up.shape[4], down.shape[4], up.shape[5]
    chunks = scatter_chunks(share, width, ff_share, ff)
    n_pieces = sum(len(chunk) for chunk in chunks)
    anywhere, inside = pl.BlockSpec(memory_space=pl.ANY), pl.BlockSpec(memory_space=pltpu.VMEM)
    low, box = jnp.bfloat16, (depth, 2, 2, 2)
    tails = [a.shape[4:] for a in far] + [(share, 3 * width), thin.shape[4:]]
    dtypes = [low] * 4 + [jnp.float32]
    shapes = [((2 if kind else 1,), tail, dtype) for kind, tail, dtype in zip(kinds, tails, dtypes)]
    scratch = []
    for middle in ((depth, 2, 2), (depth, 2), (depth,), (depth - 1,)):
        scratch += [pltpu.VMEM(head + middle + tail, dtype) for head, tail, dtype in shapes]
    scratch += [pltpu.VMEM((depth, 2, 2) + a.shape[4:], low) for a in far]
    scratch += [
        pltpu.VMEM(box + (share, 3 * width), low),
        pltpu.VMEM(thin.shape, jnp.float32),
        pltpu.VMEM((2, rows, 2 * width), low),
        pltpu.VMEM((rows, 2 * width), low),
        pltpu.VMEM((2, rows, 2 * width), low),
        pltpu.VMEM((rows, 3 * width), low),
        pltpu.VMEM((width, rows), low),
        pltpu.SemaphoreType.DMA((n_pieces, depth + 2)),
        pltpu.SemaphoreType.DMA((n_pieces, depth + 2)),
        pltpu.SemaphoreType.DMA((4,)),
        pltpu.SemaphoreType.DMA((2,)),
        pltpu.SemaphoreType.DMA((2,)),
    ]
    return pl.pallas_call(
        functools.partial(scatter_kernel, depth, kinds, chunks, SCATTER_HOOKS, thin.shape[4]),
        out_shape=[jax.ShapeDtypeStruct(head + tail, jnp.float32) for head, tail, _ in shapes]
        + [jax.ShapeDtypeStruct((rows, width), low)],
        in_specs=[anywhere] * 3 + [inside] * 3 + [anywhere] + [inside] * 5,
        out_specs=[inside] * 6,
        scratch_shapes=scratch,
        compiler_params=pltpu.CompilerParams(
            collective_id=2, has_side_effects=True, vmem_limit_bytes=63 << 20
        ),
    )(up, down, out, factor, thin, dq, dkv.reshape(2, 2, rows, 2 * width), normed, weight, tokens, residual_grad, vectors)


TQ, TK = 256, 128
BATCH, BATCH_BACK = 12, 12
PAIR = 2 * HEAD_DIM


def trail(first_op, second_op):
    return lax.dot_general(
        first_op, second_op, (((1,), (1,)), ((), ())), preferred_element_type=jnp.float32
    )


def span(kind, start, length, image_rows):
    patch_len = jnp.where(kind == 0, PATCH_S, PATCH_L)
    members = jnp.where(kind == 0, ITEMS_S, ITEMS_L)
    image = start < image_rows
    unit = jnp.where(image, patch_len, TEXT_LEN)
    begin = jnp.where(image, start, start - image_rows)
    return lax.div(begin, unit), lax.div(begin + length - 1, unit), members


def meets(kind, first, second, image_rows):
    low_a, high_a, members = span(kind, *first, image_rows)
    low_b, high_b, _ = span(kind, *second, image_rows)
    low = jnp.maximum(low_a, low_b)
    high = jnp.minimum(jnp.minimum(high_a, high_b), members - 1)
    return low <= high, jnp.logical_and(high_a >= members, high_b >= members)


def half_of(pair, which):
    lanes = lax.broadcasted_iota(jnp.int32, pair.shape, 1)
    return jnp.where((lanes < HEAD_DIM) == (which == 0), pair, jnp.zeros_like(pair))


def upper_of(pair, which):
    keep = pair[which * HEAD_DIM : (which + 1) * HEAD_DIM]
    parts = [keep, jnp.zeros_like(keep)]
    return jnp.concatenate(parts if which == 0 else parts[::-1], axis=0)


def attend_kernel(meta, q_ref, kv_ref, kmem_ref, qmem_ref, mixed_ref, ot_ref, lse_ref, vt, qs, top, total):
    kind, stream = meta[0], meta[1]
    rows, width = q_ref.shape
    heads = width // HEAD_DIM
    everyone = kv_ref.shape[0]
    image_rows = everyone - rows
    for pair in range(heads // 2):
        columns = slice(pair * PAIR, (pair + 1) * PAIR)
        value = (q_ref[:, columns] * jnp.bfloat16(HEAD_DIM ** (-0.5))).T
        for which in range(2):
            qs[2 * pair + which] = upper_of(value, which)

    @pl.loop(0, everyone // TK)
    def _(kt):
        keys = pl.ds(pl.multiple_of(kt * TK, TK), TK)
        vt[:, keys] = kv_ref[keys, width:].T

    for qt in range(rows // TQ):
        here = slice(qt * TQ, (qt + 1) * TQ)
        top[...] = jnp.full(top.shape, -1e30, jnp.float32)
        total[...] = jnp.zeros(total.shape, jnp.float32)
        ot_ref[:, here] = jnp.zeros((width, TQ), jnp.float32)

        @pl.loop(0, everyone // TK)
        def _(kt):
            shared, loose = meets(
                kind, (stream * rows + qt * TQ, TQ), (kt * TK, TK), image_rows
            )

            @pl.when(jnp.logical_or(shared, loose))
            def _():
                keys = pl.ds(pl.multiple_of(kt * TK, TK), TK)
                allowed = kmem_ref[keys, :] == qmem_ref[:, here]
                for base in range(0, heads, BATCH):
                    group = range(base, base + BATCH)
                    scores, parts, fades = [], [], []
                    for head in group:
                        pair = slice(head // 2 * PAIR, (head // 2 + 1) * PAIR)
                        raw = jnp.dot(
                            kv_ref[keys, pair], qs[head, :, here], preferred_element_type=jnp.float32
                        )
                        scores.append(jnp.where(allowed, raw, MASKED))
                    for head, score in zip(group, scores):
                        line = slice(head, head + 1)
                        old = top[line]
                        new = jnp.maximum(old, jnp.max(score, axis=0, keepdims=True))
                        top[line] = new
                        fade = jnp.exp(old - new)
                        part = jnp.exp(score - new)
                        total[line] = total[line] * fade + jnp.sum(part, axis=0, keepdims=True)
                        parts.append(part.astype(jnp.bfloat16))
                        fades.append(fade)
                    for head, part, fade in zip(group, parts, fades):
                        own = slice(head * HEAD_DIM, (head + 1) * HEAD_DIM)
                        ot_ref[own, here] = ot_ref[own, here] * fade + jnp.dot(
                            vt[own, keys], part, preferred_element_type=jnp.float32
                        )

        for head in range(heads):
            own = slice(head * HEAD_DIM, (head + 1) * HEAD_DIM)
            line = slice(head, head + 1)
            ot_ref[own, here] = ot_ref[own, here] / total[line]
        lse_ref[:, here] = top[...] + jnp.log(total[...])
        mixed_ref[here, :] = ot_ref[:, here].T.astype(jnp.bfloat16)


def attend(meta, queries, kv, key_member, own_member):
    rows, width = queries.shape
    heads = width // HEAD_DIM
    inside = pl.BlockSpec(memory_space=pltpu.VMEM)
    lines = -(-heads // 8) * 8
    return pl.pallas_call(
        attend_kernel,
        out_shape=(
            jax.ShapeDtypeStruct((rows, width), jnp.bfloat16),
            jax.ShapeDtypeStruct((width, rows), jnp.float32),
            jax.ShapeDtypeStruct((lines, rows), jnp.float32),
        ),
        in_specs=[pl.BlockSpec(memory_space=pltpu.SMEM)] + [inside] * 4,
        out_specs=(inside,) * 3,
        scratch_shapes=[
            pltpu.VMEM((width, kv.shape[0]), jnp.bfloat16),
            pltpu.VMEM((heads, PAIR, rows), jnp.bfloat16),
            pltpu.VMEM((lines, TQ), jnp.float32),
            pltpu.VMEM((lines, TQ), jnp.float32),
        ],
        compiler_params=pltpu.CompilerParams(vmem_limit_bytes=56 << 20),
    )(meta, queries, kv, key_member, own_member)


def attend_back_kernel(
    meta, q_ref, kv_ref, kmem_ref, qmem_ref, mg_ref, ot_ref, lse_ref, dq_ref, dkv_ref,
    kt_ref, qs, gs, qst, gst, dqt, delta, dk, dv,
):
    kind, stream = meta[0], meta[1]
    rows, width = q_ref.shape
    heads = width // HEAD_DIM
    everyone = kv_ref.shape[0]
    image_rows = everyone - rows
    for pair in range(heads // 2):
        columns = slice(pair * PAIR, (pair + 1) * PAIR)
        value = q_ref[:, columns] * jnp.bfloat16(HEAD_DIM ** (-0.5))
        grad = mg_ref[:, columns]
        for which in range(2):
            qs[2 * pair + which] = half_of(value, which)
            gs[2 * pair + which] = half_of(grad, which)
            qst[2 * pair + which] = upper_of(value.T, which)
            gst[2 * pair + which] = upper_of(grad.T, which)
        product = ot_ref[columns, :] * grad.astype(jnp.float32).T
        for which in range(2):
            line = 2 * pair + which
            delta[line : line + 1] = jnp.sum(
                product[which * HEAD_DIM : (which + 1) * HEAD_DIM], axis=0, keepdims=True
            )

    @pl.loop(0, everyone // TK)
    def _(kt):
        keys = pl.ds(pl.multiple_of(kt * TK, TK), TK)
        kt_ref[:, keys] = kv_ref[keys, :width].T
        dk[keys, :] = jnp.zeros((TK, width), jnp.float32)
        dv[keys, :] = jnp.zeros((TK, width), jnp.float32)

    for qt in range(rows // TQ):
        here = slice(qt * TQ, (qt + 1) * TQ)
        dqt[...] = jnp.zeros(dqt.shape, jnp.float32)

        @pl.loop(0, everyone // TK)
        def _(kt):
            shared, _ = meets(kind, (stream * rows + qt * TQ, TQ), (kt * TK, TK), image_rows)

            @pl.when(shared)
            def _():
                keys = pl.ds(pl.multiple_of(kt * TK, TK), TK)
                allowed = kmem_ref[keys, :] == qmem_ref[:, here]
                for base in range(0, heads, BATCH_BACK):
                    group = range(base, base + BATCH_BACK)
                    scores, prob_grads, probs_low, score_low = [], [], [], []
                    for head in group:
                        begin = head // 2 * PAIR
                        scores.append(
                            jnp.dot(
                                kv_ref[keys, begin : begin + PAIR],
                                qst[head, :, here],
                                preferred_element_type=jnp.float32,
                            )
                        )
                        prob_grads.append(
                            jnp.dot(
                                kv_ref[keys, width + begin : width + begin + PAIR],
                                gst[head, :, here],
                                preferred_element_type=jnp.float32,
                            )
                        )
                    for head, score, prob_grad in zip(group, scores, prob_grads):
                        line = slice(head, head + 1)
                        probs = jnp.exp(jnp.where(allowed, score - lse_ref[line, here], MASKED))
                        probs_low.append(probs.astype(jnp.bfloat16))
                        score_low.append(
                            (probs * (prob_grad - delta[line, here])).astype(jnp.bfloat16)
                        )
                    for j, head in enumerate(group):
                        own = slice(head * HEAD_DIM, (head + 1) * HEAD_DIM)
                        dqt[own, :] += jnp.dot(
                            kt_ref[own, keys], score_low[j], preferred_element_type=jnp.float32
                        )
                    for j in range(0, BATCH_BACK, 2):
                        head = base + j
                        columns = slice(head * HEAD_DIM, head * HEAD_DIM + PAIR)
                        dk[keys, columns] += jnp.dot(
                            score_low[j], qs[head, here, :], preferred_element_type=jnp.float32
                        ) + jnp.dot(
                            score_low[j + 1], qs[head + 1, here, :], preferred_element_type=jnp.float32
                        )
                        dv[keys, columns] += jnp.dot(
                            probs_low[j], gs[head, here, :], preferred_element_type=jnp.float32
                        ) + jnp.dot(
                            probs_low[j + 1], gs[head + 1, here, :], preferred_element_type=jnp.float32
                        )

        dq_ref[here, :] = (dqt[...].T * HEAD_DIM ** (-0.5)).astype(jnp.bfloat16)

    @pl.loop(0, everyone // TK)
    def _(kt):
        keys = pl.ds(pl.multiple_of(kt * TK, TK), TK)
        dkv_ref[keys, :width] = dk[keys, :].astype(jnp.bfloat16)
        dkv_ref[keys, width:] = dv[keys, :].astype(jnp.bfloat16)


def attend_back(meta, queries, kv, key_member, own_member, mixed_grad, mixed_t, log_total):
    rows, width = queries.shape
    heads = width // HEAD_DIM
    inside = pl.BlockSpec(memory_space=pltpu.VMEM)
    lines = -(-heads // 8) * 8
    everyone = kv.shape[0]
    return pl.pallas_call(
        attend_back_kernel,
        out_shape=(
            jax.ShapeDtypeStruct((rows, width), jnp.bfloat16),
            jax.ShapeDtypeStruct((everyone, 2 * width), jnp.bfloat16),
        ),
        in_specs=[pl.BlockSpec(memory_space=pltpu.SMEM)] + [inside] * 7,
        out_specs=(inside,) * 2,
        scratch_shapes=[
            pltpu.VMEM((width, everyone), jnp.bfloat16),
            pltpu.VMEM((heads, rows, PAIR), jnp.bfloat16),
            pltpu.VMEM((heads, rows, PAIR), jnp.bfloat16),
            pltpu.VMEM((heads, PAIR, rows), jnp.bfloat16),
            pltpu.VMEM((heads, PAIR, rows), jnp.bfloat16),
            pltpu.VMEM((width, TQ), jnp.float32),
            pltpu.VMEM((lines, rows), jnp.float32),
            pltpu.VMEM((everyone, width), jnp.float32),
            pltpu.VMEM((everyone, width), jnp.float32),
        ],
        compiler_params=pltpu.CompilerParams(vmem_limit_bytes=58 << 20),
    )(meta, queries, kv, key_member, own_member, mixed_grad, mixed_t, log_total)


def padded(values):
    return jnp.pad(values, ((0, 0), (0, 128 - values.shape[1])))


def body(
    near,
    tokens,
    group_kind,
    ln1_gain,
    ln1_bias,
    w_qkv,
    q_bias,
    v_bias,
    w_out,
    out_bias,
    ln2_gain,
    ln2_bias,
    w_up,
    b_up,
    w_down,
    b_down,
    cotangent,
):
    row_count, model_width = tokens.shape
    stream_size = lax.axis_size("stream")
    stream_place = lax.axis_index("stream")
    devices = lax.axis_size("items") * stream_size
    group_type = group_kind[0]
    own_positions = stream_place * row_count + jnp.arange(row_count, dtype=jnp.int32)
    own_member, own_modality = layout(group_type, own_positions, row_count)
    key_member = layout(
        group_type, jnp.arange(stream_size * row_count, dtype=jnp.int32), row_count
    )[0]
    expert_pick = jnp.where(stream_place == stream_size - 1, 1, 0).astype(jnp.int32)
    share, ff_share, ff = model_width // devices, w_down.shape[1], w_up.shape[2]
    both = ("items", "stream")
    low = jnp.bfloat16
    thin = jnp.stack([ln1_gain, ln1_bias, q_bias, v_bias, out_bias, ln2_gain, ln2_bias])
    thin = jnp.concatenate(
        [padded(thin), padded(b_up), padded(b_down), padded(group_kind.astype(low)[:, None])]
    )
    thin = jnp.pad(thin, ((0, THIN_ROWS - thin.shape[0]), (0, 0)))
    tokens_f = tokens.astype(jnp.float32)
    if near:
        depth = lax.axis_size("items") // 2
        thin_all, out_weight, up_all, down_all, qkv_weight, normed_low, queries, vectors, kv = (
            gather_all(thin, w_qkv, w_out, w_up, w_down, tokens, depth)
        )
        thin_all = thin_all.reshape(devices, THIN_ROWS, 128)
        out_weight = out_weight.reshape(model_width, model_width)
        up_all = up_all.reshape(2, model_width, ff)
        down_all = down_all.reshape(2, ff, model_width)
        kv = kv.reshape(stream_size * row_count, 2 * model_width)
    else:
        thin_all = lax.all_gather(thin, both, axis=0)
        qkv_weight = lax.all_gather(w_qkv, both, axis=0, tiled=True)
        out_weight = lax.all_gather(w_out, both, axis=0, tiled=True)
        up_all = lax.all_gather(w_up, both, axis=1, tiled=True)
        down_all = lax.all_gather(w_down, both, axis=1, tiled=True)
        vectors = (
            thin_all[:, :, :share].transpose(1, 0, 2).reshape(THIN_ROWS, -1).astype(jnp.float32)
        )
        normed_low = layer_norm(tokens_f, vectors[0], vectors[1]).astype(low)
        shifts = jnp.concatenate([vectors[2], jnp.zeros_like(vectors[2]), vectors[3]])
        projected = (product(normed_low, qkv_weight) + shifts).astype(low)
        queries = projected[:, :model_width]
        kv = lax.all_gather(projected[:, model_width:], "stream", axis=0, tiled=True)
    out_shift, gain_two, shift_two = vectors[4], vectors[5], vectors[6]
    down_shift = jnp.where(expert_pick == 0, vectors[9], vectors[10])
    up_shift_all = thin_all[:, 7:9, :ff_share].transpose(1, 0, 2).reshape(2, ff)
    kinds = vectors[11, :: stream_size * share].astype(jnp.int32)
    tally = []
    for kind in range(2):
        modality = layout(
            jnp.int32(kind), jnp.arange(stream_size * row_count, dtype=jnp.int32), row_count
        )[1]
        tally.append([jnp.sum((modality == e).astype(jnp.float32)) for e in range(2)])
    totals = jnp.stack(
        [jnp.sum(jnp.where(kinds == 0, tally[0][e], tally[1][e])) for e in range(2)]
    )
    meta = jnp.stack([group_type, stream_place.astype(jnp.int32)])
    own_row = own_member[None]
    key_column = key_member[:, None]
    mixed_low, mixed_t, log_total = attend(meta, queries, kv, key_column, own_row)
    residual = tokens_f + product(mixed_low, out_weight) + out_shift
    normed_two, pull_two = jax.vjp(layer_norm, residual, gain_two, shift_two)
    normed_two_low = normed_two.astype(low)
    up_weight = lax.dynamic_index_in_dim(up_all, expert_pick, 0, keepdims=False)
    up_shift = lax.dynamic_index_in_dim(up_shift_all, expert_pick, 0, keepdims=False)
    down_weight = lax.dynamic_index_in_dim(down_all, expert_pick, 0, keepdims=False)
    hidden_pre = product(normed_two_low, up_weight) + up_shift.astype(jnp.float32)
    hidden, pull_gelu = jax.vjp(gelu_exact, hidden_pre)
    hidden_low = hidden.astype(low)
    branch = product(hidden_low, down_weight) + down_shift
    expert_mask = (own_modality == expert_pick).astype(jnp.float32)[:, None]
    output = (residual + branch * expert_mask).astype(low)
    live_rows = (own_modality < 2).astype(jnp.float32)[:, None]
    out_grad = cotangent.astype(jnp.float32) * live_rows
    branch_grad = (out_grad * expert_mask).astype(low)
    grad_down = product_lead(hidden_low, branch_grad)
    grad_down_shift = jnp.sum(branch_grad.astype(jnp.float32), axis=0)
    hidden_grad = product_trail(branch_grad, down_weight)
    pre_grad = pull_gelu(hidden_grad)[0].astype(low)
    grad_up = product_lead(normed_two_low, pre_grad)
    grad_up_shift = jnp.sum(pre_grad.astype(jnp.float32), axis=0)
    norm_two_grad = product_trail(pre_grad, up_weight)
    residual_part, grad_gain_two, grad_shift_two = pull_two(norm_two_grad)
    residual_grad = out_grad + residual_part
    residual_low = residual_grad.astype(low)
    grad_out_weight = product_lead(mixed_low, residual_low)
    grad_out_shift = jnp.sum(residual_low.astype(jnp.float32), axis=0)
    mixed_grad = product_trail(residual_low, out_weight).astype(low)
    query_grad, kv_terms = attend_back(
        meta, queries, kv, key_column, own_row, mixed_grad, mixed_t, log_total
    )
    factor = lax.rsqrt(totals)
    pick = (jnp.arange(2, dtype=jnp.int32) == expert_pick).astype(jnp.float32) * factor

    def lanes(values):
        values = values.reshape(values.shape[0], devices, -1).transpose(1, 0, 2)
        return jnp.pad(values, ((0, 0), (0, 0), (0, 128 - values.shape[2])))

    def thin_of(rows):
        thin_terms = jnp.concatenate(
            [
                lanes(jnp.stack(rows)),
                lanes(pick[:, None] * grad_up_shift[None]),
                lanes(pick[:, None] * grad_down_shift[None]),
            ],
            axis=1,
        )
        return jnp.pad(thin_terms, ((0, 0), (0, THIN_ROWS - thin_terms.shape[1]), (0, 0)))

    late = [grad_out_shift, grad_gain_two, grad_shift_two]
    if near:
        box = (depth, 2, 2, 2)
        up_sum, down_sum, out_sum, qkv_sum, thin_sum, token_grad = scatter_all(
            grad_up.astype(low).reshape(box + (share, ff)),
            grad_down.astype(low).reshape(box + (ff_share, model_width)),
            grad_out_weight.astype(low).reshape(box + (share, model_width)),
            jnp.broadcast_to(jnp.repeat(factor, 128)[None], (8, 256)),
            thin_of([jnp.zeros_like(grad_out_shift)] * 4 + late).reshape(box + (THIN_ROWS, 128)),
            query_grad,
            kv_terms,
            normed_low,
            qkv_weight,
            tokens,
            residual_grad,
            vectors,
            depth,
        )
        out_sum, qkv_sum, thin_sum = out_sum[0], qkv_sum[0], thin_sum[0]
    else:
        scatter = functools.partial(
            lax.psum_scatter, axis_name=both, scatter_dimension=0, tiled=True
        )
        wide = functools.partial(lax.psum_scatter, axis_name=both, scatter_dimension=1, tiled=True)
        kv_grad = lax.psum_scatter(
            kv_terms.astype(jnp.float32), "stream", scatter_dimension=0, tiled=True
        )
        qkv_grad = jnp.concatenate([query_grad, kv_grad.astype(low)], axis=1)
        grad_qkv = product_lead(normed_low, qkv_grad)
        early = [
            jnp.sum(qkv_grad[:, :model_width].astype(jnp.float32), axis=0),
            jnp.sum(qkv_grad[:, 2 * model_width :].astype(jnp.float32), axis=0),
        ]
        norm_one_grad = product_trail(qkv_grad, qkv_weight)
        token_part, *grads_one = jax.vjp(layer_norm, tokens_f, vectors[0], vectors[1])[1](
            norm_one_grad
        )
        token_grad = (residual_grad + token_part).astype(low)
        up_sum = wide(pick[:, None, None] * grad_up[None])
        down_sum = wide(pick[:, None, None] * grad_down[None])
        out_sum, qkv_sum = scatter(grad_out_weight), scatter(grad_qkv)
        thin_sum = scatter(thin_of(grads_one + early + late))[0]
    small = [thin_sum[k, :share] for k in range(7)]
    return (
        output,
        token_grad,
        small[0],
        small[1],
        qkv_sum,
        small[2],
        small[3],
        out_sum,
        small[4],
        small[5],
        small[6],
        up_sum,
        thin_sum[7:9, :ff_share],
        down_sum,
        thin_sum[9:11, :share],
        totals,
    )


def solution(mesh):
    placed = (
        P(("items", "stream"), None),
        P("items"),
        P(("items", "stream")),
        P(("items", "stream")),
        P(("items", "stream"), None),
        P(("items", "stream")),
        P(("items", "stream")),
        P(("items", "stream"), None),
        P(("items", "stream")),
        P(("items", "stream")),
        P(("items", "stream")),
        P(None, ("items", "stream"), None),
        P(None, ("items", "stream")),
        P(None, ("items", "stream"), None),
        P(None, ("items", "stream")),
        P(("items", "stream"), None),
    )
    near = mesh.shape["items"] == 8 and mesh.shape["stream"] == 4
    return jax.shard_map(
        functools.partial(body, near),
        mesh=mesh,
        in_specs=placed,
        out_specs=(
            P(("items", "stream"), None),
            P(("items", "stream"), None),
            P(("items", "stream")),
            P(("items", "stream")),
            P(("items", "stream"), None),
            P(("items", "stream")),
            P(("items", "stream")),
            P(("items", "stream"), None),
            P(("items", "stream")),
            P(("items", "stream")),
            P(("items", "stream")),
            P(None, ("items", "stream"), None),
            P(None, ("items", "stream")),
            P(None, ("items", "stream"), None),
            P(None, ("items", "stream")),
            P(),
        ),
        check_vma=False,
    )
```

time: 651 us -> 495 us (0.76)
  Pallas kernels: 245 us -> 377 us
  matrix products: 187 us -> 61.3 us
  waiting for transfers between devices: 70.9 us -> 0 us
  local copies, waits for them, and re-layouts: 66.4 us -> 22.3 us
  other arithmetic: 59.1 us -> 23.3 us
  between operations: 16.3 us -> 2.15 us
    pallas_call x2 -> x4, Pallas kernels: 245 us -> 377 us  [the longest x1 184 us: scatter_all(): pl.pallas_call(functools.partial(scatter_kernel, depth, kinds, chunks, SC...]
    dot_general x28 -> x3, matrix products: 67.9 us -> 13.9 us  [product_lead(): lax.dot_general(first_op, second_op, (((0,), (0,)), ((), ())), preferred_...]
    reduce_scatter x2 -> x0, waiting for transfers between devices: 38.2 us -> none  [the longest x1 38.2 us: body(): lax.psum_scatter(value_terms, 'stream', scatter_dimension=0, tiled=True)]
    dot_general x28 -> x3, matrix products: 54.3 us -> 17.2 us  [product_trail(): lax.dot_general(first_op, second_op, (((1,), (1,)), ((), ())), preferred_...]
    dot_general x28 -> x3, matrix products: 64.5 us -> 30.2 us  [product(): return jnp.dot(first_op, second_op, preferred_element_type=jnp.float32)]
    all_gather x2 -> x0, waiting for transfers between devices: 32.6 us -> none  [the longest x1 32.6 us: body(): lax.all_gather(keys_own, 'stream', axis=0, tiled=True)]
    unnamed x318 -> x56, local copies, waits for them, and re-layouts: 41.3 us -> 15.5 us
    convert_element_type x15 -> x0, other arithmetic: 20.8 us -> none  [the longest x12 12.8 us: body(): (softmax_out * (prob_grad - centre) * score_scale).astype(jnp.bfloat16)]
  transfers between devices with their start and end apart: 4 -> 0, of which waited for: 2 -> 0; matrix products, arithmetic and copies ran while one was open for 18% -> 0% of each run, Pallas kernels for 0% -> 0%
where the time goes in v2:
time: 495 us; the launch traced here: 486 us
  Pallas kernels  377 us (76%)
  matrix products  61.3 us (12%)
  other arithmetic  23.3 us (5%)
  local copies, waits for them, and re-layouts  22.3 us (5%)
    pallas_call x1, Pallas kernels, scatter_all(): pl.pallas_call(functools.partial(scatter_kernel, depth, kinds, chunks, SC...  184 us
    pallas_call x1, Pallas kernels, gather_all(): pl.pallas_call(functools.partial(gather_kernel, depth, chunks, entries, K...  154 us
    dot_general x3, matrix products, product(): return jnp.dot(first_op, second_op, preferred_element_type=jnp.float32)  30.2 us
    pallas_call x1, Pallas kernels, attend_back(): pl.pallas_call(attend_back_kernel, out_shape=(jax.ShapeDtypeStruct((rows,...  23.6 us
    dot_general x3, matrix products, product_trail(): lax.dot_general(first_op, second_op, (((1,), (1,)), ((), ())), preferred_...  17.2 us
    pallas_call x1, Pallas kernels, attend(): pl.pallas_call(attend_kernel, out_shape=(jax.ShapeDtypeStruct((rows, widt...  16.5 us
    unnamed x56, local copies, waits for them, and re-layouts  15.5 us
    dot_general x3, matrix products, product_lead(): lax.dot_general(first_op, second_op, (((0,), (0,)), ((), ())), preferred_...  13.9 us

profile of v2, /device:TPU:0, one launch (start us, length us, event | category | flops | bytes accessed | tf_op | source)
XLA Modules:
  0.0 486.5 jit_solution(11576300523466046686)
XLA Ops:
  0.6 0.0 copy-start.3
  1.4 0.8 compare_select_fusion.3.qmem_ref
  2.2 12.0 %compare_select_fusion.kmem_ref = s32[2048,1]{1,0:T(8,128)} fusion(s32[]{:T(128)} %bitcast.11, s32[]{:T(128)} %bitcast.10, s32[]{:T(128)S(6)} %sign.97), kind=kLoop, calls=%fused_computation.32 | loop fusion | flops 45056 | bytes 8204 | tf_op jit(solution)/shard_map/jit(_where)/select_n | solution.py:43
  14.2 0.8 stack.63
  15.0 0.7 fusion.56
  15.7 0.0 copy-start.2
  15.7 1.1 copy-done.2
  16.8 1.0 copy-done.6
  17.8 1.0 copy-done.7
  18.7 0.9 copy-done.8
  19.6 0.8 copy-done.10
  20.4 153.5 %shard_map.279 = (bf16[4,2,2,2,16,128]{5,4,3,2,1,0:T(8,128)(2,1)S(1)}, bf16[4,2,2,2,24,768]{5,4,3,2,1,0:T(8,128)(2,1)S(1)}, bf16[2,4,2,2,2,24,3072]{6,5,4,3,2,1,...) custom-call(bf16[16,128]{1,0:T(8,128)(2,1)S(1)} %pad.40.refs_0_, ...), custom_call_target="tpu_custom_call" | custom-call | tf_op jit(solution)/shard_map/pallas_call | solution.py:348
  174.0 2.6 copy-done
  176.6 1.8 copy-done.1
  178.3 0.9 copy-done.4
  179.2 0.9 copy-done.5
  180.1 0.6 pad_add_fusion.meta
  180.7 16.5 %shard_map.280 = (bf16[512,768]{1,0:T(8,128)(2,1)}, f32[768,512]{1,0:T(8,128)}, f32[16,512]{1,0:T(8,128)}) custom-call(s32[2]{0:T(128)} %pad_add_fusion.meta, bf16[512,768]{1,0:T(8,128)(2,1)} %copy-done.4, bf16[2048,1536]{1,0:T(8,128)(2,1)} %bitcast.79, s32[2048,1]{1,0:T(8,128)} %compare_select_fusion.kmem_ref, s32[1,512]{1,0:T(1,128)} %compare_select_fusion.3.qmem_ref), custom_call_target="tpu_custom_call" | custom-call | tf_op jit(solution)/shard_map/pallas_call | solution.py:752
  197.2 2.0 fusion.79
  199.3 0.3 multiply_reduce_fusion.2
  199.6 0.8 copy-done.12
  200.4 0.1 reshape.361
  200.5 0.0 copy-start.16
  200.5 20.8 %multiply_convert_fusion = (bf16[512,3072]{1,0:T(8,128)(2,1)}, f32[512,3072]{1,0:T(8,128)}, f32[512,3072]{1,0:T(8,128)}) fusion(f32[3072]{0:T(1024)S(1)} %bitcast.95, bf16[2,768,3072]{2,1,0:T(8,128)(2,1)} %bitcast.109, s32[]{:T(128)S(6)} %select_n.266, f32[512,768]{1,0:T(8,128)} %copy-done.12, f32[768]{0:T(1024)S(1)} %get-tuple-element.60, ...), kind=kOutput, calls=%fused_computation.4 | convolution fusion | flops 2521694208 | bytes 22042628 | tf_op jit(solution)/shard_map/dot_general | solution.py:49
  221.4 0.1 fusion.66
  221.5 0.0 copy-done.16
  221.5 9.0 %convert_reduce_fusion = (f32[3072]{0:T(1024)S(1)}, bf16[512,3072]{1,0:T(8,128)(2,1)S(1)}) fusion(f32[512,3072]{1,0:T(8,128)} %get-tuple-element.72, bf16[2,3072,768]{2,1,0:T(8,128)(2,1)} %bitcast.107, s32[]{:T(128)S(6)} %select_n.266, bf16[512,768]{1,0:T(8,128)(2,1)S(1)} %copy-done.16, f32[512]{0:T(512)S(1)} %get-tuple-element.88, ...), kind=kOutput, calls=%fused_computation.2 | convolution fusion | flops 2444227584 | bytes 21262340 | tf_op jit(solution)/shard_map/dot_general | solution.py:59
  230.5 6.4 %multiply_reduce_fusion = (f32[768]{0:T(1024)S(1)}, f32[512]{0:T(512)S(1)}, f32[768]{0:T(1024)S(1)}, f32[512,768]{1,0:T(8,128)S(1)}) fusion(f32[512,768]{1,0:T(8,128)S(1)} %copy-done.13, f32[512]{0:T(512)S(1)} %fusion.68, f32[512]{0:T(512)S(1)} %broadcast_multiply_fusion.2, f32[768]{0:T(1024)S(1)} %get-tuple-element.61, ...), kind=kOutput, calls=%fused_computation.35 | convolution fusion | flops 2419062784 | bytes 11025412 | tf_op jit(solution)/shard_map/dot_general | solution.py:59
  237.0 0.7 fusion.77
  237.7 0.4 convert_reduce_fusion.2
  238.1 1.8 convolution_convert_fusion.3.mg_ref
  239.9 23.6 %shard_map.281 = (bf16[512,768]{1,0:T(8,128)(2,1)}, bf16[2048,1536]{1,0:T(8,128)(2,1)}) custom-call(s32[2]{0:T(128)} %pad_add_fusion.meta, bf16[512,768]{1,0:T(8,128)(2,1)} %copy-done.4, bf16[2048,1536]{1,0:T(8,128)(2,1)} %bitcast.80, s32[2048,1]{1,0:T(8,128)} %compare_select_fusion.kmem_ref, s32[1,512]{1,0:T(1,128)} %compare_select_fusion.3.qmem_ref, ...), custom_call_target="tpu_custom_call" | custom-call | tf_op jit(solution)/shard_map/pallas_call | solution.py:875
  263.5 0.1 stack.68
  263.5 0.1 stack.69
  263.6 0.1 stack.70
  263.7 0.1 maximum_bitcast_fusion
  263.8 0.1 mul.182
  263.9 0.1 slice.54
  264.0 0.6 convert_reduce_fusion.3
  264.6 0.6 convert_reduce_fusion.4
  265.2 0.6 convert_reduce_fusion.5
  265.9 0.8 convert_reduce_fusion.6
  266.7 3.2 fusion.73
  269.9 1.4 compare_select_fusion.6
  271.3 0.1 broadcast_multiply_fusion.1
  271.4 0.1 mul.186
  271.4 0.1 broadcast_multiply_fusion
  271.5 0.1 select_maximum_fusion
  271.6 0.7 pad.44
  272.3 1.8 convolution_convert_fusion.2
  274.2 7.5 %convolution_convert_fusion.1 = bf16[768,3072]{1,0:T(8,128)(2,1)} fusion(bf16[512,3072]{1,0:T(8,128)(2,1)} %copy-done.23, f32[512,768]{1,0:T(8,128)} %copy-done.12, f32[768]{0:T(1024)S(1)} %get-tuple-element.60, f32[768]{0:T(1024)S(1)} %get-tuple-element.61, f32[512]{0:T(512)S(1)} %fusion.68, f32[512]{0:T(512)S(1)} %broadcast_multiply_fusion.2), kind=kOutput, calls=%fused_computation.19 | convolution fusion | flops 2420244480 | bytes 9447424 | tf_op jit(solution)/shard_map/dot_general | solution.py:53
  281.7 4.6 convolution_convert_fusion
  286.3 0.1 broadcast_bitcast_fusion
  286.4 0.6 broadcast_in_dim.81.refs_3_
  287.0 183.8 %shard_map.282 = (f32[2,24,3072]{2,1,0:T(8,128)}, f32[2,96,768]{2,1,0:T(8,128)}, f32[1,24,768]{2,1,0:T(8,128)}, f32[1,24,2304]{2,1,0:T(8,128)}, f32[1,16,128]{2,1,0:T(8,128)}, /*index=5*/bf16[512,768]{1,0:T(8,128)(2,1)}) custom-call(bf16[4,2,2,2,24,3072]{5,4,3,2,1,0:T(8,128)(2,1)} %bitcast.86, bf16[4,2,2,2,96,768]{5,4,3,2,1,0:T(8,128)(2,1)} %bitcast.87, ...), custom_call_target="tpu_custom_call" | custom-call | tf_op jit(solution)/shard_map/pallas_call | solution.py:629
  470.8 1.5 slice_bitcast_fusion
  472.3 1.3 slice.72
  473.5 1.2 slice.73
  474.8 7.4 %add_convert_fusion.1 = bf16[512,768]{1,0:T(8,128)(2,1)} fusion(f32[512,768]{1,0:T(8,128)} %copy-done.12, bf16[512,3072]{1,0:T(8,128)(2,1)} %get-tuple-element.71, bf16[2,3072,768]{2,1,0:T(8,128)(2,1)} %bitcast.108, s32[]{:T(128)S(6)} %select_n.266, f32[512]{0:T(512)S(1)} %get-tuple-element.87, f32[768]{0:T(1024)S(1)} %get-tuple-element.59), kind=kOutput, calls=%fused_computation.41 | convolution fusion | flops 2417491968 | bytes 10228740 | tf_op jit(solution)/shard_map/dot_general | solution.py:49
  482.1 0.9 copy.50
  483.0 0.7 copy.51
  483.7 0.6 copy.52
  484.3 0.8 copy.53
  485.2 0.8 copy.54
  (48 shorter events, 0.2 us)
Async XLA Ops:
  0.6 196.6 %copy-start.3 = (bf16[512,768]{1,0:T(8,128)(2,1)S(1)}, bf16[512,768]{1,0:T(8,128)(2,1)}, u32[]{:S(2)}) copy-start(bf16[512,768]{1,0:T(8,128)(2,1)} %refs_9_.1) | copy-start | bytes 2359300
  15.7 1.1 copy-start.2
  16.8 1.0 copy-start.6
  17.8 1.0 copy-start.7
  18.7 0.9 copy-start.8
  19.6 0.8 copy-start.10
  174.0 2.6 copy-start
  176.6 1.8 copy-start.1
  178.3 0.9 copy-start.4
  179.2 0.9 copy-start.5
  180.1 83.8 %copy-start.9 = (f32[16,768]{1,0:T(8,128)}, f32[16,768]{1,0:T(8,128)S(1)}, u32[]{:S(2)}) copy-start(f32[16,768]{1,0:T(8,128)S(1)} %get-tuple-element.40.refs_11_) | copy-start | bytes 147460
  199.2 1.2 copy-start.12
  200.5 21.0 %copy-start.16 = (bf16[512,768]{1,0:T(8,128)(2,1)S(1)}, bf16[512,768]{1,0:T(8,128)(2,1)}, u32[]{:S(2)}) copy-start(bf16[512,768]{1,0:T(8,128)(2,1)} %param.31) | copy-start | bytes 2359300
  221.5 9.0 %copy-start.13 = (f32[512,768]{1,0:T(8,128)S(1)}, f32[512,768]{1,0:T(8,128)}, u32[]{:S(2)}) copy-start(f32[512,768]{1,0:T(8,128)} %copy-done.12) | copy-start | bytes 4718596
  230.5 9.4 %copy-start.23 = (bf16[512,3072]{1,0:T(8,128)(2,1)}, bf16[512,3072]{1,0:T(8,128)(2,1)S(1)}, u32[]{:S(2)}) copy-start(bf16[512,3072]{1,0:T(8,128)(2,1)S(1)} %get-tuple-element.86) | copy-start | bytes 9437188
  238.1 34.2 %copy-start.11 = (f32[512,768]{1,0:T(8,128)}, f32[512,768]{1,0:T(8,128)S(1)}, u32[]{:S(2)}) copy-start(f32[512,768]{1,0:T(8,128)S(1)} %get-tuple-element.66.refs_10_) | copy-start | bytes 4718596
  239.9 32.5 %copy-start.14 = (bf16[512,768]{1,0:T(8,128)(2,1)S(1)}, bf16[512,768]{1,0:T(8,128)(2,1)}, u32[]{:S(2)}) copy-start(bf16[512,768]{1,0:T(8,128)(2,1)} %get-tuple-element.38) | copy-start | bytes 2359300
  271.3 15.0 %copy-start.22 = (f32[2]{0:T(128)}, f32[2]{0:T(128)S(1)}, u32[]{:S(2)}) copy-start(f32[2]{0:T(128)S(1)} %get-tuple-element.120) | copy-start | bytes 28
  274.2 7.5 %copy-start.17 = (bf16[512,768]{1,0:T(8,128)(2,1)S(1)}, bf16[512,768]{1,0:T(8,128)(2,1)}, u32[]{:S(2)}) copy-start(bf16[512,768]{1,0:T(8,128)(2,1)} %param.31) | copy-start | bytes 2359300
  274.2 7.5 %copy-start.24 = (bf16[512,3072]{1,0:T(8,128)(2,1)S(1)}, bf16[512,3072]{1,0:T(8,128)(2,1)}, u32[]{:S(2)}) copy-start(bf16[512,3072]{1,0:T(8,128)(2,1)} %get-tuple-element.71) | copy-start | bytes 9437188
  474.8 7.4 %copy-start.15 = (bf16[512,768]{1,0:T(8,128)(2,1)S(1)}, bf16[512,768]{1,0:T(8,128)(2,1)}, u32[]{:S(2)}) copy-start(bf16[512,768]{1,0:T(8,128)(2,1)} %get-tuple-element.106) | copy-start | bytes 2359300
  474.8 8.3 %copy-start.20 = (f32[1,24,2304]{2,1,0:T(8,128)S(1)}, f32[1,24,2304]{2,1,0:T(8,128)}, u32[]{:S(2)}) copy-start(f32[1,24,2304]{2,1,0:T(8,128)} %get-tuple-element.52) | copy-start | bytes 663556
  474.8 8.9 %copy-start.21 = (f32[1,24,768]{2,1,0:T(8,128)S(1)}, f32[1,24,768]{2,1,0:T(8,128)}, u32[]{:S(2)}) copy-start(f32[1,24,768]{2,1,0:T(8,128)} %get-tuple-element.53) | copy-start | bytes 221188
  474.8 9.6 %copy-start.19 = (f32[2,24,3072]{2,1,0:T(8,128)S(1)}, f32[2,24,3072]{2,1,0:T(8,128)}, u32[]{:S(2)}) copy-start(f32[2,24,3072]{2,1,0:T(8,128)} %get-tuple-element.116) | copy-start | bytes 1769476
  474.8 10.4 %copy-start.18 = (f32[2,96,768]{2,1,0:T(8,128)S(1)}, f32[2,96,768]{2,1,0:T(8,128)}, u32[]{:S(2)}) copy-start(f32[2,96,768]{2,1,0:T(8,128)} %get-tuple-element.118) | copy-start | bytes 1769476

commit v3 on v2

v3 whole, which is shorter than its diff:
```python
import functools

import jax
import jax.numpy as jnp
from jax import lax
from jax.experimental import pallas as pl
from jax.experimental.pallas import tpu as pltpu
from jax.sharding import PartitionSpec as P

HEADS = 12
HEAD_DIM = 64
PATCH_S = 197
PATCH_L = 577
TEXT_LEN = 40
ITEMS_S = 7
ITEMS_L = 2


NORM_EPS = 1e-05
MASKED = -1000000000.0


def layer_norm(values, gain_row, shift_row):
    row_mean = jnp.mean(values, axis=-1, keepdims=True)
    centred = values - row_mean
    variance = jnp.mean(centred * centred, axis=-1, keepdims=True)
    return centred * lax.rsqrt(variance + NORM_EPS) * gain_row + shift_row


def gelu_exact(values):
    return jax.nn.gelu(values, approximate=False)


def layout(group_type, positions, row_count):
    patch_len = jnp.where(group_type == 0, PATCH_S, PATCH_L).astype(jnp.int32)
    members = jnp.where(group_type == 0, ITEMS_S, ITEMS_L).astype(jnp.int32)
    is_patch = positions < 3 * row_count
    patch_item = positions // patch_len
    text_item = jnp.maximum(positions - 3 * row_count, 0) // TEXT_LEN
    member = jnp.where(is_patch, patch_item, text_item)
    member = jnp.where(member < members, member, -1)
    modality = jnp.where(member < 0, 2, jnp.where(is_patch, 0, 1)).astype(jnp.int32)
    return (member, modality)


def product(first_op, second_op):
    return jnp.dot(first_op, second_op, preferred_element_type=jnp.float32)


def product_lead(first_op, second_op):
    return lax.dot_general(
        first_op, second_op, (((0,), (0,)), ((), ())), preferred_element_type=jnp.float32
    )


def product_trail(first_op, second_op):
    return lax.dot_general(
        first_op, second_op, (((1,), (1,)), ((), ())), preferred_element_type=jnp.float32
    )


def halves(length):
    return ((0, length // 2), (length // 2, length // 2))


def divided(length, unit, *shares):
    found, begin = [], 0
    for share in shares:
        found.append((begin, share * unit))
        begin += share * unit
    assert begin == length
    return found


def gather_chunks(share, width, ff_share, ff):
    rows = (0, share)
    near_cols = divided(3 * width, 128, 7, 7, 4)
    out_cols = divided(width, 128, 2, 3, 1)
    up_cols = divided(ff, 128, 6, 13, 5)
    down_rows = divided(ff_share, 16, 2, 3, 1)
    chunks = [
        [((0, None), (0, THIN_ROWS), (0, 128), 0, False)]
        + [((1, None), rows, cols, order, False) for order, cols in enumerate(near_cols)],
        [((2, None), rows, cols, order, False) for order, cols in enumerate(out_cols)],
    ]
    for e in range(2):
        chunks.append([((3, e), rows, cols, order, e == 1) for order, cols in enumerate(up_cols)])
        chunks.append(
            [((4, e), band, (0, width), order, e == 1) for order, band in enumerate(down_rows)]
        )
    return chunks


def scatter_chunks(share, width, ff_share, ff):
    rows = (0, share)
    near_cols = divided(3 * width, 128, 7, 7, 4)
    out_cols = divided(width, 128, 2, 3, 1)
    up_cols = divided(ff, 128, 6, 13, 5)
    down_rows = divided(ff_share, 16, 2, 3, 1)
    chunks = [[(2, 0, rows, cols, order) for order, cols in enumerate(out_cols)]]
    for e in range(2):
        chunks.append([(0, e, rows, cols, order) for order, cols in enumerate(up_cols)])
        chunks.append(
            [(1, e, band, (0, width), order) for order, band in enumerate(down_rows)]
        )
    chunks.append([])
    chunks.append(
        [(3, 0, rows, cols, order) for order, cols in enumerate(near_cols)]
        + [(4, 0, (0, THIN_ROWS), (0, 128), 0)]
    )
    cuts = (
        (0, up_cols[2][0]),
        (down_rows[2][0], 0),
        (0, out_cols[2][0]),
        (0, near_cols[2][0]),
        (0, 0),
    )
    return chunks, cuts


TQ, TK = 256, 128
PAIR = 2 * HEAD_DIM


def trail(first_op, second_op):
    return lax.dot_general(
        first_op, second_op, (((1,), (1,)), ((), ())), preferred_element_type=jnp.float32
    )


def span(kind, start, length, image_rows):
    patch_len, members = ((PATCH_S, ITEMS_S), (PATCH_L, ITEMS_L))[kind]
    image = start < image_rows
    low = jnp.where(image, lax.div(start, patch_len), lax.div(start - image_rows, TEXT_LEN))
    high = jnp.where(
        image,
        lax.div(start + length - 1, patch_len),
        lax.div(start + length - 1 - image_rows, TEXT_LEN),
    )
    return low, high, members


def meets(first, second, image_rows, loose):
    found = False
    for kind in range(2):
        low_a, high_a, members = span(kind, *first, image_rows)
        low_b, high_b, _ = span(kind, *second, image_rows)
        low = jnp.maximum(low_a, low_b)
        high = jnp.minimum(jnp.minimum(high_a, high_b), members - 1)
        found = jnp.logical_or(found, low <= high)
        if loose:
            both = jnp.logical_and(high_a >= members, high_b >= members)
            found = jnp.logical_or(found, both)
    return found


def member_of(kind, position, image_rows):
    patch_len = PATCH_S + kind * float(PATCH_L - PATCH_S)
    members = ITEMS_S + kind * float(ITEMS_L - ITEMS_S)
    patch = jnp.floor((position + 0.5) / patch_len)
    text = jnp.floor((position - image_rows + 0.5) * (1.0 / TEXT_LEN))
    member = jnp.where(position < image_rows, patch, text)
    return jnp.where(member < members, member, -1.0)


def same_item(kind, stream, rows, qt, kt, image_rows):
    keys = lax.broadcasted_iota(jnp.int32, (TK, 1), 0) + kt * TK
    own = lax.broadcasted_iota(jnp.int32, (1, TQ), 1) + (stream * rows + qt * TQ)
    key_member = member_of(kind, keys.astype(jnp.float32), image_rows)
    return key_member == member_of(kind, own.astype(jnp.float32), image_rows)


def half_of(pair, which):
    lanes = lax.broadcasted_iota(jnp.int32, pair.shape, 1)
    return jnp.where((lanes < HEAD_DIM) == (which == 0), pair, jnp.zeros_like(pair))


def upper_of(pair, which):
    keep = pair[which * HEAD_DIM : (which + 1) * HEAD_DIM]
    parts = [keep, jnp.zeros_like(keep)]
    return jnp.concatenate(parts if which == 0 else parts[::-1], axis=0)


def scale_queries(q_ref, scaled):
    for pair in range(q_ref.shape[1] // PAIR):
        columns = slice(pair * PAIR, (pair + 1) * PAIR)
        value = (q_ref[:, columns] * jnp.bfloat16(HEAD_DIM ** (-0.5))).T
        for which in range(2):
            scaled[2 * pair + which] = upper_of(value, which)


def flip_columns(kv_ref, begin, flipped):
    width = flipped.shape[0]

    @pl.loop(0, flipped.shape[1] // TK)
    def _(kt):
        keys = pl.ds(pl.multiple_of(kt * TK, TK), TK)
        flipped[:, keys] = kv_ref[keys, begin : begin + width].T


def attend_part(qt, begin, end, kind_ref, stream, kv_ref, values_t, scaled, mixed_ref, mixed_t, log_total, top, total):
    width, everyone = values_t.shape
    rows = mixed_ref.shape[0]
    heads = width // HEAD_DIM
    image_rows = everyone - rows
    here = slice(qt * TQ, (qt + 1) * TQ)
    if begin == 0:
        top[...] = jnp.full(top.shape, -1e30, jnp.float32)
        total[...] = jnp.zeros(total.shape, jnp.float32)
        mixed_t[:, here] = jnp.zeros((width, TQ), jnp.float32)

    @pl.loop(begin, end)
    def _(kt):
        needed = meets((stream * rows + qt * TQ, TQ), (kt * TK, TK), image_rows, True)

        @pl.when(needed)
        def _():
            keys = pl.ds(pl.multiple_of(kt * TK, TK), TK)
            allowed = same_item(kind_ref[0:1, 0:1], stream, rows, qt, kt, image_rows)
            scores, parts, fades = [], [], []
            for head in range(heads):
                pair = slice(head // 2 * PAIR, (head // 2 + 1) * PAIR)
                raw = jnp.dot(
                    kv_ref[keys, pair], scaled[head, :, here], preferred_element_type=jnp.float32
                )
                scores.append(jnp.where(allowed, raw, MASKED))
            for head, score in enumerate(scores):
                line = slice(head, head + 1)
                old = top[line]
                new = jnp.maximum(old, jnp.max(score, axis=0, keepdims=True))
                top[line] = new
                fade = jnp.exp(old - new)
                part = jnp.exp(score - new)
                total[line] = total[line] * fade + jnp.sum(part, axis=0, keepdims=True)
                parts.append(part.astype(jnp.bfloat16))
                fades.append(fade)
            for head in range(heads):
                own = slice(head * HEAD_DIM, (head + 1) * HEAD_DIM)
                mixed_t[own, here] = mixed_t[own, here] * fades[head] + jnp.dot(
                    values_t[own, keys], parts[head], preferred_element_type=jnp.float32
                )

    if end == everyone // TK:
        for head in range(heads):
            own = slice(head * HEAD_DIM, (head + 1) * HEAD_DIM)
            mixed_t[own, here] = mixed_t[own, here] / total[head : head + 1]
        log_total[:, here] = top[...] + jnp.log(total[...])
        mixed_ref[here, :] = mixed_t[:, here].T.astype(jnp.bfloat16)


def attend_kernel(kind, place_ref, q_ref, kv_ref, mixed_ref, mixed_t, log_total, values_t, scaled, top, total):
    scale_queries(q_ref, scaled)
    flip_columns(kv_ref, q_ref.shape[1], values_t)
    for qt in range(q_ref.shape[0] // TQ):
        attend_part(
            qt, 0, kv_ref.shape[0] // TK, kind, place_ref[0], kv_ref, values_t, scaled, mixed_ref,
            mixed_t, log_total, top, total,
        )


def attend(kind, place_at, queries, kv):
    rows, width = queries.shape
    heads = width // HEAD_DIM
    inside = pl.BlockSpec(memory_space=pltpu.VMEM)
    lines = -(-heads // 8) * 8
    return pl.pallas_call(
        attend_kernel,
        out_shape=(
            jax.ShapeDtypeStruct((rows, width), jnp.bfloat16),
            jax.ShapeDtypeStruct((width, rows), jnp.float32),
            jax.ShapeDtypeStruct((lines, rows), jnp.float32),
        ),
        in_specs=[inside, pl.BlockSpec(memory_space=pltpu.SMEM)] + [inside] * 2,
        out_specs=(inside,) * 3,
        scratch_shapes=[
            pltpu.VMEM((width, kv.shape[0]), jnp.bfloat16),
            pltpu.VMEM((heads, PAIR, rows), jnp.bfloat16),
            pltpu.VMEM((lines, TQ), jnp.float32),
            pltpu.VMEM((lines, TQ), jnp.float32),
        ],
        compiler_params=pltpu.CompilerParams(vmem_limit_bytes=56 << 20),
    )(kind, place_at, queries, kv)


def back_group(
    group, kind, stream, log_total, keys_ref, values_ref, q_ref, g_ref, mixed_t, dq_ref,
    keys_t, scaled, grads, scaled_t, grads_t, dq_t, centre, dk, dv,
):
    everyone, width = keys_ref.shape
    rows = q_ref.shape[0]
    heads = width // HEAD_DIM
    image_rows = everyone - rows
    for pair in range(heads // 2):
        columns = slice(pair * PAIR, (pair + 1) * PAIR)
        value = q_ref[:, columns] * jnp.bfloat16(HEAD_DIM ** (-0.5))
        grad = g_ref[:, columns]
        value_t, grad_t = value.T, grad.T
        product = mixed_t[columns, :] * grad_t.astype(jnp.float32)
        for which in range(2):
            head = 2 * pair + which
            scaled[head] = half_of(value, which)
            grads[head] = half_of(grad, which)
            scaled_t[head] = upper_of(value_t, which)
            grads_t[head] = upper_of(grad_t, which)
            centre[head : head + 1] = jnp.sum(
                product[which * HEAD_DIM : (which + 1) * HEAD_DIM], axis=0, keepdims=True
            )
    flip_columns(keys_ref, 0, keys_t)

    @pl.loop(0, everyone // TK)
    def _(kt):
        keys = pl.ds(pl.multiple_of(kt * TK, TK), TK)
        dk[keys, :] = jnp.zeros((TK, width), jnp.float32)
        dv[keys, :] = jnp.zeros((TK, width), jnp.float32)

    for qt in range(rows // TQ):
        here = slice(qt * TQ, (qt + 1) * TQ)
        dq_t[...] = jnp.zeros(dq_t.shape, jnp.float32)

        @pl.loop(0, everyone // TK)
        def _(kt, qt=qt, here=here):
            needed = meets((stream * rows + qt * TQ, TQ), (kt * TK, TK), image_rows, False)

            @pl.when(needed)
            def _():
                keys = pl.ds(pl.multiple_of(kt * TK, TK), TK)
                allowed = same_item(kind[0:1, 0:1], stream, rows, qt, kt, image_rows)
                scores, prob_grads, probs_low, score_low = [], [], [], []
                for head in range(heads):
                    pair = slice(head // 2 * PAIR, (head // 2 + 1) * PAIR)
                    scores.append(
                        jnp.dot(
                            keys_ref[keys, pair],
                            scaled_t[head, :, here],
                            preferred_element_type=jnp.float32,
                        )
                    )
                    prob_grads.append(
                        jnp.dot(
                            values_ref[keys, pair],
                            grads_t[head, :, here],
                            preferred_element_type=jnp.float32,
                        )
                    )
                for head in range(heads):
                    line = slice(group * heads + head, group * heads + head + 1)
                    shifted = scores[head] - log_total[line, here]
                    probs = jnp.exp(jnp.where(allowed, shifted, MASKED))
                    probs_low.append(probs.astype(jnp.bfloat16))
                    inner = prob_grads[head] - centre[head : head + 1, here]
                    score_low.append((probs * inner).astype(jnp.bfloat16))
                for head in range(heads):
                    own = slice(head * HEAD_DIM, (head + 1) * HEAD_DIM)
                    dq_t[own, :] += jnp.dot(
                        keys_t[own, keys], score_low[head], preferred_element_type=jnp.float32
                    )
                for head in range(0, heads, 2):
                    columns = slice(head * HEAD_DIM, head * HEAD_DIM + PAIR)
                    for terms, left, right in ((dk, score_low, scaled), (dv, probs_low, grads)):
                        terms[keys, columns] += jnp.dot(
                            left[head], right[head, here, :], preferred_element_type=jnp.float32
                        ) + jnp.dot(
                            left[head + 1],
                            right[head + 1, here, :],
                            preferred_element_type=jnp.float32,
                        )

        dq_ref[here, :] = (dq_t[...].T * HEAD_DIM ** (-0.5)).astype(jnp.bfloat16)


def attend_back_kernel(
    kind, place_ref, q_ref, kv_ref, g_ref, mixed_t, log_total, dq_ref, dkv_ref, *work
):
    width = q_ref.shape[1]
    back_group(
        0, kind, place_ref[0], log_total, kv_ref.at[:, pl.ds(0, width)],
        kv_ref.at[:, pl.ds(width, width)], q_ref, g_ref, mixed_t, dq_ref, *work,
    )
    dk, dv = work[-2:]

    @pl.loop(0, kv_ref.shape[0] // TK)
    def _(kt):
        keys = pl.ds(pl.multiple_of(kt * TK, TK), TK)
        dkv_ref[keys, :width] = dk[keys, :].astype(jnp.bfloat16)
        dkv_ref[keys, width:] = dv[keys, :].astype(jnp.bfloat16)


def attend_back(kind, place_at, queries, kv, mixed_grad, mixed_t, log_total):
    rows, width = queries.shape
    heads = width // HEAD_DIM
    inside = pl.BlockSpec(memory_space=pltpu.VMEM)
    lines = -(-heads // 8) * 8
    everyone = kv.shape[0]
    return pl.pallas_call(
        attend_back_kernel,
        out_shape=(
            jax.ShapeDtypeStruct((rows, width), jnp.bfloat16),
            jax.ShapeDtypeStruct((everyone, 2 * width), jnp.bfloat16),
        ),
        in_specs=[inside, pl.BlockSpec(memory_space=pltpu.SMEM)] + [inside] * 5,
        out_specs=(inside,) * 2,
        scratch_shapes=[
            pltpu.VMEM((width, everyone), jnp.bfloat16),
            pltpu.VMEM((heads, rows, PAIR), jnp.bfloat16),
            pltpu.VMEM((heads, rows, PAIR), jnp.bfloat16),
            pltpu.VMEM((heads, PAIR, rows), jnp.bfloat16),
            pltpu.VMEM((heads, PAIR, rows), jnp.bfloat16),
            pltpu.VMEM((width, TQ), jnp.float32),
            pltpu.VMEM((lines, rows), jnp.float32),
            pltpu.VMEM((everyone, width), jnp.float32),
            pltpu.VMEM((everyone, width), jnp.float32),
        ],
        compiler_params=pltpu.CompilerParams(vmem_limit_bytes=58 << 20),
    )(kind, place_at, queries, kv, mixed_grad, mixed_t, log_total)


MESH = pl.DeviceIdType.MESH
GATHER_ORDERS = (("z", "x", "y"), ("z", "y", "x"), ("y", "x", "z"))
SCATTER_ORDERS = (("y", "x", "z"), ("x", "y", "z"), ("z", "x", "y"))
EVERY = slice(None)
THIN_ROWS = 16


def coords():
    items, stream = lax.axis_index("items"), lax.axis_index("stream")
    return dict(z=items // 2, x=items % 2, y=stream // 2, c=stream % 2)


def place(at):
    return (at["z"] * 2 + at["x"], at["y"] * 2 + at["c"])


def moved(at, dim, by, depth):
    return {**at, dim: lax.rem(at[dim] + by, depth if dim == "z" else 2)}


def greet(at, depth):
    peers = [moved(at, "z", k, depth) for k in range(1, depth)]
    peers += [moved(at, d, 1, depth) for d in "xyc"]
    barrier = pltpu.get_barrier_semaphore()
    for peer in peers:
        pl.semaphore_signal(barrier, inc=1, device_id=place(peer), device_id_type=MESH)
    pl.semaphore_wait(barrier, len(peers))


def guard(cond, act):
    if cond is None:
        act()
    else:
        pl.when(cond)(act)


def remote(src, dst, sems, index, device):
    return pltpu.make_async_remote_copy(
        src_ref=src,
        dst_ref=dst,
        send_sem=sems[0].at[index],
        recv_sem=sems[1].at[index],
        device_id=place(device),
        device_id_type=MESH,
    )


def pipelined(chunks, n_steps, ahead, start, wait, hooks, before):
    count = len(chunks)
    for j in range(min(ahead, count)):
        start(chunks[j], 0)
    for t in range(count + n_steps - 1):
        if t in before:
            before[t]()
        if t + ahead < count:
            start(chunks[t + ahead], 0)
        for step in range(n_steps):
            j = t - step
            if 0 <= j < count:
                wait(chunks[j], step)
                if step < n_steps - 1:
                    start(chunks[j], step + 1)
                if (j, step) in hooks:
                    hooks[(j, step)]()


def spots_of(depth):
    return [(a, b, c, d) for a in range(depth) for b in range(2) for c in range(2) for d in range(2)]


def columns_over(share, width):
    column = lax.broadcasted_iota(jnp.int32, (1, width), 1).astype(jnp.float32)
    owner = jnp.floor((column + 0.5) * (1.0 / share))
    return owner, column - owner * share


def spread(thin, share, width):
    owner, lane = columns_over(share, width)
    picks = lax.broadcasted_iota(jnp.int32, (128, width), 0).astype(jnp.float32) == lane
    wide = jnp.dot(thin, picks.astype(jnp.bfloat16), preferred_element_type=jnp.float32)
    total = jnp.zeros((THIN_ROWS, width), jnp.float32)
    for device in range(thin.shape[0] // THIN_ROWS):
        part = wide[device * THIN_ROWS : (device + 1) * THIN_ROWS]
        total = total + jnp.where(owner == device, part, 0.0)
    return total


def dealt(rows, share, devices):
    width = rows.shape[1]
    owner, lane = columns_over(share, width)
    picks = lax.broadcasted_iota(jnp.int32, (128, width), 0).astype(jnp.float32) == lane
    tall = jnp.concatenate(
        [jnp.where(owner == device, rows, 0.0) for device in range(devices)], axis=0
    )
    return lax.dot_general(
        tall,
        picks.astype(jnp.float32),
        (((1,), (1,)), ((), ())),
        precision=lax.Precision.HIGHEST,
        preferred_element_type=jnp.float32,
    )


def gather_kernel(depth, chunks, entries, *refs):
    it = iter(refs)
    take = lambda count: [next(it) for _ in range(count)]
    ins = take(5)
    tokens, kind = take(2)
    thin_out, out_all, up_all, down_all = take(4)
    qkv_weight, normed, queries, vectors, kv_out, mixed, mixed_t, log_total = take(8)
    thin_all, qkv_all, kv, values_t, scaled, top, total = take(7)
    local_sem = next(it)
    sems, kv_sems = take(2), take(2)
    keep_sem = next(it)
    outs = (thin_all, qkv_all, out_all, up_all, down_all)
    rows, width = tokens.shape
    devices = depth * 8
    share = width // devices
    at = coords()
    mine = (at["z"], at["x"], at["y"], at["c"])
    slot = at["y"] * 2 + at["c"]

    def source(entry):
        k, e = entry
        return ins[k] if e is None else ins[k].at[e]

    def target(entry):
        k, e = entry
        return outs[k] if e is None else outs[k].at[e]

    local = [
        pltpu.make_async_copy(source(entry), target(entry).at[mine], local_sem.at[j])
        for j, entry in enumerate(entries)
    ]
    for copy in local:
        copy.start()
    greet(at, depth)
    for copy in local:
        copy.wait()
    lower, upper = at["y"] == 0, at["y"] == 1
    number = {piece: j for j, piece in enumerate(piece for chunk in chunks for piece in chunk)}

    def stage(piece, step):
        entry, band, cols, order, text = piece
        dims = GATHER_ORDERS[order] + ("c",)
        dim = dims[step]
        held = tuple(EVERY if d in dims[:step] else pl.ds(at[d], 1) for d in "zxyc")
        view = target(entry).at[held + (pl.ds(*band), pl.ds(*cols))]
        sends = recvs = None
        if text and dim == "y":
            sends, recvs = lower, upper
        elif text and "y" in dims[:step]:
            sends = recvs = upper
        found = []
        for k in range(1, depth if dim == "z" else 2):
            sem = {"z": k - 1, "x": depth - 1, "y": depth, "c": depth + 1}[dim]
            found.append(remote(view, view, sems, (number[piece], sem), moved(at, dim, k, depth)))
        return found, sends, recvs

    def each(chunk, step, which, call):
        for piece in chunk:
            found = stage(piece, step)

            def act(copies=found[0]):
                for copy in copies:
                    call(copy)

            guard(found[which], act)

    beside, across = moved(at, "c", 1, depth), moved(at, "y", 1, depth)
    other = across["y"] * 2 + across["c"]
    own_slot = pl.ds(pl.multiple_of(slot * rows, rows), rows)
    other_slot = pl.ds(pl.multiple_of(other * rows, rows), rows)
    to_across = remote(kv.at[own_slot], kv.at[own_slot], kv_sems, 0, across)
    to_beside = remote(kv.at[own_slot], kv.at[own_slot], kv_sems, 1, beside)
    onward = remote(kv.at[other_slot], kv.at[other_slot], kv_sems, 2, beside)
    keep_thin = pltpu.make_async_copy(thin_all, thin_out, keep_sem.at[0])
    keep_kv = pltpu.make_async_copy(kv, kv_out, keep_sem.at[1])

    def project():
        spots = spots_of(depth)
        for j, spot in enumerate(spots):
            qkv_weight[j * share : (j + 1) * share, :] = qkv_all[spot]
        thin = jnp.concatenate([thin_all[spot] for spot in spots], axis=0)
        vectors[...] = spread(thin, share, width)

        @pl.loop(0, rows // 128)
        def _(j):
            block = pl.ds(pl.multiple_of(j * 128, 128), 128)
            value = tokens[block, :].astype(jnp.float32)
            centred = value - jnp.mean(value, axis=-1, keepdims=True)
            scale = lax.rsqrt(jnp.mean(centred * centred, axis=-1, keepdims=True) + NORM_EPS)
            normed[block, :] = (centred * scale * vectors[0:1, :] + vectors[1:2, :]).astype(
                jnp.bfloat16
            )

        step = width // 2
        for part in (1, 2, 0):

            @pl.loop(0, 2)
            def _(j, part=part):
                cols = pl.ds(pl.multiple_of(j * step, 128), step)
                value = jnp.dot(
                    normed[...],
                    qkv_weight[:, pl.ds(pl.multiple_of(part * width + j * step, 128), step)],
                    preferred_element_type=jnp.float32,
                )
                if part == 0:
                    queries[:, cols] = (value + vectors[2:3, cols]).astype(jnp.bfloat16)
                elif part == 1:
                    kv[own_slot, cols] = value.astype(jnp.bfloat16)
                else:
                    kv[own_slot, pl.ds(pl.multiple_of(width + j * step, 128), step)] = (
                        value + vectors[3:4, cols]
                    ).astype(jnp.bfloat16)

            if part == 2:
                to_across.start()
                to_beside.start()
                keep_thin.start()
        scale_queries(queries, scaled)

    def pass_on():
        to_across.wait_recv()
        onward.start()

    def attend_first():
        to_beside.wait_recv()
        onward.wait_recv()
        keep_kv.start()
        flip_columns(kv, width, values_t)

    parts = (kind, slot, kv, values_t, scaled, mixed, mixed_t, log_total, top, total)

    def attention(qt, begin, end):
        def act():
            if qt == 0 and begin == 0:
                attend_first()
            attend_part(qt, begin, end, *parts)

        return act

    everyone = kv.shape[0] // TK
    pipelined(
        chunks,
        4,
        2,
        lambda chunk, step: each(chunk, step, 1, lambda copy: copy.start()),
        lambda chunk, step: each(chunk, step, 2, lambda copy: copy.wait_recv()),
        {
            (0, 3): project,
            (2, 3): pass_on,
            (3, 3): attention(0, 0, everyone),
            (4, 3): attention(1, 0, everyone // 2),
        },
        {},
    )
    attention(1, everyone // 2, everyone)()
    for copy in (to_beside, to_across, onward):
        copy.wait_send()
    keep_thin.wait()
    keep_kv.wait()
    for chunk in chunks:
        for step in range(4):
            each(chunk, step, 1, lambda copy: copy.wait_send())


def gather_all(thin, w_qkv, w_out, w_up, w_down, tokens, kind, depth):
    rows, width = tokens.shape
    share, ff_share, ff = w_qkv.shape[0], w_down.shape[1], w_up.shape[2]
    entries = [(0, None), (1, None), (2, None), (3, 0), (3, 1), (4, 0), (4, 1)]
    chunks = gather_chunks(share, width, ff_share, ff)
    n_pieces = sum(len(chunk) for chunk in chunks)
    anywhere = pl.BlockSpec(memory_space=pl.ANY)
    inside = pl.BlockSpec(memory_space=pltpu.VMEM)
    low = jnp.bfloat16
    box = (depth, 2, 2, 2)
    heads, lines = width // HEAD_DIM, -(-(width // HEAD_DIM) // 8) * 8
    return pl.pallas_call(
        functools.partial(gather_kernel, depth, chunks, entries),
        out_shape=[
            jax.ShapeDtypeStruct(box + thin.shape, low),
            jax.ShapeDtypeStruct(box + (share, width), low),
            jax.ShapeDtypeStruct((2,) + box + (share, ff), low),
            jax.ShapeDtypeStruct((2,) + box + (ff_share, width), low),
            jax.ShapeDtypeStruct((width, 3 * width), low),
            jax.ShapeDtypeStruct((rows, width), low),
            jax.ShapeDtypeStruct((rows, width), low),
            jax.ShapeDtypeStruct((THIN_ROWS, width), jnp.float32),
            jax.ShapeDtypeStruct((4 * rows, 2 * width), low),
            jax.ShapeDtypeStruct((rows, width), low),
            jax.ShapeDtypeStruct((width, rows), jnp.float32),
            jax.ShapeDtypeStruct((lines, rows), jnp.float32),
        ],
        in_specs=[anywhere] * 5 + [inside] * 2,
        out_specs=[anywhere] * 4 + [inside] * 4 + [anywhere] + [inside] * 3,
        scratch_shapes=[
            pltpu.VMEM(box + thin.shape, low),
            pltpu.VMEM(box + (share, 3 * width), low),
            pltpu.VMEM((4 * rows, 2 * width), low),
            pltpu.VMEM((width, 4 * rows), low),
            pltpu.VMEM((heads, PAIR, rows), low),
            pltpu.VMEM((lines, TQ), jnp.float32),
            pltpu.VMEM((lines, TQ), jnp.float32),
            pltpu.SemaphoreType.DMA((len(entries),)),
            pltpu.SemaphoreType.DMA((n_pieces, depth + 2)),
            pltpu.SemaphoreType.DMA((n_pieces, depth + 2)),
            pltpu.SemaphoreType.DMA((3,)),
            pltpu.SemaphoreType.DMA((3,)),
            pltpu.SemaphoreType.DMA((2,)),
        ],
        compiler_params=pltpu.CompilerParams(
            collective_id=1, has_side_effects=True, vmem_limit_bytes=48 << 20
        ),
    )(thin, w_qkv, w_out, w_up, w_down, tokens, kind)


def scatter_kernel(depth, kinds, chunks, cuts, *refs):
    n, n_far = len(kinds), 3
    it = iter(refs)
    take = lambda count: [next(it) for _ in range(count)]
    far = take(n_far)
    factor, thin_in, vectors, kind, log_total = take(5)
    queries, kv, mixed_grad, mixed_t, normed, weight, tokens, residual_grad = take(8)
    outs = take(n)
    token_grad, kv_away = take(2)
    acc, first, second, last = take(n), take(n), take(n), take(n)
    z_first, z_second, z_last = take(n), take(n), take(n)
    own_half = take(n_far)
    qkv_terms, thin_terms, kv_sum, kv_got, kv_mine, dq = take(6)
    sems = take(2)
    local_sem, away_sem = take(2)
    kv_sems = take(2)
    rows, width = residual_grad.shape
    devices = depth * 8
    share = width // devices
    at = coords()
    z, x, y, c = (at[d] for d in "zxyc")
    ins = far + [qkv_terms, thin_terms]
    local = [
        pltpu.make_async_copy(far[k].at[EVERY, EVERY, EVERY, c], own_half[k], local_sem.at[k])
        for k in range(n_far)
    ]
    for copy in local:
        copy.start()
    greet(at, depth)
    for copy in local:
        copy.wait()
    beside, across = moved(at, "c", 1, depth), moved(at, "y", 1, depth)
    kv_beside = remote(kv_away, kv_sum, kv_sems, 0, beside)
    kv_across = remote(kv_sum.at[1 - y], kv_got, kv_sems, 1, across)
    lower, upper = y == 0, y == 1
    text_device = jnp.logical_and(upper, c == 1)
    image_device = jnp.logical_or(lower, c == 0)
    beside_text = jnp.logical_and(upper, c == 0)
    beside_image = jnp.logical_or(lower, c == 1)
    number = {piece: j for j, piece in enumerate(piece for chunk in chunks for piece in chunk)}

    def boxes(piece):
        k, e, band, cols, order = piece
        cut = cuts[k] if order == 2 else (0, 0)
        return (
            (pl.ds(*band), pl.ds(*cols)),
            (pl.ds(band[0] - cut[0], band[1]), pl.ds(cols[0] - cut[1], cols[1])),
        )

    def copies_of(piece, step):
        k, e, band, cols, order = piece
        box, inner = boxes(piece)
        image, text = kinds[k] and e == 0, kinds[k] and e == 1
        dims = ("c",) + SCATTER_ORDERS[order]
        dim = dims[step]
        here = acc[k].at[e]

        def make(src, dst, sem, by=1):
            return remote(src, dst, sems, (number[piece], sem), moved(at, dim, by, depth))

        sends = recvs = None
        if dim == "c":
            if image:
                sends, recvs = image_device, beside_image
            elif text:
                sends, recvs = text_device, beside_text
            src = ins[k].at[(EVERY, EVERY, EVERY, 1 - c) + box]
            return [(make(src, here.at[(EVERY, EVERY, EVERY) + box], 0), sends, recvs)]
        if text and dim == "y":
            sends, recvs = upper, lower
        elif text and "y" not in dims[:step]:
            sends = recvs = upper
        if dim == "z":
            found = []
            for by in range(1, depth):
                to = lax.rem(z + by, depth)
                if order == 2:
                    src = here.at[(to, EVERY, EVERY) + box]
                    dst = z_first[k].at[(e, by - 1, EVERY, EVERY) + inner]
                else:
                    src = here.at[(to, x, y) + box]
                    dst = last[k].at[(e, by - 1) + inner]
                found.append((make(src, dst, 2 + by, by), sends, recvs))
            return found
        if order == 2 and dim == "x":
            src, dst = here.at[(z, 1 - x, EVERY) + box], z_second[k].at[(e, EVERY) + inner]
            return [(make(src, dst, 1), sends, recvs)]
        if order == 2:
            src, dst = here.at[(z, x, 1 - y) + box], z_last[k].at[(e,) + inner]
            return [(make(src, dst, 2), sends, recvs)]
        if step == 1:
            spot = (EVERY, EVERY, 1 - y) if dim == "y" else (EVERY, 1 - x, EVERY)
            dst = first[k].at[(e, EVERY, EVERY) + inner]
        else:
            spot = (EVERY, x, 1 - y) if dim == "y" else (EVERY, 1 - x, y)
            dst = second[k].at[(e, EVERY) + inner]
        return [(make(here.at[spot + box], dst, step), sends, recvs)]

    def combine(piece, step):
        k, e, band, cols, order = piece
        box, inner = boxes(piece)
        image, text = kinds[k] and e == 0, kinds[k] and e == 1
        dims = ("c",) + SCATTER_ORDERS[order]
        dim = dims[step]
        here = acc[k].at[e]

        def over(spots, value_of, keep):
            @pl.loop(0, depth)
            def _(level):
                for index, spot in enumerate(spots):
                    where = (level,) + spot + box
                    value = value_of(level, index, spot)
                    here[where] = value if keep else here[where] + value

        def wide(value):
            return value.astype(jnp.float32)

        if step == 0:
            spots = [(0, 0), (0, 1), (1, 0), (1, 1)]

            def own(level, index, spot):
                if k < n_far:
                    return own_half[k][(level,) + spot + box]
                return ins[k][(level,) + spot + (c,) + box]

            if image:
                pl.when(lower)(lambda: over(spots, own, False))
                pl.when(beside_text)(lambda: over(spots, own, True))
            elif text:
                pl.when(text_device)(lambda: over(spots, own, True))
            else:
                over(spots, own, False)
        elif step == 3:

            def finish(total):
                if kinds[k]:
                    total = total * factor[0:1, e * 128 : e * 128 + 1]
                outs[k][(e,) + box] = total

            def own():
                return wide(here[(z, x, y) + box])

            if order == 2:
                got = lambda: wide(z_last[k][(e,) + inner])
                if text:
                    pl.when(lower)(lambda: finish(got()))
                    pl.when(upper)(lambda: finish(own()))
                else:
                    finish(own() + got())
            else:
                total = own()
                for by in range(depth - 1):
                    total = total + wide(last[k][(e, by) + inner])
                finish(total)
        elif order == 2:

            def act():
                if step == 1:
                    for spot in [(0, 0), (0, 1), (1, 0), (1, 1)]:
                        where = (z,) + spot + box
                        total = wide(here[where])
                        for by in range(depth - 1):
                            total = total + wide(z_first[k][(e, by) + spot + inner])
                        here[where] = total.astype(here.dtype)
                else:
                    for other in range(2):
                        where = (z, x, other) + box
                        here[where] = here[where] + z_second[k][(e, other) + inner]

            guard(upper if text else None, act)
        elif step == 1:
            spots = [(0, y), (1, y)] if dim == "y" else [(x, 0), (x, 1)]
            got = lambda level, index, spot: first[k][(e, level, index) + inner]
            if text and dim == "y":
                pl.when(lower)(lambda: over(spots, got, True))
            elif text:
                pl.when(upper)(lambda: over(spots, got, False))
            else:
                over(spots, got, False)
        else:
            got = lambda level, index, spot: second[k][(e, level) + inner]
            if text and dim == "y":
                pl.when(lower)(lambda: over([(x, y)], got, True))
            else:
                over([(x, y)], got, False)

    def start(chunk, step):
        for piece in chunk:
            for copy, sends, _ in copies_of(piece, step):
                guard(sends, copy.start)

    def wait(chunk, step):
        for piece in chunk:
            for copy, _, recvs in copies_of(piece, step):
                guard(recvs, copy.wait_recv)
            combine(piece, step)

    def halve():
        kv_beside.wait_recv()

        @pl.loop(0, rows // 64)
        def _(j):
            block = pl.ds(pl.multiple_of(j * 64, 64), 64)
            for level in range(2):
                kv_sum[level, block, :] = kv_sum[level, block, :] + kv_mine[level, block, :]

        kv_across.start()

    def project_back(qkv_grad, flipped, normed_in, weight_in, tokens_in, residual_in, token_out):
        pairs = [(normed, normed_in), (weight, weight_in), (tokens, tokens_in), (residual_grad, residual_in)]
        loads = [pltpu.make_async_copy(src, dst, away_sem.at[j]) for j, (src, dst) in enumerate(pairs)]
        for copy in loads:
            copy.start()
        for copy in loads:
            copy.wait()
        flipped[...] = normed_in[...].T
        qkv_grad[:, :width] = dq[...]
        thin_terms[...] = thin_in[...]
        kv_across.wait_recv()

        def fold(value):
            return jnp.sum(value.reshape(-1, 8, width), axis=0)

        zero = jnp.zeros((8, width), jnp.float32)

        def join(j, carry):
            block = pl.ds(pl.multiple_of(j * 64, 64), 64)
            total = (
                kv_sum[y, block, :].astype(jnp.float32) + kv_got[block, :].astype(jnp.float32)
            ).astype(jnp.bfloat16)
            qkv_grad[block, width:] = total
            return (
                carry[0] + fold(dq[block, :].astype(jnp.float32)),
                carry[1] + fold(total[:, width:].astype(jnp.float32)),
            )

        sum_q, sum_v = lax.fori_loop(0, rows // 64, join, (zero, zero))
        step = width // 2
        spots = spots_of(depth)

        @pl.loop(0, 6)
        def _(j):
            cols = pl.ds(pl.multiple_of(j * step, 128), step)
            value = jnp.dot(
                flipped[...], qkv_grad[:, cols], preferred_element_type=jnp.float32
            ).astype(jnp.bfloat16)
            for index, spot in enumerate(spots):
                qkv_terms[spot + (EVERY, cols)] = value[index * share : (index + 1) * share]

        def back(j, carry):
            block = pl.ds(pl.multiple_of(j * 128, 128), 128)
            value = tokens_in[block, :].astype(jnp.float32)
            centred = value - jnp.mean(value, axis=-1, keepdims=True)
            scale = lax.rsqrt(jnp.mean(centred * centred, axis=-1, keepdims=True) + NORM_EPS)
            unit = centred * scale
            grad = product_trail(qkv_grad[block, :], weight_in[...])
            lifted = grad * vectors[0:1, :]
            inner = jnp.mean(lifted * unit, axis=-1, keepdims=True)
            part = scale * (lifted - jnp.mean(lifted, axis=-1, keepdims=True) - unit * inner)
            token_out[block, :] = (residual_in[block, :] + part).astype(jnp.bfloat16)
            return carry[0] + fold(grad * unit), carry[1] + fold(grad)

        sum_gain, sum_shift = lax.fori_loop(0, rows // 128, back, (zero, zero))
        store = pltpu.make_async_copy(token_out, token_grad, away_sem.at[0])
        store.start()
        lines = [jnp.sum(value, axis=0, keepdims=True) for value in (sum_gain, sum_shift, sum_q, sum_v)]
        stacked = jnp.concatenate(lines + [jnp.zeros((4, width), jnp.float32)], axis=0)
        flat = dealt(stacked, share, devices)
        for index, spot in enumerate(spots):
            thin_terms[spot + (slice(0, 8),)] += flat[index * 8 : (index + 1) * 8]
        store.wait()

    def project_scope():
        low = jnp.bfloat16
        pl.run_scoped(
            project_back,
            pltpu.VMEM((rows, 3 * width), low),
            pltpu.VMEM((width, rows), low),
            pltpu.VMEM((rows, width), low),
            pltpu.VMEM((width, 3 * width), low),
            pltpu.VMEM((rows, width), low),
            pltpu.VMEM((rows, width), jnp.float32),
            pltpu.VMEM((rows, width), low),
        )

    group_width = width // 2
    stream = y * 2 + c

    def attention(group):
        cols = pl.ds(group * group_width, group_width)
        value_cols = pl.ds(width + group * group_width, group_width)

        def act(keys, values, q_in, g_in, mixed_in, *work):
            pairs = [
                (kv.at[:, cols], keys),
                (kv.at[:, value_cols], values),
                (queries.at[:, cols], q_in),
                (mixed_grad.at[:, cols], g_in),
                (mixed_t.at[cols, :], mixed_in),
            ]
            loads = [pltpu.make_async_copy(src, dst, away_sem.at[j]) for j, (src, dst) in enumerate(pairs)]
            for copy in loads:
                copy.start()
            for copy in loads:
                copy.wait()
            back_group(
                group, kind, stream, log_total, keys, values, q_in, g_in, mixed_in,
                dq.at[:, cols], *work,
            )
            dk, dv = work[-2:]
            for part, (terms, rest, begin) in enumerate(((dk, keys, cols), (dv, values, value_cols))):
                for level in range(2):
                    mine = (level * 2 + c) * rows
                    away = (level * 2 + 1 - c) * rows

                    @pl.loop(0, rows // 128)
                    def _(j, level=level, mine=mine, away=away, terms=terms, rest=rest, begin=begin):
                        to = pl.ds(pl.multiple_of(j * 128, 128), 128)
                        kept = pl.ds(pl.multiple_of(mine + j * 128, 128), 128)
                        sent = pl.ds(pl.multiple_of(away + j * 128, 128), 128)
                        kv_mine[level, to, begin] = terms[kept, :].astype(jnp.bfloat16)
                        rest[sent, :] = terms[sent, :].astype(jnp.bfloat16)

            stores = []
            for part, (rest, begin) in enumerate(((keys, cols), (values, value_cols))):
                for level in range(2):
                    sent = pl.ds(pl.multiple_of((level * 2 + 1 - c) * rows, rows), rows)
                    stores.append(
                        pltpu.make_async_copy(
                            rest.at[sent], kv_away.at[level, :, begin], away_sem.at[part * 2 + level]
                        )
                    )
            for copy in stores:
                copy.start()
            for copy in stores:
                copy.wait()
            if group == 1:
                kv_beside.start()

        def scope():
            low = jnp.bfloat16
            heads = group_width // HEAD_DIM
            everyone = 4 * rows
            pl.run_scoped(
                act,
                pltpu.VMEM((everyone, group_width), low),
                pltpu.VMEM((everyone, group_width), low),
                pltpu.VMEM((rows, group_width), low),
                pltpu.VMEM((rows, group_width), low),
                pltpu.VMEM((group_width, rows), jnp.float32),
                pltpu.VMEM((group_width, everyone), low),
                pltpu.VMEM((heads, rows, PAIR), low),
                pltpu.VMEM((heads, rows, PAIR), low),
                pltpu.VMEM((heads, PAIR, rows), low),
                pltpu.VMEM((heads, PAIR, rows), low),
                pltpu.VMEM((group_width, TQ), jnp.float32),
                pltpu.VMEM((8, rows), jnp.float32),
                pltpu.VMEM((everyone, group_width), jnp.float32),
                pltpu.VMEM((everyone, group_width), jnp.float32),
            )

        return scope

    before = {0: attention(0), 1: attention(1), 3: halve, 4: project_scope}
    pipelined(chunks, 4, 2, start, wait, {}, before)
    for copy in (kv_beside, kv_across):
        copy.wait_send()
    for chunk in chunks:
        for step in range(4):
            for piece in chunk:
                for copy, sends, _ in copies_of(piece, step):
                    guard(sends, copy.wait_send)


def scatter_all(
    up, down, out, factor, thin, vectors, kind, log_total,
    queries, kv, mixed_grad, mixed_t, normed, weight, tokens, residual_grad, depth,
):
    rows, width = tokens.shape
    far = [up, down, out]
    kinds = (True, True, False, False, False)
    share, ff_share, ff = up.shape[4], down.shape[4], up.shape[5]
    chunks, cuts = scatter_chunks(share, width, ff_share, ff)
    n_pieces = sum(len(chunk) for chunk in chunks)
    anywhere, inside = pl.BlockSpec(memory_space=pl.ANY), pl.BlockSpec(memory_space=pltpu.VMEM)
    low, box = jnp.bfloat16, (depth, 2, 2, 2)
    tails = [a.shape[4:] for a in far] + [(share, 3 * width), thin.shape[4:]]
    dtypes = [low] * 4 + [jnp.float32]
    experts = [2 if kind else 1 for kind in kinds]
    scratch = [
        pltpu.VMEM((e, depth, 2, 2) + tail, dtype) for e, tail, dtype in zip(experts, tails, dtypes)
    ]
    plain, turned = [], []
    for tail, cut in zip(tails, cuts):
        plain.append((cut[0] or tail[0], cut[1] or tail[1]))
        turned.append((tail[0] - cut[0], tail[1] - cut[1]) if any(cut) else (8, 128))
    for middle in ((depth, 2), (depth,), (depth - 1,)):
        scratch += [pltpu.VMEM((e,) + middle + t, d) for e, t, d in zip(experts, plain, dtypes)]
    for middle in ((depth - 1, 2, 2), (2,), ()):
        scratch += [pltpu.VMEM((e,) + middle + t, d) for e, t, d in zip(experts, turned, dtypes)]
    scratch += [pltpu.VMEM((depth, 2, 2) + a.shape[4:], low) for a in far]
    scratch += [
        pltpu.VMEM(box + (share, 3 * width), low),
        pltpu.VMEM(thin.shape, jnp.float32),
        pltpu.VMEM((2, rows, 2 * width), low),
        pltpu.VMEM((rows, 2 * width), low),
        pltpu.VMEM((2, rows, 2 * width), low),
        pltpu.VMEM((rows, width), low),
        pltpu.SemaphoreType.DMA((n_pieces, depth + 2)),
        pltpu.SemaphoreType.DMA((n_pieces, depth + 2)),
        pltpu.SemaphoreType.DMA((3,)),
        pltpu.SemaphoreType.DMA((5,)),
        pltpu.SemaphoreType.DMA((2,)),
        pltpu.SemaphoreType.DMA((2,)),
    ]
    return pl.pallas_call(
        functools.partial(scatter_kernel, depth, kinds, chunks, cuts),
        out_shape=[
            jax.ShapeDtypeStruct((e,) + tail, jnp.float32) for e, tail in zip(experts, tails)
        ]
        + [jax.ShapeDtypeStruct((rows, width), low), jax.ShapeDtypeStruct((2, rows, 2 * width), low)],
        in_specs=[anywhere] * 3 + [inside] * 5 + [anywhere] * 8,
        out_specs=[inside] * 5 + [anywhere] * 2,
        scratch_shapes=scratch,
        compiler_params=pltpu.CompilerParams(
            collective_id=2, has_side_effects=True, vmem_limit_bytes=61 << 20
        ),
    )(
        up, down, out, factor, thin, vectors, kind, log_total,
        queries, kv, mixed_grad, mixed_t, normed, weight, tokens, residual_grad,
    )[:6]


def padded(values):
    return jnp.pad(values, ((0, 0), (0, 128 - values.shape[1])))


def body(
    near,
    tokens,
    group_kind,
    ln1_gain,
    ln1_bias,
    w_qkv,
    q_bias,
    v_bias,
    w_out,
    out_bias,
    ln2_gain,
    ln2_bias,
    w_up,
    b_up,
    w_down,
    b_down,
    cotangent,
):
    row_count, model_width = tokens.shape
    stream_size = lax.axis_size("stream")
    stream_place = lax.axis_index("stream")
    devices = lax.axis_size("items") * stream_size
    group_type = group_kind[0]
    own_positions = stream_place * row_count + jnp.arange(row_count, dtype=jnp.int32)
    own_modality = layout(group_type, own_positions, row_count)[1]
    expert_pick = jnp.where(stream_place == stream_size - 1, 1, 0).astype(jnp.int32)
    share, ff_share, ff = model_width // devices, w_down.shape[1], w_up.shape[2]
    both = ("items", "stream")
    low = jnp.bfloat16
    thin = jnp.stack([ln1_gain, ln1_bias, q_bias, v_bias, out_bias, ln2_gain, ln2_bias])
    thin = jnp.concatenate(
        [padded(thin), padded(b_up), padded(b_down), padded(group_kind.astype(low)[:, None])]
    )
    thin = jnp.pad(thin, ((0, THIN_ROWS - thin.shape[0]), (0, 0)))
    tokens_f = tokens.astype(jnp.float32)
    kind_wide = jnp.broadcast_to(group_type.astype(jnp.float32), (8, 128))
    place_at = stream_place.astype(jnp.int32)[None]
    if near:
        depth = lax.axis_size("items") // 2
        (
            thin_all,
            out_weight,
            up_all,
            down_all,
            qkv_weight,
            normed_low,
            queries,
            vectors,
            kv,
            mixed_low,
            mixed_t,
            log_total,
        ) = gather_all(thin, w_qkv, w_out, w_up, w_down, tokens, kind_wide, depth)
        thin_all = thin_all.reshape(devices, THIN_ROWS, 128)
        out_weight = out_weight.reshape(model_width, model_width)
        up_all = up_all.reshape(2, model_width, ff)
        down_all = down_all.reshape(2, ff, model_width)
    else:
        thin_all = lax.all_gather(thin, both, axis=0)
        qkv_weight = lax.all_gather(w_qkv, both, axis=0, tiled=True)
        out_weight = lax.all_gather(w_out, both, axis=0, tiled=True)
        up_all = lax.all_gather(w_up, both, axis=1, tiled=True)
        down_all = lax.all_gather(w_down, both, axis=1, tiled=True)
        vectors = (
            thin_all[:, :, :share].transpose(1, 0, 2).reshape(THIN_ROWS, -1).astype(jnp.float32)
        )
        normed_low = layer_norm(tokens_f, vectors[0], vectors[1]).astype(low)
        shifts = jnp.concatenate([vectors[2], jnp.zeros_like(vectors[2]), vectors[3]])
        projected = (product(normed_low, qkv_weight) + shifts).astype(low)
        queries = projected[:, :model_width]
        kv = lax.all_gather(projected[:, model_width:], "stream", axis=0, tiled=True)
        mixed_low, mixed_t, log_total = attend(kind_wide, place_at, queries, kv)
    out_shift, gain_two, shift_two = vectors[4], vectors[5], vectors[6]
    down_shift = jnp.where(expert_pick == 0, vectors[9], vectors[10])
    up_shift_all = thin_all[:, 7:9, :ff_share].transpose(1, 0, 2).reshape(2, ff)
    kinds = vectors[11, :: stream_size * share].astype(jnp.int32)
    tally = []
    for kind in range(2):
        modality = layout(
            jnp.int32(kind), jnp.arange(stream_size * row_count, dtype=jnp.int32), row_count
        )[1]
        tally.append([jnp.sum((modality == e).astype(jnp.float32)) for e in range(2)])
    totals = jnp.stack(
        [jnp.sum(jnp.where(kinds == 0, tally[0][e], tally[1][e])) for e in range(2)]
    )
    residual = tokens_f + product(mixed_low, out_weight) + out_shift
    normed_two, pull_two = jax.vjp(layer_norm, residual, gain_two, shift_two)
    normed_two_low = normed_two.astype(low)
    up_weight = lax.dynamic_index_in_dim(up_all, expert_pick, 0, keepdims=False)
    up_shift = lax.dynamic_index_in_dim(up_shift_all, expert_pick, 0, keepdims=False)
    down_weight = lax.dynamic_index_in_dim(down_all, expert_pick, 0, keepdims=False)
    hidden_pre = product(normed_two_low, up_weight) + up_shift.astype(jnp.float32)
    hidden, pull_gelu = jax.vjp(gelu_exact, hidden_pre)
    hidden_low = hidden.astype(low)
    branch = product(hidden_low, down_weight) + down_shift
    expert_mask = (own_modality == expert_pick).astype(jnp.float32)[:, None]
    output = (residual + branch * expert_mask).astype(low)
    live_rows = (own_modality < 2).astype(jnp.float32)[:, None]
    out_grad = cotangent.astype(jnp.float32) * live_rows
    branch_grad = (out_grad * expert_mask).astype(low)
    grad_down = product_lead(hidden_low, branch_grad)
    grad_down_shift = jnp.sum(branch_grad.astype(jnp.float32), axis=0)
    hidden_grad = product_trail(branch_grad, down_weight)
    pre_grad = pull_gelu(hidden_grad)[0].astype(low)
    grad_up = product_lead(normed_two_low, pre_grad)
    grad_up_shift = jnp.sum(pre_grad.astype(jnp.float32), axis=0)
    norm_two_grad = product_trail(pre_grad, up_weight)
    residual_part, grad_gain_two, grad_shift_two = pull_two(norm_two_grad)
    residual_grad = out_grad + residual_part
    residual_low = residual_grad.astype(low)
    grad_out_weight = product_lead(mixed_low, residual_low)
    grad_out_shift = jnp.sum(residual_low.astype(jnp.float32), axis=0)
    mixed_grad = product_trail(residual_low, out_weight).astype(low)
    factor = lax.rsqrt(totals)
    pick = (jnp.arange(2, dtype=jnp.int32) == expert_pick).astype(jnp.float32) * factor

    def lanes(values):
        values = values.reshape(values.shape[0], devices, -1).transpose(1, 0, 2)
        return jnp.pad(values, ((0, 0), (0, 0), (0, 128 - values.shape[2])))

    def thin_of(rows):
        thin_terms = jnp.concatenate(
            [
                lanes(jnp.stack(rows)),
                lanes(pick[:, None] * grad_up_shift[None]),
                lanes(pick[:, None] * grad_down_shift[None]),
            ],
            axis=1,
        )
        return jnp.pad(thin_terms, ((0, 0), (0, THIN_ROWS - thin_terms.shape[1]), (0, 0)))

    late = [grad_out_shift, grad_gain_two, grad_shift_two]
    if near:
        box = (depth, 2, 2, 2)
        up_sum, down_sum, out_sum, qkv_sum, thin_sum, token_grad = scatter_all(
            grad_up.astype(low).reshape(box + (share, ff)),
            grad_down.astype(low).reshape(box + (ff_share, model_width)),
            grad_out_weight.astype(low).reshape(box + (share, model_width)),
            jnp.broadcast_to(jnp.repeat(factor, 128)[None], (8, 256)),
            thin_of([jnp.zeros_like(grad_out_shift)] * 4 + late).reshape(box + (THIN_ROWS, 128)),
            vectors,
            kind_wide,
            log_total,
            queries,
            kv,
            mixed_grad,
            mixed_t,
            normed_low,
            qkv_weight,
            tokens,
            residual_grad,
            depth,
        )
        out_sum, qkv_sum, thin_sum = out_sum[0], qkv_sum[0], thin_sum[0]
    else:
        scatter = functools.partial(
            lax.psum_scatter, axis_name=both, scatter_dimension=0, tiled=True
        )
        wide = functools.partial(lax.psum_scatter, axis_name=both, scatter_dimension=1, tiled=True)
        query_grad, kv_terms = attend_back(
            kind_wide, place_at, queries, kv, mixed_grad, mixed_t, log_total
        )
        kv_grad = lax.psum_scatter(
            kv_terms.astype(jnp.float32), "stream", scatter_dimension=0, tiled=True
        )
        qkv_grad = jnp.concatenate([query_grad, kv_grad.astype(low)], axis=1)
        grad_qkv = product_lead(normed_low, qkv_grad)
        early = [
            jnp.sum(qkv_grad[:, :model_width].astype(jnp.float32), axis=0),
            jnp.sum(qkv_grad[:, 2 * model_width :].astype(jnp.float32), axis=0),
        ]
        norm_one_grad = product_trail(qkv_grad, qkv_weight)
        token_part, *grads_one = jax.vjp(layer_norm, tokens_f, vectors[0], vectors[1])[1](
            norm_one_grad
        )
        token_grad = (residual_grad + token_part).astype(low)
        up_sum = wide(pick[:, None, None] * grad_up[None])
        down_sum = wide(pick[:, None, None] * grad_down[None])
        out_sum, qkv_sum = scatter(grad_out_weight), scatter(grad_qkv)
        thin_sum = scatter(thin_of(grads_one + early + late))[0]
    small = [thin_sum[k, :share] for k in range(7)]
    return (
        output,
        token_grad,
        small[0],
        small[1],
        qkv_sum,
        small[2],
        small[3],
        out_sum,
        small[4],
        small[5],
        small[6],
        up_sum,
        thin_sum[7:9, :ff_share],
        down_sum,
        thin_sum[9:11, :share],
        totals,
    )


def solution(mesh):
    placed = (
        P(("items", "stream"), None),
        P("items"),
        P(("items", "stream")),
        P(("items", "stream")),
        P(("items", "stream"), None),
        P(("items", "stream")),
        P(("items", "stream")),
        P(("items", "stream"), None),
        P(("items", "stream")),
        P(("items", "stream")),
        P(("items", "stream")),
        P(None, ("items", "stream"), None),
        P(None, ("items", "stream")),
        P(None, ("items", "stream"), None),
        P(None, ("items", "stream")),
        P(("items", "stream"), None),
    )
    near = mesh.shape["items"] == 8 and mesh.shape["stream"] == 4
    return jax.shard_map(
        functools.partial(body, near),
        mesh=mesh,
        in_specs=placed,
        out_specs=(
            P(("items", "stream"), None),
            P(("items", "stream"), None),
            P(("items", "stream")),
            P(("items", "stream")),
            P(("items", "stream"), None),
            P(("items", "stream")),
            P(("items", "stream")),
            P(("items", "stream"), None),
            P(("items", "stream")),
            P(("items", "stream")),
            P(("items", "stream")),
            P(None, ("items", "stream"), None),
            P(None, ("items", "stream")),
            P(None, ("items", "stream"), None),
            P(None, ("items", "stream")),
            P(),
        ),
        check_vma=False,
    )
```

time: 495 us -> 427 us (0.86)
  the two profiles are of different devices: /device:TPU:0 before, /device:TPU:1 now
where the time goes in v3:
time: 427 us; the launch traced here: 423 us
  Pallas kernels  331 us (78%)
  matrix products  62 us (15%)
  local copies, waits for them, and re-layouts  18.5 us (4%)
  other arithmetic  9.67 us (2%)
    pallas_call x1, Pallas kernels, scatter_all(): pl.pallas_call(functools.partial(scatter_kernel, depth, kinds, chunks, cu...  189 us
    pallas_call x1, Pallas kernels, gather_all(): pl.pallas_call(functools.partial(gather_kernel, depth, chunks, entries),...  143 us
    dot_general x3, matrix products, product(): return jnp.dot(first_op, second_op, preferred_element_type=jnp.float32)  29.8 us
    dot_general x3, matrix products, product_trail(): lax.dot_general(first_op, second_op, (((1,), (1,)), ((), ())), preferred_...  16.7 us
    dot_general x3, matrix products, product_lead(): lax.dot_general(first_op, second_op, (((0,), (0,)), ((), ())), preferred_...  15.5 us
    unnamed x52, local copies, waits for them, and re-layouts  11.7 us

profile of v3, /device:TPU:1, one launch (start us, length us, event | category | flops | bytes accessed | tf_op | source)
XLA Modules:
  0.0 423.5 jit_solution(393762917677064279)
XLA Ops:
  1.3 0.0 copy-start.7
  1.3 0.8 stack.55
  2.1 0.7 fusion.53
  2.8 0.0 copy-start
  2.8 1.1 copy-done
  3.9 1.0 copy-done.3
  4.9 1.0 copy-done.4
  5.9 0.9 copy-done.5
  6.8 0.8 copy-done.8
  7.5 142.6 %shard_map.279 = (bf16[4,2,2,2,16,128]{5,4,3,2,1,0:T(8,128)(2,1)S(1)}, bf16[4,2,2,2,24,768]{5,4,3,2,1,0:T(8,128)(2,1)S(1)}, bf16[2,4,2,2,2,24,3072]{6,5,4,3,2,1,...) custom-call(bf16[16,128]{1,0:T(8,128)(2,1)S(1)} %pad.40.refs_0_, ...), custom_call_target="tpu_custom_call" | custom-call | tf_op jit(solution)/shard_map/pallas_call | solution.py:695
  150.2 0.0 copy-start.1
  150.2 0.9 copy-done.1
  151.1 0.9 copy-done.2
  152.0 0.6 copy-done.9
  152.6 2.0 fusion.76
  154.7 0.3 multiply_reduce_fusion.2
  155.0 0.8 copy-done.11
  155.8 0.1 reshape.200
  155.9 0.0 copy-start.15
  155.9 20.9 %multiply_convert_fusion = (bf16[512,3072]{1,0:T(8,128)(2,1)}, f32[512,3072]{1,0:T(8,128)}, f32[512,3072]{1,0:T(8,128)}) fusion(f32[3072]{0:T(1024)S(1)} %bitcast.90, bf16[2,768,3072]{2,1,0:T(8,128)(2,1)} %bitcast.104, s32[]{:T(128)S(6)} %select_n.176, f32[512,768]{1,0:T(8,128)} %copy-done.11, f32[768]{0:T(1024)S(1)} %get-tuple-element.56, ...), kind=kOutput, calls=%fused_computation.4 | convolution fusion | flops 2521694208 | bytes 22042628 | tf_op jit(solution)/shard_map/dot_general | solution.py:47
  176.8 0.0 copy-done.7
  176.8 0.1 fusion.63
  176.9 0.0 copy-done.15
  177.0 10.1 %convert_reduce_fusion = (f32[3072]{0:T(1024)S(1)}, bf16[512,3072]{1,0:T(8,128)(2,1)}) fusion(f32[512,3072]{1,0:T(8,128)} %get-tuple-element.68, bf16[2,3072,768]{2,1,0:T(8,128)(2,1)} %bitcast.102, s32[]{:T(128)S(6)} %select_n.176, bf16[512,768]{1,0:T(8,128)(2,1)S(1)} %copy-done.15, f32[512]{0:T(512)S(1)} %get-tuple-element.84, ...), kind=kOutput, calls=%fused_computation.2 | convolution fusion | flops 2444227584 | bytes 21262340 | tf_op jit(solution)/shard_map/dot_general | solution.py:57
  187.1 4.9 %multiply_reduce_fusion = (f32[768]{0:T(1024)S(1)}, f32[512]{0:T(512)S(1)}, f32[768]{0:T(1024)S(1)}, f32[512,768]{1,0:T(8,128)S(1)}) fusion(f32[512,768]{1,0:T(8,128)S(1)} %copy-done.12, f32[512]{0:T(512)S(1)} %fusion.65, f32[512]{0:T(512)S(1)} %broadcast_multiply_fusion.2, f32[768]{0:T(1024)S(1)} %get-tuple-element.57, ...), kind=kOutput, calls=%fused_computation.34 | convolution fusion | flops 2419062784 | bytes 11026436 | tf_op jit(solution)/shard_map/dot_general | solution.py:57
  192.0 0.7 fusion.74
  192.7 0.4 convert_reduce_fusion.2
  193.1 1.7 convolution_convert_fusion.3.refs_10_
  194.9 0.1 stack.60
  194.9 0.1 stack.61
  195.0 0.1 stack.62
  195.1 0.1 maximum_bitcast_fusion
  195.2 0.1 mul.182
  195.3 0.1 slice.54
  195.4 0.6 convert_reduce_fusion.3
  196.0 0.6 convert_reduce_fusion.4
  196.6 0.6 convert_reduce_fusion.5
  197.2 0.6 convert_reduce_fusion.6
  197.9 3.2 fusion.70
  201.1 1.4 compare_select_fusion.3
  202.4 0.1 broadcast_multiply_fusion.1
  202.5 0.1 mul.186
  202.6 0.1 broadcast_multiply_fusion
  202.7 0.1 select_maximum_fusion
  202.8 0.7 pad.44
  203.5 3.3 convolution_convert_fusion.2
  206.8 7.6 %convolution_convert_fusion.1 = bf16[768,3072]{1,0:T(8,128)(2,1)} fusion(bf16[512,3072]{1,0:T(8,128)(2,1)} %get-tuple-element.82, f32[512,768]{1,0:T(8,128)} %copy-done.11, f32[768]{0:T(1024)S(1)} %get-tuple-element.56, f32[768]{0:T(1024)S(1)} %get-tuple-element.57, f32[512]{0:T(512)S(1)} %fusion.65, f32[512]{0:T(512)S(1)} %broadcast_multiply_fusion.2), kind=kOutput, calls=%fused_computation.19 | convolution fusion | flops 2420244480 | bytes 9447424 | tf_op jit(solution)/shard_map/dot_general | solution.py:51
  214.4 0.0 copy-done.22
  214.4 4.6 %convolution_convert_fusion = bf16[3072,768]{1,0:T(8,128)(2,1)} fusion(bf16[512,3072]{1,0:T(8,128)(2,1)S(1)} %copy-done.22, bf16[512,768]{1,0:T(8,128)(2,1)S(1)} %copy-done.15, f32[512]{0:T(512)S(1)} %get-tuple-element.84, f32[512]{0:T(512)S(1)} %get-tuple-element.83), kind=kOutput, calls=%fused_computation.18 | convolution fusion | flops 2419851264 | bytes 8654848 | tf_op jit(solution)/shard_map/dot_general | solution.py:51
  219.0 0.1 broadcast_bitcast_fusion
  219.0 0.6 broadcast_in_dim.82.refs_3_
  219.6 188.6 %shard_map.280 = (f32[2,24,3072]{2,1,0:T(8,128)}, f32[2,96,768]{2,1,0:T(8,128)}, f32[1,24,768]{2,1,0:T(8,128)}, f32[1,24,2304]{2,1,0:T(8,128)}, f32[1,16,128]{2,...) custom-call(bf16[4,2,2,2,24,3072]{5,4,3,2,1,0:T(8,128)(2,1)} %bitcast.81, ...), custom_call_target="tpu_custom_call" | custom-call | tf_op jit(solution)/shard_map/pallas_call | solution.py:1149
  408.3 1.5 slice_bitcast_fusion
  409.7 1.3 slice.72
  411.0 1.2 slice.73
  412.2 0.0 copy-done.13
  412.3 6.9 %add_convert_fusion.1 = bf16[512,768]{1,0:T(8,128)(2,1)} fusion(f32[512,768]{1,0:T(8,128)S(1)} %copy-done.13, bf16[512,3072]{1,0:T(8,128)(2,1)} %get-tuple-element.67, bf16[2,3072,768]{2,1,0:T(8,128)(2,1)} %bitcast.103, s32[]{:T(128)S(6)} %select_n.176, f32[512]{0:T(512)S(1)} %get-tuple-element.83, f32[768]{0:T(1024)S(1)} %get-tuple-element.55), kind=kOutput, calls=%fused_computation.40 | convolution fusion | flops 2417491968 | bytes 10228740 | tf_op jit(solution)/shard_map/dot_general | solution.py:47
  419.2 0.0 copy-done.14
  419.2 0.9 copy.45
  420.1 0.7 copy.46
  420.8 0.6 copy.47
  421.4 0.0 copy-done.17
  421.4 0.8 copy.48
  422.2 0.8 copy.49
  (40 shorter events, 0.2 us)
Async XLA Ops:
  1.3 175.5 %copy-start.7 = (f32[8,128]{1,0:T(8,128)}, f32[8,128]{1,0:T(8,128)S(1)}, u32[]{:S(2)}) copy-start(f32[8,128]{1,0:T(8,128)S(1)} %broadcast_in_dim.71.refs_6_) | copy-start | bytes 12292
  2.8 1.1 copy-start
  3.9 1.0 copy-start.3
  4.9 1.0 copy-start.4
  5.9 0.9 copy-start.5
  6.8 0.8 copy-start.8
  150.2 0.9 copy-start.1
  151.1 0.9 copy-start.2
  152.0 0.6 copy-start.9
  152.6 42.7 %copy-start.6 = (f32[16,768]{1,0:T(8,128)}, f32[16,768]{1,0:T(8,128)S(1)}, u32[]{:S(2)}) copy-start(f32[16,768]{1,0:T(8,128)S(1)} %get-tuple-element.36.refs_5_) | copy-start | bytes 147460
  154.6 1.1 copy-start.11
  155.9 21.0 %copy-start.15 = (bf16[512,768]{1,0:T(8,128)(2,1)S(1)}, bf16[512,768]{1,0:T(8,128)(2,1)}, u32[]{:S(2)}) copy-start(bf16[512,768]{1,0:T(8,128)(2,1)} %param.31) | copy-start | bytes 2359300
  176.9 10.2 %copy-start.12 = (f32[512,768]{1,0:T(8,128)S(1)}, f32[512,768]{1,0:T(8,128)}, u32[]{:S(2)}) copy-start(f32[512,768]{1,0:T(8,128)} %copy-done.11) | copy-start | bytes 4718596
  176.9 10.2 %copy-start.21 = (bf16[2,4,2,2,2,24,3072]{6,5,4,3,2,1,0:T(8,128)(2,1)S(1)}, bf16[2,4,2,2,2,24,3072]{6,5,4,3,2,1,0:T(8,128)(2,1)}, u32[]{:S(2)}) copy-start(bf16[2,4,2,2,2,24,3072]{6,5,4,3,2,1,0:T(8,128)(2,1)} %get-tuple-element.37) | copy-start | bytes 28311556
  193.1 1.7 copy-start.10
  202.4 16.5 %copy-start.20 = (f32[2]{0:T(128)}, f32[2]{0:T(128)S(1)}, u32[]{:S(2)}) copy-start(f32[2]{0:T(128)S(1)} %get-tuple-element.116) | copy-start | bytes 28
  206.8 7.6 %copy-start.22 = (bf16[512,3072]{1,0:T(8,128)(2,1)S(1)}, bf16[512,3072]{1,0:T(8,128)(2,1)}, u32[]{:S(2)}) copy-start(bf16[512,3072]{1,0:T(8,128)(2,1)} %get-tuple-element.67) | copy-start | bytes 9437188
  219.6 192.6 %copy-start.13 = (f32[512,768]{1,0:T(8,128)S(1)}, f32[512,768]{1,0:T(8,128)}, u32[]{:S(2)}) copy-start(f32[512,768]{1,0:T(8,128)} %copy-done.11) | copy-start | bytes 4718596
  412.2 7.0 %copy-start.14 = (bf16[512,768]{1,0:T(8,128)(2,1)S(1)}, bf16[512,768]{1,0:T(8,128)(2,1)}, u32[]{:S(2)}) copy-start(bf16[512,768]{1,0:T(8,128)(2,1)} %get-tuple-element.102) | copy-start | bytes 2359300
  412.3 7.8 %copy-start.18 = (f32[1,24,2304]{2,1,0:T(8,128)S(1)}, f32[1,24,2304]{2,1,0:T(8,128)}, u32[]{:S(2)}) copy-start(f32[1,24,2304]{2,1,0:T(8,128)} %get-tuple-element.48) | copy-start | bytes 663556
  412.3 8.5 %copy-start.19 = (f32[1,24,768]{2,1,0:T(8,128)S(1)}, f32[1,24,768]{2,1,0:T(8,128)}, u32[]{:S(2)}) copy-start(f32[1,24,768]{2,1,0:T(8,128)} %get-tuple-element.49) | copy-start | bytes 221188
  412.3 9.2 %copy-start.17 = (f32[2,24,3072]{2,1,0:T(8,128)S(1)}, f32[2,24,3072]{2,1,0:T(8,128)}, u32[]{:S(2)}) copy-start(f32[2,24,3072]{2,1,0:T(8,128)} %get-tuple-element.112) | copy-start | bytes 1769476
  412.3 10.0 %copy-start.16 = (f32[2,96,768]{2,1,0:T(8,128)S(1)}, f32[2,96,768]{2,1,0:T(8,128)}, u32[]{:S(2)}) copy-start(f32[2,96,768]{2,1,0:T(8,128)} %get-tuple-element.114) | copy-start | bytes 1769476

commit v4 on v3

--- a/solution.py
+++ b/solution.py
@@ -74,16 +74,16 @@
 
 def gather_chunks(share, width, ff_share, ff):
     rows = (0, share)
-    near_cols = divided(3 * width, 128, 7, 7, 4)
-    out_cols = divided(width, 128, 2, 3, 1)
-    up_cols = divided(ff, 128, 6, 13, 5)
-    down_rows = divided(ff_share, 16, 2, 3, 1)
+    near_cols = divided(3 * width, 128, 9, 9)
+    out_cols = divided(width, 128, 3, 3)
+    up_cols = divided(ff, 128, 4, 14, 6)
+    down_rows = divided(ff_share, 16, 1, 3, 2)
     chunks = [
         [((0, None), (0, THIN_ROWS), (0, 128), 0, False)]
         + [((1, None), rows, cols, order, False) for order, cols in enumerate(near_cols)],
         [((2, None), rows, cols, order, False) for order, cols in enumerate(out_cols)],
     ]
-    for e in range(2):
+    for e in (1, 0):
         chunks.append([((3, e), rows, cols, order, e == 1) for order, cols in enumerate(up_cols)])
         chunks.append(
             [((4, e), band, (0, width), order, e == 1) for order, band in enumerate(down_rows)]
@@ -95,15 +95,15 @@
     rows = (0, share)
     near_cols = divided(3 * width, 128, 7, 7, 4)
     out_cols = divided(width, 128, 2, 3, 1)
-    up_cols = divided(ff, 128, 6, 13, 5)
-    down_rows = divided(ff_share, 16, 2, 3, 1)
+    up_cols = divided(ff, 128, 4, 14, 6)
+    down_rows = divided(ff_share, 16, 1, 3, 2)
     chunks = [[(2, 0, rows, cols, order) for order, cols in enumerate(out_cols)]]
-    for e in range(2):
+    for e in (1, 0):
         chunks.append([(0, e, rows, cols, order) for order, cols in enumerate(up_cols)])
         chunks.append(
             [(1, e, band, (0, width), order) for order, band in enumerate(down_rows)]
         )
-    chunks.append([])
+    chunks += [[], [], [], []]
     chunks.append(
         [(3, 0, rows, cols, order) for order, cols in enumerate(near_cols)]
         + [(4, 0, (0, THIN_ROWS), (0, 128), 0)]
@@ -283,7 +283,7 @@
 
 
 def back_group(
-    group, kind, stream, log_total, keys_ref, values_ref, q_ref, g_ref, mixed_t, dq_ref,
+    group, kind, stream, log_total, keys_ref, values_ref, q_ref, g_ref, mixed_t, dq_ref, between,
     keys_t, scaled, grads, scaled_t, grads_t, dq_t, centre, dk, dv,
 ):
     everyone, width = keys_ref.shape
@@ -315,6 +315,8 @@
 
     for qt in range(rows // TQ):
         here = slice(qt * TQ, (qt + 1) * TQ)
+        if qt:
+            between()
         dq_t[...] = jnp.zeros(dq_t.shape, jnp.float32)
 
         @pl.loop(0, everyone // TK)
@@ -374,7 +376,8 @@
     width = q_ref.shape[1]
     back_group(
         0, kind, place_ref[0], log_total, kv_ref.at[:, pl.ds(0, width)],
-        kv_ref.at[:, pl.ds(width, width)], q_ref, g_ref, mixed_t, dq_ref, *work,
+        kv_ref.at[:, pl.ds(width, width)], q_ref, g_ref, mixed_t, dq_ref, lambda: None,
+        *work,
     )
     dk, dv = work[-2:]
 
@@ -413,10 +416,172 @@
         compiler_params=pltpu.CompilerParams(vmem_limit_bytes=58 << 20),
     )(kind, place_at, queries, kv, mixed_grad, mixed_t, log_total)
 
+def feed_kernel(
+    pick, place_ref, kind, vectors, up_shift, tokens, mixed, out_weight, cotangent, up, down,
+    output, residual_grad, grad_out, mixed_grad, grad_up, grad_down, small, up_shift_sum,
+    residual, normed, normed_t, grad, branch, back,
+):
+    step = pl.program_id(0)
+    rows, width = tokens.shape
+    image_rows = (lax.axis_size("stream") - 1) * rows
+    tall = 128
+
+    def blocks(act):
+        @pl.loop(0, rows // tall)
+        def _(j):
+            act(pl.ds(pl.multiple_of(j * tall, tall), tall))
+
+    def unit_of(value):
+        centred = value - jnp.mean(value, axis=-1, keepdims=True)
+        scale = lax.rsqrt(jnp.mean(centred * centred, axis=-1, keepdims=True) + NORM_EPS)
+        return centred * scale, scale
+
+    def live(j_start):
+        position = lax.broadcasted_iota(jnp.int32, (tall, 1), 0) + (place_ref[0] * rows + j_start)
+        return member_of(kind[0:1, 0:1], position.astype(jnp.float32), image_rows) >= 0.0
+
+    @pl.when(step == 0)
+    def _():
+        @pl.loop(0, rows // tall)
+        def _(j):
+            block = pl.ds(pl.multiple_of(j * tall, tall), tall)
+            value = (
+                tokens[block, :].astype(jnp.float32)
+                + jnp.dot(mixed[block, :], out_weight[...], preferred_element_type=jnp.float32)
+                + vectors[4:5, :]
+            )
+            residual[block, :] = value
+            unit, _ = unit_of(value)
+            normed[block, :] = (unit * vectors[5:6, :] + vectors[6:7, :]).astype(jnp.bfloat16)
+            given = cotangent[block, :]
+            grad[block, :] = jnp.where(live(j * tall), given, jnp.zeros_like(given))
+
+        normed_t[...] = normed[...].T
+        branch[...] = jnp.zeros(branch.shape, jnp.float32)
+        back[...] = jnp.zeros(back.shape, jnp.float32)
+
+    before = (
+        jnp.dot(normed[...], up[0], preferred_element_type=jnp.float32) + up_shift[0].astype(jnp.float32)
+    )
+    hidden_grad = product_trail(grad[...], down[0])
+    half = 0.5 + 0.5 * lax.erf(before * 0.5**0.5)
+    hidden = (before * half).astype(jnp.bfloat16)
+    slope = half + before * (jnp.exp(-0.5 * before * before) * 0.3989422804014327)
+    before_grad = hidden_grad * slope
+    low_grad = before_grad.astype(jnp.bfloat16)
+    up_shift_sum[...] = jnp.broadcast_to(
+        jnp.sum(low_grad.astype(jnp.float32), axis=0, keepdims=True), up_shift_sum.shape
+    )
+    branch[...] += jnp.dot(hidden, down[0], preferred_element_type=jnp.float32)
+    back[...] += product_trail(low_grad, up[0])
+    grad_up[...] = jnp.dot(normed_t[...], low_grad, preferred_element_type=jnp.float32).astype(
+        jnp.bfloat16
+    )
+    grad_down[...] = jnp.dot(hidden.T, grad[...], preferred_element_type=jnp.float32).astype(
+        jnp.bfloat16
+    )
+
+    @pl.when(step == pl.num_programs(0) - 1)
+    def _():
+        down_shift = jnp.where(pick[0] == 0, vectors[9:10, :], vectors[10:11, :])
+
+        def fold(value):
+            return jnp.sum(value.reshape(-1, 8, width), axis=0)
+
+        def finish(j, carry):
+            block = pl.ds(pl.multiple_of(j * tall, tall), tall)
+            value = residual[block, :]
+            kept = live(j * tall)
+            output[block, :] = (
+                value + jnp.where(kept, branch[block, :] + down_shift, 0.0)
+            ).astype(jnp.bfloat16)
+            unit, scale = unit_of(value)
+            given = back[block, :]
+            lifted = given * vectors[5:6, :]
+            inner = jnp.mean(lifted * unit, axis=-1, keepdims=True)
+            own = grad[block, :].astype(jnp.float32)
+            total = own + scale * (
+                lifted - jnp.mean(lifted, axis=-1, keepdims=True) - unit * inner
+            )
+            residual_grad[block, :] = total
+            total_low = total.astype(jnp.bfloat16)
+            normed[block, :] = total_low
+            mixed_grad[block, :] = product_trail(total_low, out_weight[...]).astype(jnp.bfloat16)
+            terms = (total_low.astype(jnp.float32), given * unit, given, own)
+            return tuple(held + fold(term) for held, term in zip(carry, terms))
+
+        zero = jnp.zeros((8, width), jnp.float32)
+        sums = lax.fori_loop(0, rows // tall, finish, (zero,) * 4)
+        lines = [jnp.sum(value, axis=0, keepdims=True) for value in sums]
+        small[...] = jnp.concatenate(lines + [jnp.zeros((4, width), jnp.float32)], axis=0)
+        grad_out[...] = jnp.dot(
+            mixed[...].T, normed[...], preferred_element_type=jnp.float32
+        ).astype(jnp.bfloat16)
+
+
+def feed(pick, place_at, kind, vectors, up_shift, tokens, mixed, out_weight, cotangent, up, down):
+    rows, width = tokens.shape
+    ff = up.shape[2]
+    band = 512
+    low, wide = jnp.bfloat16, jnp.float32
+
+    def whole(array):
+        return pl.BlockSpec(array.shape, lambda i, pick, place_at: (0,) * array.ndim)
+
+    fixed = [
+        jax.ShapeDtypeStruct((rows, width), low),
+        jax.ShapeDtypeStruct((rows, width), wide),
+        jax.ShapeDtypeStruct((width, width), low),
+        jax.ShapeDtypeStruct((rows, width), low),
+    ]
+    last = jax.ShapeDtypeStruct((8, width), wide)
+    return pl.pallas_call(
+        feed_kernel,
+        out_shape=fixed
+        + [
+            jax.ShapeDtypeStruct((width, ff), low),
+            jax.ShapeDtypeStruct((ff, width), low),
+            last,
+            jax.ShapeDtypeStruct((8, ff), wide),
+        ],
+        grid_spec=pltpu.PrefetchScalarGridSpec(
+            num_scalar_prefetch=2,
+            grid=(ff // band,),
+            in_specs=[
+                whole(kind),
+                whole(vectors),
+                pl.BlockSpec((1, 1, band), lambda i, pick, place_at: (pick[0], 0, i)),
+                whole(tokens),
+                whole(mixed),
+                whole(out_weight),
+                whole(cotangent),
+                pl.BlockSpec((1, width, band), lambda i, pick, place_at: (pick[0], 0, i)),
+                pl.BlockSpec((1, band, width), lambda i, pick, place_at: (pick[0], i, 0)),
+            ],
+            out_specs=[whole(array) for array in fixed]
+            + [
+                pl.BlockSpec((width, band), lambda i, pick, place_at: (0, i)),
+                pl.BlockSpec((band, width), lambda i, pick, place_at: (i, 0)),
+                whole(last),
+                pl.BlockSpec((8, band), lambda i, pick, place_at: (0, i)),
+            ],
+            scratch_shapes=[
+                pltpu.VMEM((rows, width), wide),
+                pltpu.VMEM((rows, width), low),
+                pltpu.VMEM((width, rows), low),
+                pltpu.VMEM((rows, width), low),
+                pltpu.VMEM((rows, width), wide),
+                pltpu.VMEM((rows, width), wide),
+            ],
+        ),
+        compiler_params=pltpu.CompilerParams(vmem_limit_bytes=56 << 20),
+    )(pick, place_at, kind, vectors, up_shift, tokens, mixed, out_weight, cotangent, up, down)
+
 
 MESH = pl.DeviceIdType.MESH
-GATHER_ORDERS = (("z", "x", "y"), ("z", "y", "x"), ("y", "x", "z"))
-SCATTER_ORDERS = (("y", "x", "z"), ("x", "y", "z"), ("z", "x", "y"))
+GATHER_ORDERS = (("z", "f", "x", "y"), ("z", "f", "y", "x"), ("y", "x", "z", "f"))
+SCATTER_ORDERS = (("y", "x", "a", "z"), ("x", "y", "a", "z"), ("a", "z", "x", "y"))
+STEPS = 5
 EVERY = slice(None)
 THIN_ROWS = 16
 
@@ -461,23 +626,30 @@
     )
 
 
-def pipelined(chunks, n_steps, ahead, start, wait, hooks, before):
-    count = len(chunks)
-    for j in range(min(ahead, count)):
-        start(chunks[j], 0)
-    for t in range(count + n_steps - 1):
-        if t in before:
-            before[t]()
-        if t + ahead < count:
-            start(chunks[t + ahead], 0)
-        for step in range(n_steps):
-            j = t - step
-            if 0 <= j < count:
-                wait(chunks[j], step)
-                if step < n_steps - 1:
-                    start(chunks[j], step + 1)
-                if (j, step) in hooks:
-                    hooks[(j, step)]()
+def both_of(first, second):
+    if first is None or second is None:
+        return second if first is None else first
+    return jnp.logical_and(first, second)
+
+
+class Pipeline:
+    def __init__(self, chunks, ahead, start, wait):
+        self.chunks, self.ahead, self.start, self.wait = chunks, ahead, start, wait
+        self.ticks = 0
+        for chunk in chunks[:ahead]:
+            start(chunk, 0)
+
+    def tick(self, times=1):
+        count = len(self.chunks)
+        for t in range(self.ticks, min(self.ticks + times, count + STEPS - 1)):
+            if t + self.ahead < count:
+                self.start(self.chunks[t + self.ahead], 0)
+            for step in range(STEPS):
+                if 0 <= t - step < count:
+                    self.wait(self.chunks[t - step], step)
+                    if step < STEPS - 1:
+                        self.start(self.chunks[t - step], step + 1)
+        self.ticks += times
 
 
 def spots_of(depth):
@@ -556,32 +728,48 @@
     lower, upper = at["y"] == 0, at["y"] == 1
     number = {piece: j for j, piece in enumerate(piece for chunk in chunks for piece in chunk)}
 
+    z = at["z"]
+
     def stage(piece, step):
         entry, band, cols, order, text = piece
         dims = GATHER_ORDERS[order] + ("c",)
         dim = dims[step]
-        held = tuple(EVERY if d in dims[:step] else pl.ds(at[d], 1) for d in "zxyc")
-        view = target(entry).at[held + (pl.ds(*band), pl.ds(*cols))]
-        sends = recvs = None
+        box = (pl.ds(*band), pl.ds(*cols))
+        live = upper if text and "y" in dims[:step] else None
+
+        def held(level):
+            spot = {d: EVERY if d in dims[:step] else pl.ds(at[d], 1) for d in "zxyc"}
+            if level is not None:
+                spot["z"] = pl.ds(level, 1)
+            return target(entry).at[tuple(spot[d] for d in "zxyc") + box]
+
+        if dim == "f":
+            up_view, down_view = held(0), held(depth - 1)
+            up = remote(up_view, up_view, sems, (number[piece], depth + 2), {**at, "z": z + 1})
+            down = remote(down_view, down_view, sems, (number[piece], depth + 2), {**at, "z": z - 1})
+            return [
+                (up, both_of(live, z == depth - 2), both_of(live, z == depth - 1)),
+                (down, both_of(live, z == 1), both_of(live, z == 0)),
+            ]
+        view = held(None)
+        if dim == "z":
+            found = []
+            for k in range(1, depth):
+                to, source_level = lax.rem(z + k, depth), lax.rem(z + depth - k, depth)
+                copy = remote(view, view, sems, (number[piece], k - 1), {**at, "z": to})
+                sends = both_of(live, jnp.abs(to - z) != depth - 1)
+                found.append((copy, sends, both_of(live, jnp.abs(source_level - z) != depth - 1)))
+            return found
+        sem = {"x": depth - 1, "y": depth, "c": depth + 1}[dim]
+        copy = remote(view, view, sems, (number[piece], sem), moved(at, dim, 1, depth))
         if text and dim == "y":
-            sends, recvs = lower, upper
-        elif text and "y" in dims[:step]:
-            sends = recvs = upper
-        found = []
-        for k in range(1, depth if dim == "z" else 2):
-            sem = {"z": k - 1, "x": depth - 1, "y": depth, "c": depth + 1}[dim]
-            found.append(remote(view, view, sems, (number[piece], sem), moved(at, dim, k, depth)))
-        return found, sends, recvs
+            return [(copy, lower, upper)]
+        return [(copy, live, live)]
 
     def each(chunk, step, which, call):
         for piece in chunk:
-            found = stage(piece, step)
-
-            def act(copies=found[0]):
-                for copy in copies:
-                    call(copy)
-
-            guard(found[which], act)
+            for found in stage(piece, step):
+                guard(found[which], functools.partial(call, found[0]))
 
     beside, across = moved(at, "c", 1, depth), moved(at, "y", 1, depth)
     other = across["y"] * 2 + across["c"]
@@ -657,27 +845,31 @@
         return act
 
     everyone = kv.shape[0] // TK
-    pipelined(
+    flow = Pipeline(
         chunks,
-        4,
         2,
         lambda chunk, step: each(chunk, step, 1, lambda copy: copy.start()),
         lambda chunk, step: each(chunk, step, 2, lambda copy: copy.wait_recv()),
-        {
-            (0, 3): project,
-            (2, 3): pass_on,
-            (3, 3): attention(0, 0, everyone),
-            (4, 3): attention(1, 0, everyone // 2),
-        },
-        {},
-    )
+    )
+    flow.tick(5)
+    project()
+    flow.tick()
+    pass_on()
+    flow.tick()
+    attention(0, 0, everyone // 2)()
+    flow.tick()
+    attention(0, everyone // 2, everyone)()
+    flow.tick()
+    attention(1, 0, everyone // 2)()
+    flow.tick()
     attention(1, everyone // 2, everyone)()
+    flow.tick(STEPS + len(chunks))
     for copy in (to_beside, to_across, onward):
         copy.wait_send()
     keep_thin.wait()
     keep_kv.wait()
     for chunk in chunks:
-        for step in range(4):
+        for step in range(STEPS):
             each(chunk, step, 1, lambda copy: copy.wait_send())
 
 
@@ -719,8 +911,8 @@
             pltpu.VMEM((lines, TQ), jnp.float32),
             pltpu.VMEM((lines, TQ), jnp.float32),
             pltpu.SemaphoreType.DMA((len(entries),)),
-            pltpu.SemaphoreType.DMA((n_pieces, depth + 2)),
-            pltpu.SemaphoreType.DMA((n_pieces, depth + 2)),
+            pltpu.SemaphoreType.DMA((n_pieces, depth + 3)),
+            pltpu.SemaphoreType.DMA((n_pieces, depth + 3)),
             pltpu.SemaphoreType.DMA((3,)),
             pltpu.SemaphoreType.DMA((3,)),
             pltpu.SemaphoreType.DMA((2,)),
@@ -736,12 +928,12 @@
     it = iter(refs)
     take = lambda count: [next(it) for _ in range(count)]
     far = take(n_far)
-    factor, thin_in, vectors, kind, log_total = take(5)
+    factor, small, up_shift_sum, vectors, kind, log_total = take(6)
     queries, kv, mixed_grad, mixed_t, normed, weight, tokens, residual_grad = take(8)
     outs = take(n)
     token_grad, kv_away = take(2)
     acc, first, second, last = take(n), take(n), take(n), take(n)
-    z_first, z_second, z_last = take(n), take(n), take(n)
+    relay, z_relay, z_first, z_second, z_last = (take(n) for _ in range(5))
     own_half = take(n_far)
     qkv_terms, thin_terms, kv_sum, kv_got, kv_mine, dq = take(6)
     sems = take(2)
@@ -772,6 +964,12 @@
     beside_image = jnp.logical_or(lower, c == 1)
     number = {piece: j for j, piece in enumerate(piece for chunk in chunks for piece in chunk)}
 
+    sources = (
+        (z == 0, range(2, depth)),
+        (jnp.logical_and(z > 0, z < depth - 1), range(1, depth)),
+        (z == depth - 1, range(1, depth - 1)),
+    )
+
     def boxes(piece):
         k, e, band, cols, order = piece
         cut = cuts[k] if order == 2 else (0, 0)
@@ -803,17 +1001,31 @@
             sends, recvs = upper, lower
         elif text and "y" not in dims[:step]:
             sends = recvs = upper
+        where = (EVERY, EVERY) if order == 2 else (x, y)
+        if dim == "a":
+            src = here.at[(depth - 1 - z,) + where + box]
+            dst = z_relay[k].at[(e, EVERY, EVERY) + inner] if order == 2 else relay[k].at[(e,) + inner]
+            to = {**at, "z": jnp.where(z == 0, 1, depth - 2)}
+            copy = remote(src, dst, sems, (number[piece], depth + 2), to)
+            ends = jnp.logical_or(z == 0, z == depth - 1)
+            middle = jnp.logical_and(z > 0, z < depth - 1)
+            return [(copy, both_of(sends, ends), both_of(recvs, middle))]
         if dim == "z":
             found = []
             for by in range(1, depth):
-                to = lax.rem(z + by, depth)
+                to, source_level = lax.rem(z + by, depth), lax.rem(z + depth - by, depth)
+                src = here.at[(to,) + where + box]
                 if order == 2:
-                    src = here.at[(to, EVERY, EVERY) + box]
                     dst = z_first[k].at[(e, by - 1, EVERY, EVERY) + inner]
                 else:
-                    src = here.at[(to, x, y) + box]
                     dst = last[k].at[(e, by - 1) + inner]
-                found.append((make(src, dst, 2 + by, by), sends, recvs))
+                found.append(
+                    (
+                        make(src, dst, 2 + by, by),
+                        both_of(sends, jnp.abs(to - z) != depth - 1),
+                        both_of(recvs, jnp.abs(source_level - z) != depth - 1),
+                    )
+                )
             return found
         if order == 2 and dim == "x":
             src, dst = here.at[(z, 1 - x, EVERY) + box], z_second[k].at[(e, EVERY) + inner]
@@ -863,7 +1075,21 @@
                 pl.when(text_device)(lambda: over(spots, own, True))
             else:
                 over(spots, own, False)
-        elif step == 3:
+        elif dim == "a":
+            dest = jnp.where(z == 1, depth - 1, 0)
+
+            def act():
+                if order == 2:
+                    for spot in [(0, 0), (0, 1), (1, 0), (1, 1)]:
+                        where = (dest,) + spot + box
+                        here[where] = here[where] + z_relay[k][(e,) + spot + inner]
+                else:
+                    where = (dest, x, y) + box
+                    here[where] = here[where] + relay[k][(e,) + inner]
+
+            middle = jnp.logical_and(z > 0, z < depth - 1)
+            guard(both_of(upper if text and order == 2 else None, middle), act)
+        elif step == STEPS - 1:
 
             def finish(total):
                 if kinds[k]:
@@ -881,24 +1107,32 @@
                 else:
                     finish(own() + got())
             else:
-                total = own()
-                for by in range(depth - 1):
-                    total = total + wide(last[k][(e, by) + inner])
-                finish(total)
-        elif order == 2:
-
-            def act():
-                if step == 1:
+                for cond, bys in sources:
+
+                    @pl.when(cond)
+                    def _(bys=bys):
+                        total = own()
+                        for by in bys:
+                            total = total + wide(last[k][(e, by - 1) + inner])
+                        finish(total)
+        elif dim == "z":
+            for cond, bys in sources:
+
+                def act(bys=bys):
                     for spot in [(0, 0), (0, 1), (1, 0), (1, 1)]:
                         where = (z,) + spot + box
                         total = wide(here[where])
-                        for by in range(depth - 1):
-                            total = total + wide(z_first[k][(e, by) + spot + inner])
+                        for by in bys:
+                            total = total + wide(z_first[k][(e, by - 1) + spot + inner])
                         here[where] = total.astype(here.dtype)
-                else:
-                    for other in range(2):
-                        where = (z, x, other) + box
-                        here[where] = here[where] + z_second[k][(e, other) + inner]
+
+                guard(both_of(upper if text else None, cond), act)
+        elif order == 2:
+
+            def act():
+                for other in range(2):
+                    where = (z, x, other) + box
+                    here[where] = here[where] + z_second[k][(e, other) + inner]
 
             guard(upper if text else None, act)
         elif step == 1:
@@ -948,7 +1182,6 @@
             copy.wait()
         flipped[...] = normed_in[...].T
         qkv_grad[:, :width] = dq[...]
-        thin_terms[...] = thin_in[...]
         kv_across.wait_recv()
 
         def fold(value):
@@ -997,10 +1230,24 @@
         store = pltpu.make_async_copy(token_out, token_grad, away_sem.at[0])
         store.start()
         lines = [jnp.sum(value, axis=0, keepdims=True) for value in (sum_gain, sum_shift, sum_q, sum_v)]
-        stacked = jnp.concatenate(lines + [jnp.zeros((4, width), jnp.float32)], axis=0)
-        flat = dealt(stacked, share, devices)
+        def stack(parts):
+            count = sum(part.shape[0] for part in parts)
+            return jnp.concatenate(parts + [jnp.zeros((8 - count, parts[0].shape[1]), jnp.float32)])
+
+        scales = [
+            jnp.where(text_device == (e == 1), factor[0:1, e * 128 : e * 128 + 1], 0.0)
+            for e in range(2)
+        ]
+        down_part = [small[3:4, :] * scale for scale in scales]
+        up_part = [up_shift_sum[0:1, :] * scale for scale in scales]
+        ff = up_shift_sum.shape[1]
+        head = dealt(stack(lines + [small[0:3, :]]), share, devices)
+        tail = dealt(stack(down_part), share, devices) + dealt(
+            stack([jnp.zeros((2, ff), jnp.float32)] + up_part), ff // devices, devices
+        )
         for index, spot in enumerate(spots):
-            thin_terms[spot + (slice(0, 8),)] += flat[index * 8 : (index + 1) * 8]
+            rows_of = slice(index * 8, (index + 1) * 8)
+            thin_terms[spot] = jnp.concatenate([head[rows_of], tail[rows_of]], axis=0)
         store.wait()
 
     def project_scope():
@@ -1038,7 +1285,7 @@
                 copy.wait()
             back_group(
                 group, kind, stream, log_total, keys, values, q_in, g_in, mixed_in,
-                dq.at[:, cols], *work,
+                dq.at[:, cols], flow.tick, *work,
             )
             dk, dv = work[-2:]
             for part, (terms, rest, begin) in enumerate(((dk, keys, cols), (dv, values, value_cols))):
@@ -1094,19 +1341,27 @@
 
         return scope
 
-    before = {0: attention(0), 1: attention(1), 3: halve, 4: project_scope}
-    pipelined(chunks, 4, 2, start, wait, {}, before)
+    flow = Pipeline(chunks, 2, start, wait)
+    flow.tick(2)
+    attention(0)()
+    flow.tick()
+    attention(1)()
+    flow.tick()
+    halve()
+    flow.tick()
+    project_scope()
+    flow.tick(STEPS + len(chunks))
     for copy in (kv_beside, kv_across):
         copy.wait_send()
     for chunk in chunks:
-        for step in range(4):
+        for step in range(STEPS):
             for piece in chunk:
                 for copy, sends, _ in copies_of(piece, step):
                     guard(sends, copy.wait_send)
 
 
 def scatter_all(
-    up, down, out, factor, thin, vectors, kind, log_total,
+    up, down, out, factor, small, up_shift_sum, vectors, kind, log_total,
     queries, kv, mixed_grad, mixed_t, normed, weight, tokens, residual_grad, depth,
 ):
     rows, width = tokens.shape
@@ -1117,7 +1372,7 @@
     n_pieces = sum(len(chunk) for chunk in chunks)
     anywhere, inside = pl.BlockSpec(memory_space=pl.ANY), pl.BlockSpec(memory_space=pltpu.VMEM)
     low, box = jnp.bfloat16, (depth, 2, 2, 2)
-    tails = [a.shape[4:] for a in far] + [(share, 3 * width), thin.shape[4:]]
+    tails = [a.shape[4:] for a in far] + [(share, 3 * width), (THIN_ROWS, 128)]
     dtypes = [low] * 4 + [jnp.float32]
     experts = [2 if kind else 1 for kind in kinds]
     scratch = [
@@ -1129,18 +1384,19 @@
         turned.append((tail[0] - cut[0], tail[1] - cut[1]) if any(cut) else (8, 128))
     for middle in ((depth, 2), (depth,), (depth - 1,)):
         scratch += [pltpu.VMEM((e,) + middle + t, d) for e, t, d in zip(experts, plain, dtypes)]
-    for middle in ((depth - 1, 2, 2), (2,), ()):
+    scratch += [pltpu.VMEM((e,) + t, d) for e, t, d in zip(experts, plain, dtypes)]
+    for middle in ((2, 2), (depth - 1, 2, 2), (2,), ()):
         scratch += [pltpu.VMEM((e,) + middle + t, d) for e, t, d in zip(experts, turned, dtypes)]
     scratch += [pltpu.VMEM((depth, 2, 2) + a.shape[4:], low) for a in far]
     scratch += [
         pltpu.VMEM(box + (share, 3 * width), low),
-        pltpu.VMEM(thin.shape, jnp.float32),
+        pltpu.VMEM(box + (THIN_ROWS, 128), jnp.float32),
         pltpu.VMEM((2, rows, 2 * width), low),
         pltpu.VMEM((rows, 2 * width), low),
         pltpu.VMEM((2, rows, 2 * width), low),
         pltpu.VMEM((rows, width), low),
-        pltpu.SemaphoreType.DMA((n_pieces, depth + 2)),
-        pltpu.SemaphoreType.DMA((n_pieces, depth + 2)),
+        pltpu.SemaphoreType.DMA((n_pieces, depth + 3)),
+        pltpu.SemaphoreType.DMA((n_pieces, depth + 3)),
         pltpu.SemaphoreType.DMA((3,)),
         pltpu.SemaphoreType.DMA((5,)),
         pltpu.SemaphoreType.DMA((2,)),
@@ -1152,14 +1408,14 @@
             jax.ShapeDtypeStruct((e,) + tail, jnp.float32) for e, tail in zip(experts, tails)
         ]
         + [jax.ShapeDtypeStruct((rows, width), low), jax.ShapeDtypeStruct((2, rows, 2 * width), low)],
-        in_specs=[anywhere] * 3 + [inside] * 5 + [anywhere] * 8,
+        in_specs=[anywhere] * 3 + [inside] * 6 + [anywhere] * 8,
         out_specs=[inside] * 5 + [anywhere] * 2,
         scratch_shapes=scratch,
         compiler_params=pltpu.CompilerParams(
             collective_id=2, has_side_effects=True, vmem_limit_bytes=61 << 20
         ),
     )(
-        up, down, out, factor, thin, vectors, kind, log_total,
+        up, down, out, factor, small, up_shift_sum, vectors, kind, log_total,
         queries, kv, mixed_grad, mixed_t, normed, weight, tokens, residual_grad,
     )[:6]
 
@@ -1192,8 +1448,6 @@
     stream_place = lax.axis_index("stream")
     devices = lax.axis_size("items") * stream_size
     group_type = group_kind[0]
-    own_positions = stream_place * row_count + jnp.arange(row_count, dtype=jnp.int32)
-    own_modality = layout(group_type, own_positions, row_count)[1]
     expert_pick = jnp.where(stream_place == stream_size - 1, 1, 0).astype(jnp.int32)
     share, ff_share, ff = model_width // devices, w_down.shape[1], w_up.shape[2]
     both = ("items", "stream")
@@ -1241,8 +1495,6 @@
         queries = projected[:, :model_width]
         kv = lax.all_gather(projected[:, model_width:], "stream", axis=0, tiled=True)
         mixed_low, mixed_t, log_total = attend(kind_wide, place_at, queries, kv)
-    out_shift, gain_two, shift_two = vectors[4], vectors[5], vectors[6]
-    down_shift = jnp.where(expert_pick == 0, vectors[9], vectors[10])
     up_shift_all = thin_all[:, 7:9, :ff_share].transpose(1, 0, 2).reshape(2, ff)
     kinds = vectors[11, :: stream_size * share].astype(jnp.int32)
     tally = []
@@ -1254,61 +1506,38 @@
     totals = jnp.stack(
         [jnp.sum(jnp.where(kinds == 0, tally[0][e], tally[1][e])) for e in range(2)]
     )
-    residual = tokens_f + product(mixed_low, out_weight) + out_shift
-    normed_two, pull_two = jax.vjp(layer_norm, residual, gain_two, shift_two)
-    normed_two_low = normed_two.astype(low)
-    up_weight = lax.dynamic_index_in_dim(up_all, expert_pick, 0, keepdims=False)
-    up_shift = lax.dynamic_index_in_dim(up_shift_all, expert_pick, 0, keepdims=False)
-    down_weight = lax.dynamic_index_in_dim(down_all, expert_pick, 0, keepdims=False)
-    hidden_pre = product(normed_two_low, up_weight) + up_shift.astype(jnp.float32)
-    hidden, pull_gelu = jax.vjp(gelu_exact, hidden_pre)
-    hidden_low = hidden.astype(low)
-    branch = product(hidden_low, down_weight) + down_shift
-    expert_mask = (own_modality == expert_pick).astype(jnp.float32)[:, None]
-    output = (residual + branch * expert_mask).astype(low)
-    live_rows = (own_modality < 2).astype(jnp.float32)[:, None]
-    out_grad = cotangent.astype(jnp.float32) * live_rows
-    branch_grad = (out_grad * expert_mask).astype(low)
-    grad_down = product_lead(hidden_low, branch_grad)
-    grad_down_shift = jnp.sum(branch_grad.astype(jnp.float32), axis=0)
-    hidden_grad = product_trail(branch_grad, down_weight)
-    pre_grad = pull_gelu(hidden_grad)[0].astype(low)
-    grad_up = product_lead(normed_two_low, pre_grad)
-    grad_up_shift = jnp.sum(pre_grad.astype(jnp.float32), axis=0)
-    norm_two_grad = product_trail(pre_grad, up_weight)
-    residual_part, grad_gain_two, grad_shift_two = pull_two(norm_two_grad)
-    residual_grad = out_grad + residual_part
-    residual_low = residual_grad.astype(low)
-    grad_out_weight = product_lead(mixed_low, residual_low)
-    grad_out_shift = jnp.sum(residual_low.astype(jnp.float32), axis=0)
-    mixed_grad = product_trail(residual_low, out_weight).astype(low)
+    (
+        output,
+        residual_grad,
+        grad_out_weight,
+        mixed_grad,
+        grad_up,
+        grad_down,
+        small,
+        grad_up_shift,
+    ) = feed(
+        expert_pick[None],
+        place_at,
+        kind_wide,
+        vectors,
+        up_shift_all[:, None],
+        tokens,
+        mixed_low,
+        out_weight,
+        cotangent,
+        up_all,
+        down_all,
+    )
     factor = lax.rsqrt(totals)
-    pick = (jnp.arange(2, dtype=jnp.int32) == expert_pick).astype(jnp.float32) * factor
-
-    def lanes(values):
-        values = values.reshape(values.shape[0], devices, -1).transpose(1, 0, 2)
-        return jnp.pad(values, ((0, 0), (0, 0), (0, 128 - values.shape[2])))
-
-    def thin_of(rows):
-        thin_terms = jnp.concatenate(
-            [
-                lanes(jnp.stack(rows)),
-                lanes(pick[:, None] * grad_up_shift[None]),
-                lanes(pick[:, None] * grad_down_shift[None]),
-            ],
-            axis=1,
-        )
-        return jnp.pad(thin_terms, ((0, 0), (0, THIN_ROWS - thin_terms.shape[1]), (0, 0)))
-
-    late = [grad_out_shift, grad_gain_two, grad_shift_two]
     if near:
         box = (depth, 2, 2, 2)
         up_sum, down_sum, out_sum, qkv_sum, thin_sum, token_grad = scatter_all(
-            grad_up.astype(low).reshape(box + (share, ff)),
-            grad_down.astype(low).reshape(box + (ff_share, model_width)),
-            grad_out_weight.astype(low).reshape(box + (share, model_width)),
+            grad_up.reshape(box + (share, ff)),
+            grad_down.reshape(box + (ff_share, model_width)),
+            grad_out_weight.reshape(box + (share, model_width)),
             jnp.broadcast_to(jnp.repeat(factor, 128)[None], (8, 256)),
-            thin_of([jnp.zeros_like(grad_out_shift)] * 4 + late).reshape(box + (THIN_ROWS, 128)),
+            small,
+            grad_up_shift,
             vectors,
             kind_wide,
             log_total,
@@ -1324,6 +1553,12 @@
         )
         out_sum, qkv_sum, thin_sum = out_sum[0], qkv_sum[0], thin_sum[0]
     else:
+        pick = (jnp.arange(2, dtype=jnp.int32) == expert_pick).astype(jnp.float32) * factor
+
+        def lanes(values):
+            values = values.reshape(values.shape[0], devices, -1).transpose(1, 0, 2)
+            return jnp.pad(values, ((0, 0), (0, 0), (0, 128 - values.shape[2])))
+
         scatter = functools.partial(
             lax.psum_scatter, axis_name=both, scatter_dimension=0, tiled=True
         )
@@ -1345,27 +1580,34 @@
             norm_one_grad
         )
         token_grad = (residual_grad + token_part).astype(low)
-        up_sum = wide(pick[:, None, None] * grad_up[None])
-        down_sum = wide(pick[:, None, None] * grad_down[None])
-        out_sum, qkv_sum = scatter(grad_out_weight), scatter(grad_qkv)
-        thin_sum = scatter(thin_of(grads_one + early + late))[0]
-    small = [thin_sum[k, :share] for k in range(7)]
+        up_sum = wide(pick[:, None, None] * grad_up.astype(jnp.float32)[None])
+        down_sum = wide(pick[:, None, None] * grad_down.astype(jnp.float32)[None])
+        out_sum, qkv_sum = scatter(grad_out_weight.astype(jnp.float32)), scatter(grad_qkv)
+        thin_terms = [
+            lanes(jnp.stack(grads_one + early + [small[0], small[1], small[2]])),
+            jnp.zeros((devices, 1, 128), jnp.float32),
+            lanes(pick[:, None] * small[3][None]),
+            lanes(pick[:, None] * grad_up_shift[0][None]),
+            jnp.zeros((devices, THIN_ROWS - 12, 128), jnp.float32),
+        ]
+        thin_sum = scatter(jnp.concatenate(thin_terms, axis=1))[0]
+    lines = [thin_sum[k, :share] for k in range(7)]
     return (
         output,
         token_grad,
-        small[0],
-        small[1],
+        lines[0],
+        lines[1],
         qkv_sum,
-        small[2],
-        small[3],
+        lines[2],
+        lines[3],
         out_sum,
-        small[4],
-        small[5],
-        small[6],
+        lines[4],
+        lines[5],
+        lines[6],
         up_sum,
-        thin_sum[7:9, :ff_share],
+        thin_sum[10:12, :ff_share],
         down_sum,
-        thin_sum[9:11, :share],
+        thin_sum[8:10, :share],
         totals,
     )
 

time: 427 us -> 371 us (0.87)
  the two profiles are of different devices: /device:TPU:1 before, /device:TPU:0 now
where the time goes in v4:
time: 371 us; the launch traced here: 370 us
  Pallas kernels  336 us (91%)
  local copies, waits for them, and re-layouts  24.5 us (7%)
  other arithmetic  8.22 us (2%)
    pallas_call x1, Pallas kernels, scatter_all(): pl.pallas_call(functools.partial(scatter_kernel, depth, kinds, chunks, cu...  168 us
    pallas_call x1, Pallas kernels, gather_all(): pl.pallas_call(functools.partial(gather_kernel, depth, chunks, entries),...  139 us
    pallas_call x1, Pallas kernels, feed(): pl.pallas_call(feed_kernel, out_shape=fixed + [jax.ShapeDtypeStruct((widt...  28.7 us
    unnamed x32, local copies, waits for them, and re-layouts  17.6 us

profile of v4, /device:TPU:0, one launch (start us, length us, event | category | flops | bytes accessed | tf_op | source)
XLA Modules:
  0.0 369.9 jit_solution(8576112222504140257)
XLA Ops:
  1.3 0.0 copy-start.9
  1.3 0.8 stack.40
  2.1 0.7 fusion.30
  2.8 0.0 copy-start
  2.8 1.1 copy-done
  3.9 0.0 copy-start.5
  3.9 1.0 copy-done.5
  4.9 0.0 copy-start.6
  4.9 1.0 copy-done.6
  5.9 0.0 copy-start.8
  5.9 0.9 copy-done.8
  6.8 0.0 copy-start.10
  6.8 0.8 copy-done.10
  7.5 138.8 %shard_map.279 = (bf16[4,2,2,2,16,128]{5,4,3,2,1,0:T(8,128)(2,1)S(1)}, bf16[4,2,2,2,24,768]{5,4,3,2,1,0:T(8,128)(2,1)S(1)}, bf16[2,4,2,2,2,24,3072]{6,5,4,3,2,1,...) custom-call(bf16[16,128]{1,0:T(8,128)(2,1)S(1)} %pad.24.refs_0_, ...), custom_call_target="tpu_custom_call" | custom-call | tf_op jit(solution)/shard_map/pallas_call | solution.py:887
  146.3 0.0 copy-start.1
  146.4 1.0 copy-done.1
  147.4 0.0 copy-start.2
  147.4 0.9 copy-done.2
  148.2 0.0 copy-start.3
  148.3 0.9 copy-done.3
  149.1 0.0 copy-start.4
  149.1 0.9 copy-done.4
  150.0 0.0 copy-start.7
  150.0 0.6 copy-done.7
  150.6 0.0 copy-start.11
  150.6 0.6 copy-done.11
  151.3 0.7 broadcast_in_dim_reshape.5.up_shift
  152.0 0.0 copy-done.9
  152.0 28.7 %shard_map.280 = (bf16[512,768]{1,0:T(8,128)(2,1)}, f32[512,768]{1,0:T(8,128)}, bf16[768,768]{1,0:T(8,128)(2,1)}, bf16[512,768]{1,0:T(8,128)(2,1)}, bf16[768,307...) custom-call(s32[1]{0:T(128)} %bitcast.pick, s32[1]{0:T(128)} %bitcast.1.place_ref, ...), custom_call_target="tpu_custom_call" | custom-call | tf_op jit(solution)/shard_map/pallas_call | solution.py:538
  180.7 0.8 slice.34
  181.5 0.6 convert_reduce_fusion
  182.1 0.6 convert_reduce_fusion.1
  182.8 0.6 convert_reduce_fusion.2
  183.4 0.6 convert_reduce_fusion.3
  184.0 3.2 fusion.32
  187.2 1.9 fusion.34
  189.1 0.1 broadcast_bitcast_fusion
  189.1 0.6 broadcast_in_dim.61.refs_3_
  189.7 168.3 %shard_map.281 = (f32[2,24,3072]{2,1,0:T(8,128)}, f32[2,96,768]{2,1,0:T(8,128)}, f32[1,24,768]{2,1,0:T(8,128)}, f32[1,24,2304]{2,1,0:T(8,128)}, f32[1,16,128]{2,...) custom-call(bf16[4,2,2,2,24,3072]{5,4,3,2,1,0:T(8,128)(2,1)} %bitcast.46, ...), custom_call_target="tpu_custom_call" | custom-call | tf_op jit(solution)/shard_map/pallas_call | solution.py:1405
  358.0 0.0 copy-start.12
  358.0 1.5 slice_bitcast_fusion
  359.5 1.2 slice.52
  360.7 1.2 slice.53
  362.0 2.1 copy.44
  364.0 1.6 copy.45
  365.7 1.5 copy.46
  367.2 1.9 copy.47
  369.1 0.0 copy-done.12
  369.1 0.8 copy.48
  (4 shorter events, 0.0 us)
Async XLA Ops:
  1.3 150.7 %copy-start.9 = (f32[8,128]{1,0:T(8,128)}, f32[8,128]{1,0:T(8,128)S(1)}, u32[]{:S(2)}) copy-start(f32[8,128]{1,0:T(8,128)S(1)} %broadcast_in_dim.52.refs_6_.kind.refs_7_) | copy-start | bytes 12292
  2.8 1.1 copy-start
  3.9 1.0 copy-start.5
  4.9 1.0 copy-start.6
  5.9 0.9 copy-start.8
  6.8 0.8 copy-start.10
  146.3 1.0 copy-start.1
  147.4 0.9 copy-start.2
  148.2 0.9 copy-start.3
  149.1 0.9 copy-start.4
  150.0 0.6 copy-start.7
  150.6 0.6 copy-start.11
  358.0 11.1 %copy-start.12 = (f32[2,96,768]{2,1,0:T(8,128)S(1)}, f32[2,96,768]{2,1,0:T(8,128)}, u32[]{:S(2)}) copy-start(f32[2,96,768]{2,1,0:T(8,128)} %get-tuple-element.108) | copy-start | bytes 1769476

commit v5 on v4

--- a/solution.py
+++ b/solution.py
@@ -83,11 +83,20 @@
         + [((1, None), rows, cols, order, False) for order, cols in enumerate(near_cols)],
         [((2, None), rows, cols, order, False) for order, cols in enumerate(out_cols)],
     ]
-    for e in (1, 0):
-        chunks.append([((3, e), rows, cols, order, e == 1) for order, cols in enumerate(up_cols)])
-        chunks.append(
-            [((4, e), band, (0, width), order, e == 1) for order, band in enumerate(down_rows)]
-        )
+    def up_chunk(e, parts):
+        return [((3, e), rows, cols, order, e == 1) for order, cols in enumerate(parts) if cols[1]]
+
+    def down_chunk(e, parts):
+        return [((4, e), band, (0, width), order, e == 1) for order, band in enumerate(parts)]
+
+    chunks += [up_chunk(1, up_cols), down_chunk(1, down_rows), down_chunk(0, down_rows)]
+    unit, begin = 128, 0
+    for shares in ((2, 7, 3), (1, 5, 2), (1, 2, 1)):
+        parts = []
+        for blocks in shares:
+            parts.append((begin * unit, blocks * unit))
+            begin += blocks
+        chunks.append(up_chunk(0, parts))
     return chunks
 
 
@@ -103,7 +112,7 @@
         chunks.append(
             [(1, e, band, (0, width), order) for order, band in enumerate(down_rows)]
         )
-    chunks += [[], [], [], []]
+    chunks += [[], []]
     chunks.append(
         [(3, 0, rows, cols, order) for order, cols in enumerate(near_cols)]
         + [(4, 0, (0, THIN_ROWS), (0, 128), 0)]
@@ -574,7 +583,7 @@
                 pltpu.VMEM((rows, width), wide),
             ],
         ),
-        compiler_params=pltpu.CompilerParams(vmem_limit_bytes=56 << 20),
+        compiler_params=pltpu.CompilerParams(vmem_limit_bytes=62 << 20),
     )(pick, place_at, kind, vectors, up_shift, tokens, mixed, out_weight, cotangent, up, down)
 
 
@@ -695,8 +704,9 @@
     ins = take(5)
     tokens, kind = take(2)
     thin_out, out_all, up_all, down_all = take(4)
-    qkv_weight, normed, queries, vectors, kv_out, mixed, mixed_t, log_total = take(8)
+    weight_out, normed_out, queries_out, vectors, kv_out, mixed, mixed_t_out, log_total = take(8)
     thin_all, qkv_all, kv, values_t, scaled, top, total = take(7)
+    qkv_weight, normed, queries, mixed_t = take(4)
     local_sem = next(it)
     sems, kv_sems = take(2), take(2)
     keep_sem = next(it)
@@ -778,8 +788,14 @@
     to_across = remote(kv.at[own_slot], kv.at[own_slot], kv_sems, 0, across)
     to_beside = remote(kv.at[own_slot], kv.at[own_slot], kv_sems, 1, beside)
     onward = remote(kv.at[other_slot], kv.at[other_slot], kv_sems, 2, beside)
-    keep_thin = pltpu.make_async_copy(thin_all, thin_out, keep_sem.at[0])
-    keep_kv = pltpu.make_async_copy(kv, kv_out, keep_sem.at[1])
+    keep_kv = pltpu.make_async_copy(kv, kv_out, keep_sem.at[0])
+    keep_mixed = pltpu.make_async_copy(mixed_t, mixed_t_out, keep_sem.at[1])
+    keep_early = [
+        pltpu.make_async_copy(src, dst, keep_sem.at[2 + j])
+        for j, (src, dst) in enumerate(
+            [(thin_all, thin_out), (qkv_weight, weight_out), (normed, normed_out), (queries, queries_out)]
+        )
+    ]
 
     def project():
         spots = spots_of(depth)
@@ -821,7 +837,8 @@
             if part == 2:
                 to_across.start()
                 to_beside.start()
-                keep_thin.start()
+        for copy in keep_early:
+            copy.start()
         scale_queries(queries, scaled)
 
     def pass_on():
@@ -866,8 +883,9 @@
     flow.tick(STEPS + len(chunks))
     for copy in (to_beside, to_across, onward):
         copy.wait_send()
-    keep_thin.wait()
-    keep_kv.wait()
+    keep_mixed.start()
+    for copy in keep_early + [keep_kv, keep_mixed]:
+        copy.wait()
     for chunk in chunks:
         for step in range(STEPS):
             each(chunk, step, 1, lambda copy: copy.wait_send())
@@ -900,8 +918,8 @@
             jax.ShapeDtypeStruct((width, rows), jnp.float32),
             jax.ShapeDtypeStruct((lines, rows), jnp.float32),
         ],
-        in_specs=[anywhere] * 5 + [inside] * 2,
-        out_specs=[anywhere] * 4 + [inside] * 4 + [anywhere] + [inside] * 3,
+        in_specs=[inside] * 7,
+        out_specs=[anywhere] * 7 + [inside, anywhere, inside, anywhere, inside],
         scratch_shapes=[
             pltpu.VMEM(box + thin.shape, low),
             pltpu.VMEM(box + (share, 3 * width), low),
@@ -910,17 +928,26 @@
             pltpu.VMEM((heads, PAIR, rows), low),
             pltpu.VMEM((lines, TQ), jnp.float32),
             pltpu.VMEM((lines, TQ), jnp.float32),
+            pltpu.VMEM((width, 3 * width), low),
+            pltpu.VMEM((rows, width), low),
+            pltpu.VMEM((rows, width), low),
+            pltpu.VMEM((width, rows), jnp.float32),
             pltpu.SemaphoreType.DMA((len(entries),)),
             pltpu.SemaphoreType.DMA((n_pieces, depth + 3)),
             pltpu.SemaphoreType.DMA((n_pieces, depth + 3)),
             pltpu.SemaphoreType.DMA((3,)),
             pltpu.SemaphoreType.DMA((3,)),
-            pltpu.SemaphoreType.DMA((2,)),
+            pltpu.SemaphoreType.DMA((6,)),
         ],
         compiler_params=pltpu.CompilerParams(
-            collective_id=1, has_side_effects=True, vmem_limit_bytes=48 << 20
+            collective_id=1, has_side_effects=True, vmem_limit_bytes=62 << 20
         ),
     )(thin, w_qkv, w_out, w_up, w_down, tokens, kind)
+
+
+def rows_of_kind(kind, rows):
+    patch_len, members = ((PATCH_S, ITEMS_S), (PATCH_L, ITEMS_L))[kind]
+    return float(min(patch_len * members, 3 * rows)), float(min(TEXT_LEN * members, rows))
 
 
 def scatter_kernel(depth, kinds, chunks, cuts, *refs):
@@ -928,7 +955,7 @@
     it = iter(refs)
     take = lambda count: [next(it) for _ in range(count)]
     far = take(n_far)
-    factor, small, up_shift_sum, vectors, kind, log_total = take(6)
+    small, up_shift_sum, vectors, kind, log_total = take(5)
     queries, kv, mixed_grad, mixed_t, normed, weight, tokens, residual_grad = take(8)
     outs = take(n)
     token_grad, kv_away = take(2)
@@ -945,6 +972,17 @@
     at = coords()
     z, x, y, c = (at[d] for d in "zxyc")
     ins = far + [qkv_terms, thin_terms]
+    groups = devices // 4
+    lane = lax.broadcasted_iota(jnp.int32, (1, width), 1)
+    marks = functools.reduce(
+        jnp.logical_or, [lane == group * (width // groups) for group in range(groups)]
+    )
+    second_kind = jnp.sum(jnp.where(marks, vectors[11:12, :], 0.0), axis=1, keepdims=True)
+    counts = [
+        first_count * (groups - second_kind) + second_count * second_kind
+        for first_count, second_count in zip(*(rows_of_kind(kind_of, rows) for kind_of in range(2)))
+    ]
+    factors = [lax.rsqrt(count) for count in counts]
     local = [
         pltpu.make_async_copy(far[k].at[EVERY, EVERY, EVERY, c], own_half[k], local_sem.at[k])
         for k in range(n_far)
@@ -1093,7 +1131,7 @@
 
             def finish(total):
                 if kinds[k]:
-                    total = total * factor[0:1, e * 128 : e * 128 + 1]
+                    total = total * factors[e]
                 outs[k][(e,) + box] = total
 
             def own():
@@ -1235,7 +1273,7 @@
             return jnp.concatenate(parts + [jnp.zeros((8 - count, parts[0].shape[1]), jnp.float32)])
 
         scales = [
-            jnp.where(text_device == (e == 1), factor[0:1, e * 128 : e * 128 + 1], 0.0)
+            jnp.where(text_device == (e == 1), factors[e], 0.0)
             for e in range(2)
         ]
         down_part = [small[3:4, :] * scale for scale in scales]
@@ -1342,7 +1380,6 @@
         return scope
 
     flow = Pipeline(chunks, 2, start, wait)
-    flow.tick(2)
     attention(0)()
     flow.tick()
     attention(1)()
@@ -1351,6 +1388,10 @@
     flow.tick()
     project_scope()
     flow.tick(STEPS + len(chunks))
+    lane = lax.broadcasted_iota(jnp.int32, (1, 128), 1)
+    outs[4][0, THIN_ROWS - 1 : THIN_ROWS, :] = jnp.where(
+        lane == 0, counts[0], jnp.where(lane == 1, counts[1], 0.0)
+    )
     for copy in (kv_beside, kv_across):
         copy.wait_send()
     for chunk in chunks:
@@ -1361,7 +1402,7 @@
 
 
 def scatter_all(
-    up, down, out, factor, small, up_shift_sum, vectors, kind, log_total,
+    up, down, out, small, up_shift_sum, vectors, kind, log_total,
     queries, kv, mixed_grad, mixed_t, normed, weight, tokens, residual_grad, depth,
 ):
     rows, width = tokens.shape
@@ -1408,16 +1449,33 @@
             jax.ShapeDtypeStruct((e,) + tail, jnp.float32) for e, tail in zip(experts, tails)
         ]
         + [jax.ShapeDtypeStruct((rows, width), low), jax.ShapeDtypeStruct((2, rows, 2 * width), low)],
-        in_specs=[anywhere] * 3 + [inside] * 6 + [anywhere] * 8,
+        in_specs=[anywhere] * 3 + [inside] * 5 + [anywhere] * 8,
         out_specs=[inside] * 5 + [anywhere] * 2,
         scratch_shapes=scratch,
         compiler_params=pltpu.CompilerParams(
             collective_id=2, has_side_effects=True, vmem_limit_bytes=61 << 20
         ),
     )(
-        up, down, out, factor, small, up_shift_sum, vectors, kind, log_total,
+        up, down, out, small, up_shift_sum, vectors, kind, log_total,
         queries, kv, mixed_grad, mixed_t, normed, weight, tokens, residual_grad,
     )[:6]
+
+
+def publish_kernel(*refs):
+    count = len(refs) // 2
+    for src, dst in zip(refs[:count], refs[count:]):
+        dst[...] = src[...]
+
+
+def publish(arrays):
+    inside = pl.BlockSpec(memory_space=pltpu.VMEM)
+    return pl.pallas_call(
+        publish_kernel,
+        out_shape=[jax.ShapeDtypeStruct(array.shape, array.dtype) for array in arrays],
+        in_specs=[inside] * len(arrays),
+        out_specs=[inside] * len(arrays),
+        compiler_params=pltpu.CompilerParams(vmem_limit_bytes=32 << 20),
+    )(*arrays)
 
 
 def padded(values):
@@ -1496,16 +1554,6 @@
         kv = lax.all_gather(projected[:, model_width:], "stream", axis=0, tiled=True)
         mixed_low, mixed_t, log_total = attend(kind_wide, place_at, queries, kv)
     up_shift_all = thin_all[:, 7:9, :ff_share].transpose(1, 0, 2).reshape(2, ff)
-    kinds = vectors[11, :: stream_size * share].astype(jnp.int32)
-    tally = []
-    for kind in range(2):
-        modality = layout(
-            jnp.int32(kind), jnp.arange(stream_size * row_count, dtype=jnp.int32), row_count
-        )[1]
-        tally.append([jnp.sum((modality == e).astype(jnp.float32)) for e in range(2)])
-    totals = jnp.stack(
-        [jnp.sum(jnp.where(kinds == 0, tally[0][e], tally[1][e])) for e in range(2)]
-    )
     (
         output,
         residual_grad,
@@ -1528,14 +1576,12 @@
         up_all,
         down_all,
     )
-    factor = lax.rsqrt(totals)
     if near:
         box = (depth, 2, 2, 2)
         up_sum, down_sum, out_sum, qkv_sum, thin_sum, token_grad = scatter_all(
             grad_up.reshape(box + (share, ff)),
             grad_down.reshape(box + (ff_share, model_width)),
             grad_out_weight.reshape(box + (share, model_width)),
-            jnp.broadcast_to(jnp.repeat(factor, 128)[None], (8, 256)),
             small,
             grad_up_shift,
             vectors,
@@ -1551,8 +1597,23 @@
             residual_grad,
             depth,
         )
-        out_sum, qkv_sum, thin_sum = out_sum[0], qkv_sum[0], thin_sum[0]
+        thin_sum = thin_sum[0]
+        totals = thin_sum[THIN_ROWS - 1, :2]
+        up_sum, down_sum, out_sum, qkv_sum, token_grad = publish(
+            [up_sum, down_sum, out_sum[0], qkv_sum[0], token_grad]
+        )
     else:
+        kinds = vectors[11, :: stream_size * share].astype(jnp.int32)
+        tally = []
+        for kind in range(2):
+            modality = layout(
+                jnp.int32(kind), jnp.arange(stream_size * row_count, dtype=jnp.int32), row_count
+            )[1]
+            tally.append([jnp.sum((modality == e).astype(jnp.float32)) for e in range(2)])
+        totals = jnp.stack(
+            [jnp.sum(jnp.where(kinds == 0, tally[0][e], tally[1][e])) for e in range(2)]
+        )
+        factor = lax.rsqrt(totals)
         pick = (jnp.arange(2, dtype=jnp.int32) == expert_pick).astype(jnp.float32) * factor
 
         def lanes(values):

time: 371 us -> 349 us (0.941)
  local copies, waits for them, and re-layouts: 24.5 us -> 13.8 us
  other arithmetic: 8.22 us -> 0.68 us
  Pallas kernels: 336 us -> 329 us
    unnamed x32 -> x11, local copies, waits for them, and re-layouts: 17.6 us -> 5.08 us
    pallas_call x1, Pallas kernels: 168 us -> 160 us  [scatter_all(): pl.pallas_call(functools.partial(scatter_kernel, depth, kinds, chunks, cu...]
    reduce_sum x5 -> x0, other arithmetic: 5.66 us -> none  [the longest x1 3.19 us: body(): jnp.sum(jnp.where(kinds == 0, tally[0][e], tally[1][e]))]
where the time goes in v5:
time: 349 us; the launch traced here: 345 us
  Pallas kernels  329 us (94%)
  local copies, waits for them, and re-layouts  13.8 us (4%)
    pallas_call x1, Pallas kernels, scatter_all(): pl.pallas_call(functools.partial(scatter_kernel, depth, kinds, chunks, cu...  160 us
    pallas_call x1, Pallas kernels, gather_all(): pl.pallas_call(functools.partial(gather_kernel, depth, chunks, entries),...  139 us
    pallas_call x1, Pallas kernels, feed(): pl.pallas_call(feed_kernel, out_shape=fixed + [jax.ShapeDtypeStruct((widt...  28.7 us

profile of v5, /device:TPU:0, one launch (start us, length us, event | category | flops | bytes accessed | tf_op | source)
XLA Modules:
  0.0 345.0 jit_solution(15486896501160145681)
XLA Ops:
  1.3 0.8 stack.31
  2.1 0.7 fusion.7
  2.8 0.6 pad.24.refs_0_
  3.4 0.6 broadcast_in_dim.14.refs_6_.kind
  4.0 138.5 %shard_map.279 = (bf16[4,2,2,2,16,128]{5,4,3,2,1,0:T(8,128)(2,1)}, bf16[4,2,2,2,24,768]{5,4,3,2,1,0:T(8,128)(2,1)}, bf16[2,4,2,2,2,24,3072]{6,5,4,3,2,1,0:T(8,12...) custom-call(bf16[16,128]{1,0:T(8,128)(2,1)} %pad.24.refs_0_, ...), custom_call_target="tpu_custom_call" | custom-call | tf_op jit(solution)/shard_map/pallas_call | solution.py:905
  142.5 0.9 slice.44
  143.5 0.7 broadcast_in_dim_reshape.4.up_shift
  144.2 28.7 %shard_map.280 = (bf16[512,768]{1,0:T(8,128)(2,1)}, f32[512,768]{1,0:T(8,128)}, bf16[768,768]{1,0:T(8,128)(2,1)}, bf16[512,768]{1,0:T(8,128)(2,1)}, bf16[768,307...) custom-call(s32[1]{0:T(128)} %bitcast.pick, s32[1]{0:T(128)} %bitcast.1.place_ref, ...), custom_call_target="tpu_custom_call" | custom-call | tf_op jit(solution)/shard_map/pallas_call | solution.py:547
  172.8 160.4 %shard_map.281 = (f32[2,24,3072]{2,1,0:T(8,128)}, f32[2,96,768]{2,1,0:T(8,128)}, f32[1,24,768]{2,1,0:T(8,128)}, f32[1,24,2304]{2,1,0:T(8,128)}, f32[1,16,128]{2,...) custom-call(bf16[4,2,2,2,24,3072]{5,4,3,2,1,0:T(8,128)(2,1)} %bitcast.44, ...), custom_call_target="tpu_custom_call" | custom-call | tf_op jit(solution)/shard_map/pallas_call | solution.py:1446
  333.2 0.0 copy-start
  333.3 1.1 copy-done
  334.4 0.0 copy-start.1
  334.4 1.1 copy-done.1
  335.4 0.0 copy-start.2
  335.4 1.1 copy-done.2
  336.5 0.0 copy-start.3
  336.5 0.9 copy-done.3
  337.4 0.0 copy-start.4
  337.4 0.9 copy-done.4
  338.3 1.5 shard_map.282
  339.8 1.2 slice_bitcast_fusion
  341.0 1.2 slice.52
  342.3 1.2 slice.53
  343.5 1.5 slice_bitcast_fusion.1
  (1 shorter events, 0.0 us)
Async XLA Ops:
  333.2 1.1 copy-start
  334.4 1.1 copy-start.1
  335.4 1.1 copy-start.2
  336.5 0.9 copy-start.3
  337.4 0.9 copy-start.4

commit v6 on v5

--- a/solution.py
+++ b/solution.py
@@ -112,11 +112,11 @@
         chunks.append(
             [(1, e, band, (0, width), order) for order, band in enumerate(down_rows)]
         )
-    chunks += [[], []]
+    chunks.append([])
     chunks.append(
         [(3, 0, rows, cols, order) for order, cols in enumerate(near_cols)]
-        + [(4, 0, (0, THIN_ROWS), (0, 128), 0)]
-    )
+    )
+    chunks.append([(4, 0, (0, THIN_ROWS), (0, 128), 0)])
     cuts = (
         (0, up_cols[2][0]),
         (down_rows[2][0], 0),
@@ -705,8 +705,9 @@
     tokens, kind = take(2)
     thin_out, out_all, up_all, down_all = take(4)
     weight_out, normed_out, queries_out, vectors, kv_out, mixed, mixed_t_out, log_total = take(8)
+    (far_normed_out,) = take(1)
     thin_all, qkv_all, kv, values_t, scaled, top, total = take(7)
-    qkv_weight, normed, queries, mixed_t = take(4)
+    qkv_weight, normed, queries, mixed_t, far_tokens, far_normed = take(6)
     local_sem = next(it)
     sems, kv_sems = take(2), take(2)
     keep_sem = next(it)
@@ -785,15 +786,22 @@
     other = across["y"] * 2 + across["c"]
     own_slot = pl.ds(pl.multiple_of(slot * rows, rows), rows)
     other_slot = pl.ds(pl.multiple_of(other * rows, rows), rows)
-    to_across = remote(kv.at[own_slot], kv.at[own_slot], kv_sems, 0, across)
+    to_across = remote(tokens, far_tokens, kv_sems, 0, across)
     to_beside = remote(kv.at[own_slot], kv.at[own_slot], kv_sems, 1, beside)
     onward = remote(kv.at[other_slot], kv.at[other_slot], kv_sems, 2, beside)
+    to_across.start()
     keep_kv = pltpu.make_async_copy(kv, kv_out, keep_sem.at[0])
     keep_mixed = pltpu.make_async_copy(mixed_t, mixed_t_out, keep_sem.at[1])
     keep_early = [
         pltpu.make_async_copy(src, dst, keep_sem.at[2 + j])
         for j, (src, dst) in enumerate(
-            [(thin_all, thin_out), (qkv_weight, weight_out), (normed, normed_out), (queries, queries_out)]
+            [
+                (thin_all, thin_out),
+                (qkv_weight, weight_out),
+                (normed, normed_out),
+                (far_normed, far_normed_out),
+                (queries, queries_out),
+            ]
         )
     ]
 
@@ -804,15 +812,18 @@
         thin = jnp.concatenate([thin_all[spot] for spot in spots], axis=0)
         vectors[...] = spread(thin, share, width)
 
-        @pl.loop(0, rows // 128)
-        def _(j):
-            block = pl.ds(pl.multiple_of(j * 128, 128), 128)
-            value = tokens[block, :].astype(jnp.float32)
-            centred = value - jnp.mean(value, axis=-1, keepdims=True)
-            scale = lax.rsqrt(jnp.mean(centred * centred, axis=-1, keepdims=True) + NORM_EPS)
-            normed[block, :] = (centred * scale * vectors[0:1, :] + vectors[1:2, :]).astype(
-                jnp.bfloat16
-            )
+        to_across.wait_recv()
+        for given, made in ((tokens, normed), (far_tokens, far_normed)):
+
+            @pl.loop(0, rows // 128)
+            def _(j, given=given, made=made):
+                block = pl.ds(pl.multiple_of(j * 128, 128), 128)
+                value = given[block, :].astype(jnp.float32)
+                centred = value - jnp.mean(value, axis=-1, keepdims=True)
+                scale = lax.rsqrt(jnp.mean(centred * centred, axis=-1, keepdims=True) + NORM_EPS)
+                made[block, :] = (centred * scale * vectors[0:1, :] + vectors[1:2, :]).astype(
+                    jnp.bfloat16
+                )
 
         step = width // 2
         for part in (1, 2, 0):
@@ -820,30 +831,23 @@
             @pl.loop(0, 2)
             def _(j, part=part):
                 cols = pl.ds(pl.multiple_of(j * step, 128), step)
-                value = jnp.dot(
-                    normed[...],
-                    qkv_weight[:, pl.ds(pl.multiple_of(part * width + j * step, 128), step)],
-                    preferred_element_type=jnp.float32,
-                )
+                weight_cols = qkv_weight[:, pl.ds(pl.multiple_of(part * width + j * step, 128), step)]
+                value = jnp.dot(normed[...], weight_cols, preferred_element_type=jnp.float32)
                 if part == 0:
                     queries[:, cols] = (value + vectors[2:3, cols]).astype(jnp.bfloat16)
-                elif part == 1:
-                    kv[own_slot, cols] = value.astype(jnp.bfloat16)
-                else:
-                    kv[own_slot, pl.ds(pl.multiple_of(width + j * step, 128), step)] = (
-                        value + vectors[3:4, cols]
-                    ).astype(jnp.bfloat16)
+                    return
+                far_value = jnp.dot(far_normed[...], weight_cols, preferred_element_type=jnp.float32)
+                to = pl.ds(pl.multiple_of((part - 1) * width + j * step, 128), step)
+                shift = vectors[3:4, cols] if part == 2 else 0.0
+                kv[own_slot, to] = (value + shift).astype(jnp.bfloat16)
+                kv[other_slot, to] = (far_value + shift).astype(jnp.bfloat16)
 
             if part == 2:
-                to_across.start()
                 to_beside.start()
+                onward.start()
         for copy in keep_early:
             copy.start()
         scale_queries(queries, scaled)
-
-    def pass_on():
-        to_across.wait_recv()
-        onward.start()
 
     def attend_first():
         to_beside.wait_recv()
@@ -870,8 +874,6 @@
     )
     flow.tick(5)
     project()
-    flow.tick()
-    pass_on()
     flow.tick()
     attention(0, 0, everyone // 2)()
     flow.tick()
@@ -917,9 +919,10 @@
             jax.ShapeDtypeStruct((rows, width), low),
             jax.ShapeDtypeStruct((width, rows), jnp.float32),
             jax.ShapeDtypeStruct((lines, rows), jnp.float32),
+            jax.ShapeDtypeStruct((rows, width), low),
         ],
         in_specs=[inside] * 7,
-        out_specs=[anywhere] * 7 + [inside, anywhere, inside, anywhere, inside],
+        out_specs=[anywhere] * 7 + [inside, anywhere, inside, anywhere, inside, anywhere],
         scratch_shapes=[
             pltpu.VMEM(box + thin.shape, low),
             pltpu.VMEM(box + (share, 3 * width), low),
@@ -932,12 +935,14 @@
             pltpu.VMEM((rows, width), low),
             pltpu.VMEM((rows, width), low),
             pltpu.VMEM((width, rows), jnp.float32),
+            pltpu.VMEM((rows, width), low),
+            pltpu.VMEM((rows, width), low),
             pltpu.SemaphoreType.DMA((len(entries),)),
             pltpu.SemaphoreType.DMA((n_pieces, depth + 3)),
             pltpu.SemaphoreType.DMA((n_pieces, depth + 3)),
             pltpu.SemaphoreType.DMA((3,)),
             pltpu.SemaphoreType.DMA((3,)),
-            pltpu.SemaphoreType.DMA((6,)),
+            pltpu.SemaphoreType.DMA((7,)),
         ],
         compiler_params=pltpu.CompilerParams(
             collective_id=1, has_side_effects=True, vmem_limit_bytes=62 << 20
@@ -956,13 +961,13 @@
     take = lambda count: [next(it) for _ in range(count)]
     far = take(n_far)
     small, up_shift_sum, vectors, kind, log_total = take(5)
-    queries, kv, mixed_grad, mixed_t, normed, weight, tokens, residual_grad = take(8)
+    queries, kv, mixed_grad, mixed_t, normed, far_normed, weight, tokens, residual_grad = take(9)
     outs = take(n)
     token_grad, kv_away = take(2)
     acc, first, second, last = take(n), take(n), take(n), take(n)
     relay, z_relay, z_first, z_second, z_last = (take(n) for _ in range(5))
     own_half = take(n_far)
-    qkv_terms, thin_terms, kv_sum, kv_got, kv_mine, dq = take(6)
+    qkv_terms, thin_terms, kv_sum, far_terms, far_got, kv_mine, dq = take(7)
     sems = take(2)
     local_sem, away_sem = take(2)
     kv_sems = take(2)
@@ -994,7 +999,7 @@
         copy.wait()
     beside, across = moved(at, "c", 1, depth), moved(at, "y", 1, depth)
     kv_beside = remote(kv_away, kv_sum, kv_sems, 0, beside)
-    kv_across = remote(kv_sum.at[1 - y], kv_got, kv_sems, 1, across)
+    kv_across = remote(far_terms, far_got, kv_sems, 1, across)
     lower, upper = y == 0, y == 1
     text_device = jnp.logical_and(upper, c == 1)
     image_device = jnp.logical_or(lower, c == 0)
@@ -1209,47 +1214,68 @@
             for level in range(2):
                 kv_sum[level, block, :] = kv_sum[level, block, :] + kv_mine[level, block, :]
 
-        kv_across.start()
-
-    def project_back(qkv_grad, flipped, normed_in, weight_in, tokens_in, residual_in, token_out):
-        pairs = [(normed, normed_in), (weight, weight_in), (tokens, tokens_in), (residual_grad, residual_in)]
+    def project_back(qkv_grad, flipped, normed_in, far_in, weight_in, tokens_in, residual_in, token_out):
+        pairs = [
+            (weight, weight_in),
+            (normed, normed_in),
+            (far_normed, far_in),
+            (tokens, tokens_in),
+            (residual_grad, residual_in),
+        ]
         loads = [pltpu.make_async_copy(src, dst, away_sem.at[j]) for j, (src, dst) in enumerate(pairs)]
         for copy in loads:
             copy.start()
+        halve()
+        qkv_grad[:rows, :width] = dq[...]
+        qkv_grad[:rows, width:] = kv_sum[y]
+        qkv_grad[rows:, width:] = kv_sum[1 - y]
         for copy in loads:
             copy.wait()
-        flipped[...] = normed_in[...].T
-        qkv_grad[:, :width] = dq[...]
-        kv_across.wait_recv()
+
+        @pl.loop(0, rows // 128)
+        def _(j):
+            block = pl.ds(pl.multiple_of(j * 128, 128), 128)
+            below = pl.ds(pl.multiple_of(rows + j * 128, 128), 128)
+            far_terms[block, :] = product_trail(
+                qkv_grad[below, width:], weight_in[:, width:]
+            ).astype(jnp.bfloat16)
+
+        kv_across.start()
+        flipped[:, :rows] = normed_in[...].T
+        flipped[:, rows:] = far_in[...].T
 
         def fold(value):
             return jnp.sum(value.reshape(-1, 8, width), axis=0)
 
         zero = jnp.zeros((8, width), jnp.float32)
 
-        def join(j, carry):
+        def gather_sums(j, carry):
             block = pl.ds(pl.multiple_of(j * 64, 64), 64)
-            total = (
-                kv_sum[y, block, :].astype(jnp.float32) + kv_got[block, :].astype(jnp.float32)
-            ).astype(jnp.bfloat16)
-            qkv_grad[block, width:] = total
+            below = pl.ds(pl.multiple_of(rows + j * 64, 64), 64)
+            own, far_part = qkv_grad[block, 2 * width :], qkv_grad[below, 2 * width :]
             return (
                 carry[0] + fold(dq[block, :].astype(jnp.float32)),
-                carry[1] + fold(total[:, width:].astype(jnp.float32)),
+                carry[1] + fold(own.astype(jnp.float32) + far_part.astype(jnp.float32)),
             )
 
-        sum_q, sum_v = lax.fori_loop(0, rows // 64, join, (zero, zero))
+        sum_q, sum_v = lax.fori_loop(0, rows // 64, gather_sums, (zero, zero))
         step = width // 2
         spots = spots_of(depth)
-
-        @pl.loop(0, 6)
-        def _(j):
-            cols = pl.ds(pl.multiple_of(j * step, 128), step)
-            value = jnp.dot(
-                flipped[...], qkv_grad[:, cols], preferred_element_type=jnp.float32
-            ).astype(jnp.bfloat16)
-            for index, spot in enumerate(spots):
-                qkv_terms[spot + (EVERY, cols)] = value[index * share : (index + 1) * share]
+        for begin, count, depth_rows in ((0, 2, rows), (2, 4, 2 * rows)):
+
+            @pl.loop(begin, begin + count)
+            def _(j, depth_rows=depth_rows):
+                cols = pl.ds(pl.multiple_of(j * step, 128), step)
+                value = jnp.dot(
+                    flipped[:, :depth_rows],
+                    qkv_grad[:depth_rows, cols],
+                    preferred_element_type=jnp.float32,
+                ).astype(jnp.bfloat16)
+                for index, spot in enumerate(spots):
+                    qkv_terms[spot + (EVERY, cols)] = value[index * share : (index + 1) * share]
+
+        flow.tick()
+        kv_across.wait_recv()
 
         def back(j, carry):
             block = pl.ds(pl.multiple_of(j * 128, 128), 128)
@@ -1257,7 +1283,9 @@
             centred = value - jnp.mean(value, axis=-1, keepdims=True)
             scale = lax.rsqrt(jnp.mean(centred * centred, axis=-1, keepdims=True) + NORM_EPS)
             unit = centred * scale
-            grad = product_trail(qkv_grad[block, :], weight_in[...])
+            grad = product_trail(qkv_grad[block, :], weight_in[...]) + far_got[block, :].astype(
+                jnp.float32
+            )
             lifted = grad * vectors[0:1, :]
             inner = jnp.mean(lifted * unit, axis=-1, keepdims=True)
             part = scale * (lifted - jnp.mean(lifted, axis=-1, keepdims=True) - unit * inner)
@@ -1292,8 +1320,9 @@
         low = jnp.bfloat16
         pl.run_scoped(
             project_back,
-            pltpu.VMEM((rows, 3 * width), low),
-            pltpu.VMEM((width, rows), low),
+            pltpu.VMEM((2 * rows, 3 * width), low),
+            pltpu.VMEM((width, 2 * rows), low),
+            pltpu.VMEM((rows, width), low),
             pltpu.VMEM((rows, width), low),
             pltpu.VMEM((width, 3 * width), low),
             pltpu.VMEM((rows, width), low),
@@ -1384,8 +1413,6 @@
     flow.tick()
     attention(1)()
     flow.tick()
-    halve()
-    flow.tick()
     project_scope()
     flow.tick(STEPS + len(chunks))
     lane = lax.broadcasted_iota(jnp.int32, (1, 128), 1)
@@ -1403,7 +1430,7 @@
 
 def scatter_all(
     up, down, out, small, up_shift_sum, vectors, kind, log_total,
-    queries, kv, mixed_grad, mixed_t, normed, weight, tokens, residual_grad, depth,
+    queries, kv, mixed_grad, mixed_t, normed, far_normed, weight, tokens, residual_grad, depth,
 ):
     rows, width = tokens.shape
     far = [up, down, out]
@@ -1433,7 +1460,8 @@
         pltpu.VMEM(box + (share, 3 * width), low),
         pltpu.VMEM(box + (THIN_ROWS, 128), jnp.float32),
         pltpu.VMEM((2, rows, 2 * width), low),
-        pltpu.VMEM((rows, 2 * width), low),
+        pltpu.VMEM((rows, width), low),
+        pltpu.VMEM((rows, width), low),
         pltpu.VMEM((2, rows, 2 * width), low),
         pltpu.VMEM((rows, width), low),
         pltpu.SemaphoreType.DMA((n_pieces, depth + 3)),
@@ -1449,7 +1477,7 @@
             jax.ShapeDtypeStruct((e,) + tail, jnp.float32) for e, tail in zip(experts, tails)
         ]
         + [jax.ShapeDtypeStruct((rows, width), low), jax.ShapeDtypeStruct((2, rows, 2 * width), low)],
-        in_specs=[anywhere] * 3 + [inside] * 5 + [anywhere] * 8,
+        in_specs=[anywhere] * 3 + [inside] * 5 + [anywhere] * 9,
         out_specs=[inside] * 5 + [anywhere] * 2,
         scratch_shapes=scratch,
         compiler_params=pltpu.CompilerParams(
@@ -1457,25 +1485,44 @@
         ),
     )(
         up, down, out, small, up_shift_sum, vectors, kind, log_total,
-        queries, kv, mixed_grad, mixed_t, normed, weight, tokens, residual_grad,
+        queries, kv, mixed_grad, mixed_t, normed, far_normed, weight, tokens, residual_grad,
     )[:6]
 
 
-def publish_kernel(*refs):
-    count = len(refs) // 2
-    for src, dst in zip(refs[:count], refs[count:]):
-        dst[...] = src[...]
-
-
-def publish(arrays):
-    inside = pl.BlockSpec(memory_space=pltpu.VMEM)
+def publish_kernel(count, share, ff_share, *refs):
+    far, thin = refs[:count], refs[count]
+    outs, smalls = refs[count + 1 : 2 * count + 1], refs[2 * count + 1 : 2 * count + 11]
+    held, sems = refs[2 * count + 11 : 3 * count + 11], refs[-1]
+    inward = [pltpu.make_async_copy(far[j], held[j], sems.at[0, j]) for j in range(count)]
+    outward = [pltpu.make_async_copy(held[j], outs[j], sems.at[1, j]) for j in range(count)]
+    for copy in inward:
+        copy.start()
+    for j in range(7):
+        smalls[j][...] = thin[j, :share]
+    smalls[7][...] = thin[10:12, :ff_share]
+    smalls[8][...] = thin[8:10, :share]
+    smalls[9][...] = thin[THIN_ROWS - 1, :2]
+    for first, second in zip(inward, outward):
+        first.wait()
+        second.start()
+    for copy in outward:
+        copy.wait()
+
+
+def publish(arrays, thin, share, ff_share):
+    anywhere, inside = pl.BlockSpec(memory_space=pl.ANY), pl.BlockSpec(memory_space=pltpu.VMEM)
+    count = len(arrays)
+    small = [(share,)] * 7 + [(2, ff_share), (2, share), (2,)]
     return pl.pallas_call(
-        publish_kernel,
-        out_shape=[jax.ShapeDtypeStruct(array.shape, array.dtype) for array in arrays],
-        in_specs=[inside] * len(arrays),
-        out_specs=[inside] * len(arrays),
-        compiler_params=pltpu.CompilerParams(vmem_limit_bytes=32 << 20),
-    )(*arrays)
+        functools.partial(publish_kernel, count, share, ff_share),
+        out_shape=[jax.ShapeDtypeStruct(array.shape, array.dtype) for array in arrays]
+        + [jax.ShapeDtypeStruct(shape, jnp.float32) for shape in small],
+        in_specs=[anywhere] * count + [inside],
+        out_specs=[anywhere] * count + [inside] * len(small),
+        scratch_shapes=[pltpu.VMEM(array.shape, array.dtype) for array in arrays]
+        + [pltpu.SemaphoreType.DMA((2, count))],
+        compiler_params=pltpu.CompilerParams(vmem_limit_bytes=62 << 20),
+    )(*arrays, thin)
 
 
 def padded(values):
@@ -1533,6 +1580,7 @@
             mixed_low,
             mixed_t,
             log_total,
+            far_normed,
         ) = gather_all(thin, w_qkv, w_out, w_up, w_down, tokens, kind_wide, depth)
         thin_all = thin_all.reshape(devices, THIN_ROWS, 128)
         out_weight = out_weight.reshape(model_width, model_width)
@@ -1592,15 +1640,25 @@
             mixed_grad,
             mixed_t,
             normed_low,
+            far_normed,
             qkv_weight,
             tokens,
             residual_grad,
             depth,
         )
         thin_sum = thin_sum[0]
-        totals = thin_sum[THIN_ROWS - 1, :2]
-        up_sum, down_sum, out_sum, qkv_sum, token_grad = publish(
-            [up_sum, down_sum, out_sum[0], qkv_sum[0], token_grad]
+        (
+            up_sum,
+            down_sum,
+            out_sum,
+            qkv_sum,
+            token_grad,
+            *lines,
+            up_shift_sum,
+            down_shift_sum,
+            totals,
+        ) = publish(
+            [up_sum, down_sum, out_sum[0], qkv_sum[0], token_grad], thin_sum, share, ff_share
         )
     else:
         kinds = vectors[11, :: stream_size * share].astype(jnp.int32)
@@ -1652,7 +1710,8 @@
             jnp.zeros((devices, THIN_ROWS - 12, 128), jnp.float32),
         ]
         thin_sum = scatter(jnp.concatenate(thin_terms, axis=1))[0]
-    lines = [thin_sum[k, :share] for k in range(7)]
+        lines = [thin_sum[k, :share] for k in range(7)]
+        up_shift_sum, down_shift_sum = thin_sum[10:12, :ff_share], thin_sum[8:10, :share]
     return (
         output,
         token_grad,
@@ -1666,9 +1725,9 @@
         lines[5],
         lines[6],
         up_sum,
-        thin_sum[10:12, :ff_share],
+        up_shift_sum,
         down_sum,
-        thin_sum[8:10, :share],
+        down_shift_sum,
         totals,
     )
 

time: 349 us -> 304 us (0.87)
  Pallas kernels: 329 us -> 294 us
  local copies, waits for them, and re-layouts: 13.8 us -> 3.62 us
    pallas_call x1, Pallas kernels: 160 us -> 137 us  [scatter_all(): pl.pallas_call(functools.partial(scatter_kernel, depth, kinds, chunks, cu...]
    pallas_call x1, Pallas kernels: 139 us -> 125 us  [gather_all(): pl.pallas_call(functools.partial(gather_kernel, depth, chunks, entries),...]
    unnamed x11 -> x1, local copies, waits for them, and re-layouts: 5.08 us -> 0.01 us
where the time goes in v6:
time: 304 us; the launch traced here: 300 us
  Pallas kernels  294 us (97%)
  local copies, waits for them, and re-layouts  3.62 us (1%)
    pallas_call x1, Pallas kernels, scatter_all(): pl.pallas_call(functools.partial(scatter_kernel, depth, kinds, chunks, cu...  137 us
    pallas_call x1, Pallas kernels, gather_all(): pl.pallas_call(functools.partial(gather_kernel, depth, chunks, entries),...  125 us
    pallas_call x1, Pallas kernels, feed(): pl.pallas_call(feed_kernel, out_shape=fixed + [jax.ShapeDtypeStruct((widt...  28.7 us

profile of v6, /device:TPU:0, one launch (start us, length us, event | category | flops | bytes accessed | tf_op | source)
XLA Modules:
  0.0 299.6 jit_solution(500168200667292116)
XLA Ops:
  1.3 0.8 stack.31
  2.1 0.7 fusion.7
  2.8 0.6 pad.24.refs_0_
  3.4 0.6 broadcast_in_dim.14.refs_6_.kind
  4.0 124.5 %shard_map.279 = (bf16[4,2,2,2,16,128]{5,4,3,2,1,0:T(8,128)(2,1)}, bf16[4,2,2,2,24,768]{5,4,3,2,1,0:T(8,128)(2,1)}, bf16[2,4,2,2,2,24,3072]{6,5,4,3,2,1,0:T(8,12...) custom-call(bf16[16,128]{1,0:T(8,128)(2,1)} %pad.24.refs_0_, ...), custom_call_target="tpu_custom_call" | custom-call | tf_op jit(solution)/shard_map/pallas_call | solution.py:907
  128.5 0.9 slice.4
  129.4 0.7 broadcast_in_dim_reshape.4.up_shift
  130.2 28.7 %shard_map.280 = (bf16[512,768]{1,0:T(8,128)(2,1)}, f32[512,768]{1,0:T(8,128)}, bf16[768,768]{1,0:T(8,128)(2,1)}, bf16[512,768]{1,0:T(8,128)(2,1)}, bf16[768,307...) custom-call(s32[1]{0:T(128)} %bitcast.pick, s32[1]{0:T(128)} %bitcast.1.place_ref, ...), custom_call_target="tpu_custom_call" | custom-call | tf_op jit(solution)/shard_map/pallas_call | solution.py:547
  158.8 136.7 %shard_map.281 = (f32[2,24,3072]{2,1,0:T(8,128)}, f32[2,96,768]{2,1,0:T(8,128)}, f32[1,24,768]{2,1,0:T(8,128)}, f32[1,24,2304]{2,1,0:T(8,128)}, f32[1,16,128]{2,...) custom-call(bf16[4,2,2,2,24,3072]{5,4,3,2,1,0:T(8,128)(2,1)} %bitcast.26, ...), custom_call_target="tpu_custom_call" | custom-call | tf_op jit(solution)/shard_map/pallas_call | solution.py:1474
  295.5 3.9 %shard_map.282 = (f32[2,24,3072]{2,1,0:T(8,128)}, f32[2,96,768]{2,1,0:T(8,128)}, f32[24,768]{1,0:T(8,128)}, f32[24,2304]{1,0:T(8,128)}, bf16[512,768]{1,0:T(8,12...) custom-call(f32[2,24,3072]{2,1,0:T(8,128)} %get-tuple-element.79.ref, ...), custom_call_target="tpu_custom_call" | custom-call | tf_op jit(solution)/shard_map/pallas_call | solution.py:1516
  (1 shorter events, 0.0 us)

commit v7 on v6

--- a/solution.py
+++ b/solution.py
@@ -76,8 +76,8 @@
     rows = (0, share)
     near_cols = divided(3 * width, 128, 9, 9)
     out_cols = divided(width, 128, 3, 3)
-    up_cols = divided(ff, 128, 4, 14, 6)
-    down_rows = divided(ff_share, 16, 1, 3, 2)
+    up_cols = divided(ff, 128, 8, 8, 8)
+    down_rows = divided(ff_share, 16, 2, 2, 2)
     chunks = [
         [((0, None), (0, THIN_ROWS), (0, 128), 0, False)]
         + [((1, None), rows, cols, order, False) for order, cols in enumerate(near_cols)],
@@ -91,7 +91,7 @@
 
     chunks += [up_chunk(1, up_cols), down_chunk(1, down_rows), down_chunk(0, down_rows)]
     unit, begin = 128, 0
-    for shares in ((2, 7, 3), (1, 5, 2), (1, 2, 1)):
+    for shares in ((4, 4, 4), (3, 2, 3), (1, 2, 1)):
         parts = []
         for blocks in shares:
             parts.append((begin * unit, blocks * unit))
@@ -112,7 +112,7 @@
         chunks.append(
             [(1, e, band, (0, width), order) for order, band in enumerate(down_rows)]
         )
-    chunks.append([])
+    chunks += [[], []]
     chunks.append(
         [(3, 0, rows, cols, order) for order, cols in enumerate(near_cols)]
     )
@@ -995,8 +995,6 @@
     for copy in local:
         copy.start()
     greet(at, depth)
-    for copy in local:
-        copy.wait()
     beside, across = moved(at, "c", 1, depth), moved(at, "y", 1, depth)
     kv_beside = remote(kv_away, kv_sum, kv_sems, 0, beside)
     kv_across = remote(far_terms, far_got, kv_sems, 1, across)
@@ -1409,6 +1407,9 @@
         return scope
 
     flow = Pipeline(chunks, 2, start, wait)
+    for copy in local:
+        copy.wait()
+    flow.tick()
     attention(0)()
     flow.tick()
     attention(1)()

time: 304 us -> 289 us (0.951)
  Pallas kernels: 294 us -> 279 us
    pallas_call x1, Pallas kernels: 125 us -> 116 us  [gather_all(): pl.pallas_call(functools.partial(gather_kernel, depth, chunks, entries),...]
    pallas_call x1, Pallas kernels: 137 us -> 131 us  [scatter_all(): pl.pallas_call(functools.partial(scatter_kernel, depth, kinds, chunks, cu...]
where the time goes in v7:
time: 289 us; the launch traced here: 285 us
  Pallas kernels  279 us (97%)
  local copies, waits for them, and re-layouts  3.62 us (1%)
    pallas_call x1, Pallas kernels, scatter_all(): pl.pallas_call(functools.partial(scatter_kernel, depth, kinds, chunks, cu...  131 us
    pallas_call x1, Pallas kernels, gather_all(): pl.pallas_call(functools.partial(gather_kernel, depth, chunks, entries),...  116 us
    pallas_call x1, Pallas kernels, feed(): pl.pallas_call(feed_kernel, out_shape=fixed + [jax.ShapeDtypeStruct((widt...  28.7 us

profile of v7, /device:TPU:0, one launch (start us, length us, event | category | flops | bytes accessed | tf_op | source)
XLA Modules:
  0.0 284.7 jit_solution(8059718429652358524)
XLA Ops:
  1.3 0.8 stack.31
  2.1 0.7 fusion.7
  2.8 0.6 pad.24.refs_0_
  3.4 0.6 broadcast_in_dim.14.refs_6_.kind
  4.0 115.6 %shard_map.279 = (bf16[4,2,2,2,16,128]{5,4,3,2,1,0:T(8,128)(2,1)}, bf16[4,2,2,2,24,768]{5,4,3,2,1,0:T(8,128)(2,1)}, bf16[2,4,2,2,2,24,3072]{6,5,4,3,2,1,0:T(8,12...) custom-call(bf16[16,128]{1,0:T(8,128)(2,1)} %pad.24.refs_0_, ...), custom_call_target="tpu_custom_call" | custom-call | tf_op jit(solution)/shard_map/pallas_call | solution.py:907
  119.5 0.9 slice.4
  120.5 0.7 broadcast_in_dim_reshape.4.up_shift
  121.2 28.7 %shard_map.280 = (bf16[512,768]{1,0:T(8,128)(2,1)}, f32[512,768]{1,0:T(8,128)}, bf16[768,768]{1,0:T(8,128)(2,1)}, bf16[512,768]{1,0:T(8,128)(2,1)}, bf16[768,307...) custom-call(s32[1]{0:T(128)} %bitcast.pick, s32[1]{0:T(128)} %bitcast.1.place_ref, ...), custom_call_target="tpu_custom_call" | custom-call | tf_op jit(solution)/shard_map/pallas_call | solution.py:547
  149.9 130.8 %shard_map.281 = (f32[2,24,3072]{2,1,0:T(8,128)}, f32[2,96,768]{2,1,0:T(8,128)}, f32[1,24,768]{2,1,0:T(8,128)}, f32[1,24,2304]{2,1,0:T(8,128)}, f32[1,16,128]{2,...) custom-call(bf16[4,2,2,2,24,3072]{5,4,3,2,1,0:T(8,128)(2,1)} %bitcast.26, ...), custom_call_target="tpu_custom_call" | custom-call | tf_op jit(solution)/shard_map/pallas_call | solution.py:1475
  280.7 3.9 %shard_map.282 = (f32[2,24,3072]{2,1,0:T(8,128)}, f32[2,96,768]{2,1,0:T(8,128)}, f32[24,768]{1,0:T(8,128)}, f32[24,2304]{1,0:T(8,128)}, bf16[512,768]{1,0:T(8,12...) custom-call(f32[2,24,3072]{2,1,0:T(8,128)} %get-tuple-element.79.ref, ...), custom_call_target="tpu_custom_call" | custom-call | tf_op jit(solution)/shard_map/pallas_call | solution.py:1517
  (1 shorter events, 0.0 us)

commit v8 on v7

--- a/solution.py
+++ b/solution.py
@@ -104,8 +104,8 @@
     rows = (0, share)
     near_cols = divided(3 * width, 128, 7, 7, 4)
     out_cols = divided(width, 128, 2, 3, 1)
-    up_cols = divided(ff, 128, 4, 14, 6)
-    down_rows = divided(ff_share, 16, 1, 3, 2)
+    up_cols = divided(ff, 128, 6, 10, 8)
+    down_rows = divided(ff_share, 16, 2, 2, 2)
     chunks = [[(2, 0, rows, cols, order) for order, cols in enumerate(out_cols)]]
     for e in (1, 0):
         chunks.append([(0, e, rows, cols, order) for order, cols in enumerate(up_cols)])

time: 289 us -> 284 us (0.983)
  Pallas kernels: 279 us -> 274 us
    pallas_call x1, Pallas kernels: 131 us -> 125 us  [scatter_all(): pl.pallas_call(functools.partial(scatter_kernel, depth, kinds, chunks, cu...]
where the time goes in v8:
time: 284 us; the launch traced here: 279 us
  Pallas kernels  274 us (96%)
  local copies, waits for them, and re-layouts  3.62 us (1%)
    pallas_call x1, Pallas kernels, scatter_all(): pl.pallas_call(functools.partial(scatter_kernel, depth, kinds, chunks, cu...  125 us
    pallas_call x1, Pallas kernels, gather_all(): pl.pallas_call(functools.partial(gather_kernel, depth, chunks, entries),...  116 us
    pallas_call x1, Pallas kernels, feed(): pl.pallas_call(feed_kernel, out_shape=fixed + [jax.ShapeDtypeStruct((widt...  28.7 us

profile of v8, /device:TPU:0, one launch (start us, length us, event | category | flops | bytes accessed | tf_op | source)
XLA Modules:
  0.0 279.4 jit_solution(10983043625022697177)
XLA Ops:
  1.3 0.8 stack.31
  2.1 0.7 fusion.7
  2.8 0.6 pad.24.refs_0_
  3.4 0.6 broadcast_in_dim.14.refs_6_.kind
  4.0 115.6 %shard_map.279 = (bf16[4,2,2,2,16,128]{5,4,3,2,1,0:T(8,128)(2,1)}, bf16[4,2,2,2,24,768]{5,4,3,2,1,0:T(8,128)(2,1)}, bf16[2,4,2,2,2,24,3072]{6,5,4,3,2,1,0:T(8,12...) custom-call(bf16[16,128]{1,0:T(8,128)(2,1)} %pad.24.refs_0_, ...), custom_call_target="tpu_custom_call" | custom-call | tf_op jit(solution)/shard_map/pallas_call | solution.py:907
  119.5 0.9 slice.4
  120.5 0.7 broadcast_in_dim_reshape.4.up_shift
  121.2 28.7 %shard_map.280 = (bf16[512,768]{1,0:T(8,128)(2,1)}, f32[512,768]{1,0:T(8,128)}, bf16[768,768]{1,0:T(8,128)(2,1)}, bf16[512,768]{1,0:T(8,128)(2,1)}, bf16[768,307...) custom-call(s32[1]{0:T(128)} %bitcast.pick, s32[1]{0:T(128)} %bitcast.1.place_ref, ...), custom_call_target="tpu_custom_call" | custom-call | tf_op jit(solution)/shard_map/pallas_call | solution.py:547
  149.9 125.5 %shard_map.281 = (f32[2,24,3072]{2,1,0:T(8,128)}, f32[2,96,768]{2,1,0:T(8,128)}, f32[1,24,768]{2,1,0:T(8,128)}, f32[1,24,2304]{2,1,0:T(8,128)}, f32[1,16,128]{2,...) custom-call(bf16[4,2,2,2,24,3072]{5,4,3,2,1,0:T(8,128)(2,1)} %bitcast.26, ...), custom_call_target="tpu_custom_call" | custom-call | tf_op jit(solution)/shard_map/pallas_call | solution.py:1475
  275.4 3.9 %shard_map.282 = (f32[2,24,3072]{2,1,0:T(8,128)}, f32[2,96,768]{2,1,0:T(8,128)}, f32[24,768]{1,0:T(8,128)}, f32[24,2304]{1,0:T(8,128)}, bf16[512,768]{1,0:T(8,12...) custom-call(f32[2,24,3072]{2,1,0:T(8,128)} %get-tuple-element.79.ref, ...), custom_call_target="tpu_custom_call" | custom-call | tf_op jit(solution)/shard_map/pallas_call | solution.py:1517
  (1 shorter events, 0.0 us)
